TPU v7x, 1024 devices: a whole 8x8x8 slice. The times are simulated.
1024 devices in a mesh: dom: 128 (over x, y, core), inst: 8 (over z).
Axes of the slice: x: 8, y: 8, z: 8, core: 2. Of those that a mesh axis runs over, the one named last changes fastest.
Arguments:
- adjoint: float32 [16, 5, 131072], P('inst', None, 'dom'), may hold values from -6 to 6
- gradient: float32 [16, 5, 131072], P('inst', None, 'dom'), may hold values from -6 to 6
- jac_blocks: float32 [16, 6, 5, 5, 131072], P('inst', None, None, None, 'dom'), may hold values from -0.9 to 0.9
- diag_inverse: float32 [16, 5, 5, 131072], P('inst', None, None, 'dom'), may hold values from -2.4 to 2.4
- volume: float32 [131072], P('dom'), may hold values from 0.05 to 0.2
- columns: int32 [6, 131072], P(None, 'dom'), may hold values from 0 to 1535, as said below
- send_rows: int32 [512, 128], P('dom'), may hold values from 0 to 1023, as said below
- counts: int32 [128], P('dom'), may hold values from 512 to 1024, as said below
Outputs:
- swept: float32 [16, 5, 131072], P('inst', None, 'dom')
Inputs may be any that keep to these rules, and one draw needn't show every extreme that they name: `counts`: at least half of 1024 for every partition; some partition uses all 1024 slots. `columns`: for block k < 4 the entry is a live cell of the same partition; for the other two it is 1024 plus a row of the four interface blocks; every interface row of a partition is named by some live cell. `send_rows`: live cells of the sending partition.
All inputs are finite; a program needn't handle non-finite values.
Results may differ from a plain program's by a relative error of at most 0.0001.
Values sent between devices are 32-bit elements; how exact they have to be, the bound alone decides.
No kernel may reach another device: no remote copies, remote signals or barrier semaphores. Data moves between devices by JAX's collectives and lax.ppermute only.
A program may use at most 128 MiB of HBM per device.

v0:
```python
import math

import jax
import jax.numpy as jnp
from jax import lax
from jax.sharding import PartitionSpec as P

NI = 16
NV = 5
NBR = 6
SWEEPS = 2


OFFSETS = (1, -1, 2, -2)


def shifted(value, axis, steps):
    count = lax.axis_size(axis)
    pairs = [(source, (source + steps) % count) for source in range(count)]
    return lax.ppermute(value, axis, pairs)


def spectral_matrix(count):
    index = jnp.arange(count, dtype=jnp.int32)
    differ = index[:, None] - index[None, :]
    parity = (1 - 2 * jnp.mod(differ, 2)).astype(jnp.float32)
    safe_diff = jnp.where(differ == 0, 1, differ).astype(jnp.float32)
    angle = math.pi * safe_diff / count
    values = 0.5 * parity * jnp.cos(angle) / jnp.sin(angle)
    return jnp.where(differ == 0, 0.0, values)


def interface_blocks(current, send_rows):
    rim_rows = send_rows.shape[1]
    flat_rows = send_rows.reshape(-1)
    outgoing = jnp.take(current, flat_rows, axis=2)
    slots = [
        lax.slice_in_dim(outgoing, slot_index * rim_rows, (slot_index + 1) * rim_rows, axis=2)
        for slot_index in range(4)
    ]
    arrived = []
    for slot_index, offset in enumerate(OFFSETS):
        arrived.append(shifted(slots[slot_index], "dom", offset))
    return arrived


def on_device(adjoint, gradient, jac_blocks, diag_inverse, volume, columns, send_rows, counts):
    local_inst = adjoint.shape[0]
    cells_here = adjoint.shape[2]
    spectral = spectral_matrix(NI)
    inst_start = lax.axis_index("inst") * local_inst
    spec_cols = lax.dynamic_slice_in_dim(spectral, inst_start, local_inst, 1)
    live_mask = (jnp.arange(cells_here, dtype=jnp.int32) < counts[0]).astype(jnp.float32)
    rim_cols = columns[NBR - 2 :] - cells_here
    current = adjoint
    for sweep_index in range(SWEEPS):
        arrived = interface_blocks(current, send_rows)
        rim_block = jnp.concatenate(arrived, axis=2)
        coupling = jnp.zeros(current.shape, jnp.float32)
        for block_index in range(NBR):
            if block_index < NBR - 2:
                picked = jnp.take(current, columns[block_index], axis=2)
            else:
                picked = jnp.take(rim_block, rim_cols[block_index - (NBR - 2)], axis=2)
            for var_index in range(NV):
                coupling = (
                    coupling
                    + jac_blocks[:, block_index, :, var_index, :]
                    * picked[:, var_index, :][:, None, :]
                )
        derivative = jnp.einsum(
            "ml,mvc->lvc",
            spec_cols,
            lax.all_gather(current, "inst", axis=0, tiled=True),
            precision=lax.Precision.HIGHEST,
        )
        remainder = gradient - coupling - volume[None, None, :] * derivative
        updated = jnp.zeros(current.shape, jnp.float32)
        for var_index in range(NV):
            updated = (
                updated + diag_inverse[:, :, var_index, :] * remainder[:, var_index, :][:, None, :]
            )
        current = live_mask[None, None, :] * updated
    return current


def solution(mesh):
    in_specs = (
        P("inst", None, "dom"),
        P("inst", None, "dom"),
        P("inst", None, None, None, "dom"),
        P("inst", None, None, "dom"),
        P("dom"),
        P(None, "dom"),
        P("dom", None),
        P("dom"),
    )
    out_specs = P("inst", None, "dom")
    return jax.shard_map(
        on_device, mesh=mesh, in_specs=in_specs, out_specs=out_specs, check_vma=False
    )
```

profile of v0, /device:TPU:1, one launch (start us, length us, event | category | flops | bytes accessed | tf_op | source)
XLA Modules:
  0.0 474.9 jit_solution(3562172317506949823)
XLA Ops:
  3.6 2.1 gather_fusion.4
  8.3 4.7 collective-permute-start
  13.1 13.3 %collective-permute-start.1 = (f32[2,5,128]{1,0,2:T(2,128)}, f32[2,5,128]{1,0,2:T(2,128)}, u32[]{:S(2)}, u32[]{:S(2)}) collective-permute-start(f32[2,5,128]{1,0,2:T(2,128)} %get-tuple-element.74), channel_id=1, source_target_pairs={{0,1016},{8,0},{16,8},{24,16},{32,24},{40,32},{48,40},{56,48},{64,... | collective-permute-start | bytes 15368 | tf_op jit(solution)/shard_map/ppermute | solution.py:20
  28.3 6.7 %collective-permute-start.3 = (f32[2,5,128]{1,0,2:T(2,128)}, f32[2,5,128]{1,0,2:T(2,128)S(1)}, u32[]{:S(2)}, u32[]{:S(2)}) collective-permute-start(f32[2,5,128]{1,0,2:T(2,128)} %get-tuple-element.72), channel_id=1, source_target_pairs={{0,1008},{8,1016},{16,0},{24,8},{32,16},{40,24},{48,32},{56,40},{6... | collective-permute-start | bytes 15368 | tf_op jit(solution)/shard_map/ppermute | solution.py:20
  37.3 23.4 %all_gather.6 = f32[16,5,1024]{2,1,0:T(8,128)} all-gather(f32[2,5,1024]{2,1,0:T(8,128)S(1)} %copy.447), channel_id=1, replica_groups=mesh['dom'=128,'inst'=8] {'inst'}, dimensions={0}, use_global_device_ids=true | all-gather | bytes 368640 | tf_op jit(solution)/shard_map/all_gather | solution.py:74
  60.6 3.7 gather_fusion.3
  64.3 3.7 select_bitcast_fusion.8
  68.1 5.9 %fusion.105 = (f32[2,1,1024]{1,0,2:T(2,128)}, f32[2,1,1024]{1,0,2:T(2,128)}, f32[2,1,1024]{1,0,2:T(2,128)}, f32[2,1,1024]{1,0,2:T(2,128)}, f32[2,1,1024]{1,0,2:T(2,128)}) fusion(f32[2,5,1024]{1,0,2:T(2,128)S(1)} %select_bitcast_fusion.8), kind=kLoop, calls=%fused_computation.245 | loop fusion | bytes 81920 | tf_op jit(solution)/shard_map/slice | solution.py:69
  74.0 3.5 gather_fusion.2
  77.6 3.7 select_bitcast_fusion.9
  81.3 5.9 %fusion.104 = (f32[2,1,1024]{1,0,2:T(2,128)}, f32[2,1,1024]{1,0,2:T(2,128)}, f32[2,1,1024]{1,0,2:T(2,128)}, f32[2,1,1024]{1,0,2:T(2,128)}, f32[2,1,1024]{1,0,2:T(2,128)}) fusion(f32[2,5,1024]{1,0,2:T(2,128)S(1)} %select_bitcast_fusion.9), kind=kLoop, calls=%fused_computation.244 | loop fusion | bytes 81920 | tf_op jit(solution)/shard_map/slice | solution.py:69
  87.3 3.5 gather_fusion.1
  90.8 3.7 select_bitcast_fusion.10
  94.6 5.9 %fusion.103 = (f32[2,1,1024]{1,0,2:T(2,128)}, f32[2,1,1024]{1,0,2:T(2,128)}, f32[2,1,1024]{1,0,2:T(2,128)}, f32[2,1,1024]{1,0,2:T(2,128)}, f32[2,1,1024]{1,0,2:T(2,128)}) fusion(f32[2,5,1024]{1,0,2:T(2,128)S(1)} %select_bitcast_fusion.10), kind=kLoop, calls=%fused_computation.243 | loop fusion | bytes 81920 | tf_op jit(solution)/shard_map/slice | solution.py:69
  100.5 3.6 gather_fusion
  104.1 3.7 select_bitcast_fusion.11
  107.8 5.9 %fusion.102 = (f32[2,1,1024]{1,0,2:T(2,128)}, f32[2,1,1024]{1,0,2:T(2,128)}, f32[2,1,1024]{1,0,2:T(2,128)}, f32[2,1,1024]{1,0,2:T(2,128)}, f32[2,1,1024]{1,0,2:T(2,128)}) fusion(f32[2,5,1024]{1,0,2:T(2,128)S(1)} %select_bitcast_fusion.11), kind=kLoop, calls=%fused_computation.242 | loop fusion | bytes 81920 | tf_op jit(solution)/shard_map/slice | solution.py:69
  152.2 8.5 %gather_fusion.6 = f32[1024,2,5]{2,1,0:T(2,128)} fusion(f32[2,5,512]{1,0,2:T(2,128)} %constant_dynamic-update-slice_fusion, s32[1024]{0:T(1024)S(1)} %get-tuple-element.102), kind=kCustom, calls=%fused_computation.11.clone | custom fusion | bytes 86016 | tf_op jit(solution)/shard_map/jit(_take)/gather | solution.py:64
  160.7 5.3 %select_bitcast_fusion.6 = f32[2,5,1024]{1,0,2:T(2,128)S(1)} fusion(f32[1024,2,5]{2,1,0:T(2,128)} %gather_fusion.6, pred[1024]{0:T(1024)(128)(4,1)S(1)} %compare_and_fusion.1), kind=kLoop, calls=%fused_computation.44 | loop fusion | flops 10240 | bytes 82944 | tf_op jit(solution)/shard_map/jit(_take)/select_n | solution.py:64
  166.0 5.9 %fusion.107 = (f32[2,1,1024]{1,0,2:T(2,128)}, f32[2,1,1024]{1,0,2:T(2,128)}, f32[2,1,1024]{1,0,2:T(2,128)}, f32[2,1,1024]{1,0,2:T(2,128)}, f32[2,1,1024]{1,0,2:T(2,128)}) fusion(f32[2,5,1024]{1,0,2:T(2,128)S(1)} %select_bitcast_fusion.6), kind=kLoop, calls=%fused_computation.247 | loop fusion | bytes 81920 | tf_op jit(solution)/shard_map/slice | solution.py:69
  179.1 8.5 %gather_fusion.5 = f32[1024,2,5]{2,1,0:T(2,128)} fusion(f32[2,5,512]{1,0,2:T(2,128)} %constant_dynamic-update-slice_fusion, s32[1024]{0:T(1024)S(1)} %get-tuple-element.101), kind=kCustom, calls=%fused_computation.2.clone | custom fusion | bytes 86016 | tf_op jit(solution)/shard_map/jit(_take)/gather | solution.py:64
  187.6 5.3 %select_bitcast_fusion.7 = f32[2,5,1024]{1,0,2:T(2,128)S(1)} fusion(f32[1024,2,5]{2,1,0:T(2,128)} %gather_fusion.5, pred[1024]{0:T(1024)(128)(4,1)S(1)} %compare_and_fusion.2), kind=kLoop, calls=%fused_computation.45 | loop fusion | flops 10240 | bytes 82944 | tf_op jit(solution)/shard_map/jit(_take)/select_n | solution.py:64
  192.9 5.9 %fusion.106 = (f32[2,1,1024]{1,0,2:T(2,128)}, f32[2,1,1024]{1,0,2:T(2,128)}, f32[2,1,1024]{1,0,2:T(2,128)}, f32[2,1,1024]{1,0,2:T(2,128)}, f32[2,1,1024]{1,0,2:T(2,128)}) fusion(f32[2,5,1024]{1,0,2:T(2,128)S(1)} %select_bitcast_fusion.7), kind=kLoop, calls=%fused_computation.246 | loop fusion | bytes 81920 | tf_op jit(solution)/shard_map/slice | solution.py:69
  206.0 2.4 fusion.1
  213.6 10.0 %fusion.3 = f32[2,5,1024]{1,0,2:T(2,128)} fusion(f32[2,5,1,1024]{1,0,3,2:T(2,128)S(1)} %copy.530, f32[2,5,1,1024]{1,0,3,2:T(2,128)S(1)} %copy.529, f32[2,5,1,1024]{1,0,3,2:T(2,128)S(1)} %copy.528, f32[2,5,1,1024]{1,0,3,2:T(2,128)} %copy.527, f32[2,5,1,1024]{1,0,3,2:T(2,128)} %copy.496, f32[1024]{0:T(1024)S(1)} %fusion.81, f32[2,1024]{0,1:T(8,128)} %copy.457, ...), kind=kLoop, calls=%fused_computation.21 | loop fusion | flops 102400 | bytes 290816 | tf_op jit(solution)/shard_map/mul | solution.py:83
  225.0 3.5 gather_fusion.11
  228.5 8.7 %gather_fusion.10 = f32[1024,2,5]{2,1,0:T(2,128)} fusion(f32[2,5,1024]{1,0,2:T(2,128)} %fusion.3, s32[1024]{0:T(1024)S(1)} %get-tuple-element.100), kind=kCustom, calls=%fused_computation.9.clone | custom fusion | bytes 86016 | tf_op jit(solution)/shard_map/jit(_take)/gather | solution.py:62
  237.2 8.7 %gather_fusion.9 = f32[1024,2,5]{2,1,0:T(2,128)} fusion(f32[2,5,1024]{1,0,2:T(2,128)} %fusion.3, s32[1024]{0:T(1024)S(1)} %get-tuple-element.99), kind=kCustom, calls=%fused_computation.8.clone | custom fusion | bytes 86016 | tf_op jit(solution)/shard_map/jit(_take)/gather | solution.py:62
  245.9 8.7 %gather_fusion.8 = f32[1024,2,5]{2,1,0:T(2,128)} fusion(f32[2,5,1024]{1,0,2:T(2,128)} %fusion.3, s32[1024]{0:T(1024)S(1)} %get-tuple-element.98), kind=kCustom, calls=%fused_computation.7.clone | custom fusion | bytes 86016 | tf_op jit(solution)/shard_map/jit(_take)/gather | solution.py:62
  254.6 8.7 %gather_fusion.7 = f32[1024,2,5]{2,1,0:T(2,128)} fusion(f32[2,5,1024]{1,0,2:T(2,128)} %fusion.3, s32[1024]{0:T(1024)S(1)} %fusion.87), kind=kCustom, calls=%fused_computation.6.clone | custom fusion | bytes 86016 | tf_op jit(solution)/shard_map/jit(_take)/gather | solution.py:62
  263.4 21.6 %all_gather.7 = f32[16,5,1024]{2,1,0:T(8,128)} all-gather(f32[2,5,1024]{2,1,0:T(8,128)S(1)} %copy.488), channel_id=1, replica_groups=mesh['dom'=128,'inst'=8] {'inst'}, dimensions={0}, use_global_device_ids=true | all-gather | bytes 368640 | tf_op jit(solution)/shard_map/all_gather | solution.py:74
  285.0 3.0 select_bitcast_fusion.12
  288.9 14.6 %collective-permute-start.4 = (f32[2,5,128]{1,0,2:T(2,128)}, f32[2,5,128]{1,0,2:T(2,128)}, u32[]{:S(2)}, u32[]{:S(2)}) collective-permute-start(f32[2,5,128]{1,0,2:T(2,128)} %get-tuple-element.71), channel_id=1, source_target_pairs={{0,8},{8,16},{16,24},{24,32},{32,40},{40,48},{48,56},{56,64},{64,7... | collective-permute-start | bytes 15368 | tf_op jit(solution)/shard_map/ppermute | solution.py:20
  303.5 5.6 %collective-permute-start.5 = (f32[2,5,128]{1,0,2:T(2,128)}, f32[2,5,128]{1,0,2:T(2,128)S(1)}, u32[]{:S(2)}, u32[]{:S(2)}) collective-permute-start(f32[2,5,128]{1,0,2:T(2,128)} %get-tuple-element.70), channel_id=1, source_target_pairs={{0,1016},{8,0},{16,8},{24,16},{32,24},{40,32},{48,40},{56,48},{64,... | collective-permute-start | bytes 15368 | tf_op jit(solution)/shard_map/ppermute | solution.py:20
  311.0 6.7 %collective-permute-start.7 = (f32[2,5,128]{1,0,2:T(2,128)}, f32[2,5,128]{1,0,2:T(2,128)S(1)}, u32[]{:S(2)}, u32[]{:S(2)}) collective-permute-start(f32[2,5,128]{1,0,2:T(2,128)} %get-tuple-element.68), channel_id=1, source_target_pairs={{0,1008},{8,1016},{16,0},{24,8},{32,16},{40,24},{48,32},{56,40},{6... | collective-permute-start | bytes 15368 | tf_op jit(solution)/shard_map/ppermute | solution.py:20
  317.7 4.1 select_bitcast_fusion.2
  321.9 5.9 %fusion.99 = (f32[2,1,1024]{1,0,2:T(2,128)}, f32[2,1,1024]{1,0,2:T(2,128)}, f32[2,1,1024]{1,0,2:T(2,128)}, f32[2,1,1024]{1,0,2:T(2,128)}, f32[2,1,1024]{1,0,2:T(2,128)}) fusion(f32[2,5,1024]{1,0,2:T(2,128)S(1)} %select_bitcast_fusion.2), kind=kLoop, calls=%fused_computation.239 | loop fusion | bytes 81920 | tf_op jit(solution)/shard_map/slice | solution.py:69
  327.9 3.7 select_bitcast_fusion.3
  331.6 6.0 %fusion.98 = (f32[2,1,1024]{1,0,2:T(2,128)}, f32[2,1,1024]{1,0,2:T(2,128)}, f32[2,1,1024]{1,0,2:T(2,128)}, f32[2,1,1024]{1,0,2:T(2,128)}, f32[2,1,1024]{1,0,2:T(2,128)}) fusion(f32[2,5,1024]{1,0,2:T(2,128)S(1)} %select_bitcast_fusion.3), kind=kLoop, calls=%fused_computation.238 | loop fusion | bytes 81920 | tf_op jit(solution)/shard_map/slice | solution.py:69
  337.6 3.7 select_bitcast_fusion.4
  341.4 5.9 %fusion.97 = (f32[2,1,1024]{1,0,2:T(2,128)}, f32[2,1,1024]{1,0,2:T(2,128)}, f32[2,1,1024]{1,0,2:T(2,128)}, f32[2,1,1024]{1,0,2:T(2,128)}, f32[2,1,1024]{1,0,2:T(2,128)}) fusion(f32[2,5,1024]{1,0,2:T(2,128)S(1)} %select_bitcast_fusion.4), kind=kLoop, calls=%fused_computation.237 | loop fusion | bytes 81920 | tf_op jit(solution)/shard_map/slice | solution.py:69
  347.3 3.7 select_bitcast_fusion.5
  351.0 6.0 %fusion.96 = (f32[2,1,1024]{1,0,2:T(2,128)}, f32[2,1,1024]{1,0,2:T(2,128)}, f32[2,1,1024]{1,0,2:T(2,128)}, f32[2,1,1024]{1,0,2:T(2,128)}, f32[2,1,1024]{1,0,2:T(2,128)}) fusion(f32[2,5,1024]{1,0,2:T(2,128)S(1)} %select_bitcast_fusion.5), kind=kLoop, calls=%fused_computation.236 | loop fusion | bytes 81920 | tf_op jit(solution)/shard_map/slice | solution.py:69
  357.0 2.0 copy.477
  359.0 2.0 copy.476
  361.0 2.0 copy.475
  369.0 2.0 copy.471
  371.0 2.0 copy.470
  373.0 2.0 copy.469
  375.0 2.0 copy.468
  381.1 2.0 copy.465
  385.1 2.0 copy.463
  391.1 2.0 copy.460
  393.1 2.0 copy.459
  395.1 2.0 copy.458
  400.7 8.5 %gather_fusion.13 = f32[1024,2,5]{2,1,0:T(2,128)} fusion(f32[2,5,512]{1,0,2:T(2,128)} %constant_dynamic-update-slice_fusion.4, s32[1024]{0:T(1024)S(1)} %get-tuple-element.102), kind=kCustom, calls=%fused_computation.13.clone | custom fusion | bytes 86016 | tf_op jit(solution)/shard_map/jit(_take)/gather | solution.py:64
  409.2 8.5 %gather_fusion.12 = f32[1024,2,5]{2,1,0:T(2,128)} fusion(f32[2,5,512]{1,0,2:T(2,128)} %constant_dynamic-update-slice_fusion.4, s32[1024]{0:T(1024)S(1)} %get-tuple-element.101), kind=kCustom, calls=%fused_computation.12.clone | custom fusion | bytes 86016 | tf_op jit(solution)/shard_map/jit(_take)/gather | solution.py:64
  417.7 5.4 %select_bitcast_fusion = f32[2,5,1024]{1,0,2:T(2,128)S(1)} fusion(f32[1024,2,5]{2,1,0:T(2,128)} %gather_fusion.13, pred[1024]{0:T(1024)(128)(4,1)S(1)} %copy-done.9), kind=kLoop, calls=%fused_computation.38 | loop fusion | flops 10240 | bytes 82944 | tf_op jit(solution)/shard_map/jit(_take)/select_n | solution.py:64
  423.2 6.0 %fusion.101 = (f32[2,1,1024]{1,0,2:T(2,128)}, f32[2,1,1024]{1,0,2:T(2,128)}, f32[2,1,1024]{1,0,2:T(2,128)}, f32[2,1,1024]{1,0,2:T(2,128)}, f32[2,1,1024]{1,0,2:T(2,128)}) fusion(f32[2,5,1024]{1,0,2:T(2,128)S(1)} %select_bitcast_fusion), kind=kLoop, calls=%fused_computation.241 | loop fusion | bytes 81920 | tf_op jit(solution)/shard_map/slice | solution.py:69
  436.3 5.3 %select_bitcast_fusion.1 = f32[2,5,1024]{1,0,2:T(2,128)S(1)} fusion(f32[1024,2,5]{2,1,0:T(2,128)} %gather_fusion.12, pred[1024]{0:T(1024)(128)(4,1)S(1)} %copy-done.7), kind=kLoop, calls=%fused_computation.39 | loop fusion | flops 10240 | bytes 82944 | tf_op jit(solution)/shard_map/jit(_take)/select_n | solution.py:64
  441.6 5.9 %fusion.100 = (f32[2,1,1024]{1,0,2:T(2,128)}, f32[2,1,1024]{1,0,2:T(2,128)}, f32[2,1,1024]{1,0,2:T(2,128)}, f32[2,1,1024]{1,0,2:T(2,128)}, f32[2,1,1024]{1,0,2:T(2,128)}) fusion(f32[2,5,1024]{1,0,2:T(2,128)S(1)} %select_bitcast_fusion.1), kind=kLoop, calls=%fused_computation.240 | loop fusion | bytes 81920 | tf_op jit(solution)/shard_map/slice | solution.py:69
  455.2 2.3 fusion
  462.7 10.0 %fusion.5 = f32[2,5,1024]{1,0,2:T(2,128)} fusion(f32[2,5,1,1024]{1,0,3,2:T(2,128)S(1)} %copy.530, f32[2,5,1,1024]{1,0,3,2:T(2,128)S(1)} %copy.529, f32[2,5,1,1024]{1,0,3,2:T(2,128)S(1)} %copy.528, f32[2,5,1,1024]{1,0,3,2:T(2,128)} %copy.527, f32[2,5,1,1024]{1,0,3,2:T(2,128)} %copy.496, f32[1024]{0:T(1024)S(1)} %fusion.81, f32[2,1024]{0,1:T(8,128)} %copy.494, ...), kind=kLoop, calls=%fused_computation.23 | loop fusion | flops 102400 | bytes 290816 | tf_op jit(solution)/shard_map/mul | solution.py:83
  472.7 2.0 copy.495
  (198 shorter events, 111.1 us)
Async XLA Ops:
  1.4 7.0 %copy-start.38 = (pred[512]{0:T(512)(128)(4,1)}, pred[512]{0:T(512)(128)(4,1)S(1)}, u32[]{:S(2)}) copy-start(pred[512]{0:T(512)(128)(4,1)S(1)} %compare_and_fusion.6) | copy-start | bytes 1540
  2.6 32.3 %copy-start.5 = (f32[2,5,1024]{2,0,1:T(2,128)S(1)}, f32[2,5,1024]{2,0,1:T(2,128)}, u32[]{:S(2)}) copy-start(f32[2,5,1024]{2,0,1:T(2,128)} %param.14) | copy-start | bytes 122884
  2.7 33.9 %copy-start.4 = (f32[2,5,5,1024]{3,0,2,1:T(2,128)S(1)}, f32[2,5,5,1024]{3,0,2,1:T(2,128)}, u32[]{:S(2)}) copy-start(f32[2,5,5,1024]{3,0,2,1:T(2,128)} %param.17) | copy-start | bytes 614404
  8.3 138.5 %collective-permute-start = (f32[2,5,128]{1,0,2:T(2,128)}, f32[2,5,128]{1,0,2:T(2,128)}, u32[]{:S(2)}, u32[]{:S(2)}) collective-permute-start(f32[2,5,128]{1,0,2:T(2,128)} %get-tuple-element.75), channel_id=1, source_target_pairs={{0,8},{8,16},{16,24},{24,32},{32,40},{40,48},{48,56},{56,64},{64,7... | collective-permute-start | bytes 15368 | tf_op jit(solution)/shard_map/ppermute | solution.py:20
  13.1 135.3 %collective-permute-start.1 = (f32[2,5,128]{1,0,2:T(2,128)}, f32[2,5,128]{1,0,2:T(2,128)}, u32[]{:S(2)}, u32[]{:S(2)}) collective-permute-start(f32[2,5,128]{1,0,2:T(2,128)} %get-tuple-element.74), channel_id=1, source_target_pairs={{0,1016},{8,0},{16,8},{24,16},{32,24},{40,32},{48,40},{56,48},{64,... | collective-permute-start | bytes 15368 | tf_op jit(solution)/shard_map/ppermute | solution.py:20
  26.3 123.6 %collective-permute-start.2 = (f32[2,5,128]{1,0,2:T(2,128)}, f32[2,5,128]{1,0,2:T(2,128)}, u32[]{:S(2)}, u32[]{:S(2)}) collective-permute-start(f32[2,5,128]{1,0,2:T(2,128)} %get-tuple-element.73), channel_id=1, source_target_pairs={{0,16},{8,24},{16,32},{24,40},{32,48},{40,56},{48,64},{56,72},{64,... | collective-permute-start | bytes 15368 | tf_op jit(solution)/shard_map/ppermute | solution.py:20
  28.3 123.3 %collective-permute-start.3 = (f32[2,5,128]{1,0,2:T(2,128)}, f32[2,5,128]{1,0,2:T(2,128)S(1)}, u32[]{:S(2)}, u32[]{:S(2)}) collective-permute-start(f32[2,5,128]{1,0,2:T(2,128)} %get-tuple-element.72), channel_id=1, source_target_pairs={{0,1008},{8,1016},{16,0},{24,8},{32,16},{40,24},{48,32},{56,40},{6... | collective-permute-start | bytes 15368 | tf_op jit(solution)/shard_map/ppermute | solution.py:20
  35.8 124.9 %copy-start.8 = (pred[1024]{0:T(1024)(128)(4,1)}, pred[1024]{0:T(1024)(128)(4,1)S(1)}, u32[]{:S(2)}) copy-start(pred[1024]{0:T(1024)(128)(4,1)S(1)} %compare_and_fusion.1) | copy-start | bytes 3076
  35.8 151.8 %copy-start.6 = (pred[1024]{0:T(1024)(128)(4,1)}, pred[1024]{0:T(1024)(128)(4,1)S(1)}, u32[]{:S(2)}) copy-start(pred[1024]{0:T(1024)(128)(4,1)S(1)} %compare_and_fusion.2) | copy-start | bytes 3076
  35.8 32.2 %copy-start.16 = (pred[1024]{0:T(1024)(128)(4,1)}, pred[1024]{0:T(1024)(128)(4,1)S(1)}, u32[]{:S(2)}) copy-start(pred[1024]{0:T(1024)(128)(4,1)S(1)} %compare_and_fusion.3) | copy-start | bytes 3076
  35.9 41.7 %copy-start.14 = (pred[1024]{0:T(1024)(128)(4,1)}, pred[1024]{0:T(1024)(128)(4,1)S(1)}, u32[]{:S(2)}) copy-start(pred[1024]{0:T(1024)(128)(4,1)S(1)} %compare_and_fusion.4) | copy-start | bytes 3076
  35.9 54.9 %copy-start.12 = (pred[1024]{0:T(1024)(128)(4,1)}, pred[1024]{0:T(1024)(128)(4,1)S(1)}, u32[]{:S(2)}) copy-start(pred[1024]{0:T(1024)(128)(4,1)S(1)} %compare_and_fusion.5) | copy-start | bytes 3076
  36.0 68.1 %copy-start.10 = (pred[1024]{0:T(1024)(128)(4,1)}, pred[1024]{0:T(1024)(128)(4,1)S(1)}, u32[]{:S(2)}) copy-start(pred[1024]{0:T(1024)(128)(4,1)S(1)} %compare_and_fusion) | copy-start | bytes 3076
  113.7 92.3 %copy-start.40 = (pred[16,16]{0,1:T(8,128)(4,1)}, pred[16,16]{0,1:T(8,128)(4,1)S(1)}, u32[]{:S(2)}) copy-start(pred[16,16]{0,1:T(8,128)(4,1)S(1)} %fusion.77) | copy-start | bytes 772
  203.1 2.9 copy-start.41
  203.1 2.9 copy-start.43
  223.6 61.4 %copy-start.39 = (pred[512]{0:T(512)(128)(4,1)S(1)}, pred[512]{0:T(512)(128)(4,1)}, u32[]{:S(2)}) copy-start(pred[512]{0:T(512)(128)(4,1)} %copy-done.38) | copy-start | bytes 1540
  263.4 54.4 %copy-start.3 = (f32[1024,2,5]{2,1,0:T(2,128)S(1)}, f32[1024,2,5]{2,1,0:T(2,128)}, u32[]{:S(2)}) copy-start(f32[1024,2,5]{2,1,0:T(2,128)} %gather_fusion.10) | copy-start | bytes 122884
  263.4 54.4 %copy-start.17 = (pred[1024]{0:T(1024)(128)(4,1)S(1)}, pred[1024]{0:T(1024)(128)(4,1)}, u32[]{:S(2)}) copy-start(pred[1024]{0:T(1024)(128)(4,1)} %copy-done.16) | copy-start | bytes 3076
  288.9 108.3 %collective-permute-start.4 = (f32[2,5,128]{1,0,2:T(2,128)}, f32[2,5,128]{1,0,2:T(2,128)}, u32[]{:S(2)}, u32[]{:S(2)}) collective-permute-start(f32[2,5,128]{1,0,2:T(2,128)} %get-tuple-element.71), channel_id=1, source_target_pairs={{0,8},{8,16},{16,24},{24,32},{32,40},{40,48},{48,56},{56,64},{64,7... | collective-permute-start | bytes 15368 | tf_op jit(solution)/shard_map/ppermute | solution.py:20
  303.5 95.2 %collective-permute-start.5 = (f32[2,5,128]{1,0,2:T(2,128)}, f32[2,5,128]{1,0,2:T(2,128)S(1)}, u32[]{:S(2)}, u32[]{:S(2)}) collective-permute-start(f32[2,5,128]{1,0,2:T(2,128)} %get-tuple-element.70), channel_id=1, source_target_pairs={{0,1016},{8,0},{16,8},{24,16},{32,24},{40,32},{48,40},{56,48},{64,... | collective-permute-start | bytes 15368 | tf_op jit(solution)/shard_map/ppermute | solution.py:20
  309.1 90.3 %collective-permute-start.6 = (f32[2,5,128]{1,0,2:T(2,128)}, f32[2,5,128]{1,0,2:T(2,128)S(1)}, u32[]{:S(2)}, u32[]{:S(2)}) collective-permute-start(f32[2,5,128]{1,0,2:T(2,128)} %get-tuple-element.69), channel_id=1, source_target_pairs={{0,16},{8,24},{16,32},{24,40},{32,48},{40,56},{48,64},{56,72},{64,... | collective-permute-start | bytes 15368 | tf_op jit(solution)/shard_map/ppermute | solution.py:20
  311.0 89.0 %collective-permute-start.7 = (f32[2,5,128]{1,0,2:T(2,128)}, f32[2,5,128]{1,0,2:T(2,128)S(1)}, u32[]{:S(2)}, u32[]{:S(2)}) collective-permute-start(f32[2,5,128]{1,0,2:T(2,128)} %get-tuple-element.68), channel_id=1, source_target_pairs={{0,1008},{8,1016},{16,0},{24,8},{32,16},{40,24},{48,32},{56,40},{6... | collective-permute-start | bytes 15368 | tf_op jit(solution)/shard_map/ppermute | solution.py:20
  321.9 6.0 %copy-start.2 = (f32[1024,2,5]{2,1,0:T(2,128)S(1)}, f32[1024,2,5]{2,1,0:T(2,128)}, u32[]{:S(2)}) copy-start(f32[1024,2,5]{2,1,0:T(2,128)} %gather_fusion.9) | copy-start | bytes 122884
  321.9 6.0 %copy-start.15 = (pred[1024]{0:T(1024)(128)(4,1)S(1)}, pred[1024]{0:T(1024)(128)(4,1)}, u32[]{:S(2)}) copy-start(pred[1024]{0:T(1024)(128)(4,1)} %copy-done.14) | copy-start | bytes 3076
  331.6 6.0 %copy-start.1 = (f32[1024,2,5]{2,1,0:T(2,128)S(1)}, f32[1024,2,5]{2,1,0:T(2,128)}, u32[]{:S(2)}) copy-start(f32[1024,2,5]{2,1,0:T(2,128)} %gather_fusion.8) | copy-start | bytes 122884
  331.6 6.0 %copy-start.13 = (pred[1024]{0:T(1024)(128)(4,1)S(1)}, pred[1024]{0:T(1024)(128)(4,1)}, u32[]{:S(2)}) copy-start(pred[1024]{0:T(1024)(128)(4,1)} %copy-done.12) | copy-start | bytes 3076
  341.3 5.9 %copy-start = (f32[1024,2,5]{2,1,0:T(2,128)S(1)}, f32[1024,2,5]{2,1,0:T(2,128)}, u32[]{:S(2)}) copy-start(f32[1024,2,5]{2,1,0:T(2,128)} %gather_fusion.7) | copy-start | bytes 122884
  341.4 5.9 %copy-start.11 = (pred[1024]{0:T(1024)(128)(4,1)S(1)}, pred[1024]{0:T(1024)(128)(4,1)}, u32[]{:S(2)}) copy-start(pred[1024]{0:T(1024)(128)(4,1)} %copy-done.10) | copy-start | bytes 3076
  395.1 22.6 %copy-start.9 = (pred[1024]{0:T(1024)(128)(4,1)S(1)}, pred[1024]{0:T(1024)(128)(4,1)}, u32[]{:S(2)}) copy-start(pred[1024]{0:T(1024)(128)(4,1)} %copy-done.8) | copy-start | bytes 3076
  433.4 2.9 copy-start.7
  451.8 3.2 copy-start.18
  451.8 3.2 copy-start.19
  451.8 3.2 copy-start.20
  451.8 3.2 copy-start.21
  451.9 3.2 copy-start.22
  451.9 3.2 copy-start.23
  451.9 3.2 copy-start.24
  451.9 3.2 copy-start.25
  451.9 3.2 copy-start.26
  451.9 3.2 copy-start.27
  451.9 3.2 copy-start.28
  451.9 3.2 copy-start.29
  451.9 3.2 copy-start.30
  451.9 3.2 copy-start.31
  452.0 3.2 copy-start.32
  452.0 3.2 copy-start.33
  452.0 3.2 copy-start.34
  452.0 3.2 copy-start.35
  452.0 3.2 copy-start.36
  452.0 3.2 copy-start.37
  452.0 3.2 copy-start.42
  452.0 3.2 copy-start.44
where the time goes:
time: 483 us; the launch traced here: 475 us
  local copies, waits for them, and re-layouts  289 us (60%)
  other arithmetic  79.1 us (16%)
  starting transfers between devices  55.4 us (11%)
  blocking collectives  44.9 us (9%)
    slice x72, local copies, waits for them, and re-layouts, on_device(): picked[:, var_index, :][:, None, :]  169 us
    ppermute x8, starting transfers between devices, shifted(): return lax.ppermute(value, axis, pairs)  55.4 us
    gather x8, local copies, waits for them, and re-layouts, on_device(): picked = jnp.take(current, columns[block_index], axis=2)  49.2 us
    all_gather x2, blocking collectives, on_device(): lax.all_gather(current, 'inst', axis=0, tiled=True)  44.9 us
    gather x4, local copies, waits for them, and re-layouts, on_device(): picked = jnp.take(rim_block, rim_cols[block_index - (NBR - 2)], axis=2)  34.1 us
    select_n x8, other arithmetic, on_device(): picked = jnp.take(current, columns[block_index], axis=2)  30.3 us
    select_n x4, other arithmetic, on_device(): picked = jnp.take(rim_block, rim_cols[block_index - (NBR - 2)], axis=2)  21.3 us
    mul x2, other arithmetic, on_device(): current = live_mask[None, None, :] * updated  19.9 us
  transfers between devices with their start and end apart: 8, of which 0 were waited for; matrix products, arithmetic and copies ran while one was open for 37% of the time, Pallas kernels for 0%

commit v1 on v0

v1 whole, which is shorter than its diff:
```python
import functools
import math

import jax
import jax.numpy as jnp
from jax import lax
from jax.experimental import pallas as pl
from jax.experimental.pallas import tpu as pltpu
from jax.sharding import PartitionSpec as P

NI = 16
NV = 5
NBR = 6
NEAR = 4
SLOTS = 4
OFFSETS = (1, -1, 2, -2)
LANES = 128
ROWS = 16
HALF = 8
BLOCKS = 8


def spectral(diff):
    diff = diff % NI
    if diff == 0:
        return 0.0
    angle = math.pi * diff / NI
    return 0.5 * (-1) ** diff * math.cos(angle) / math.sin(angle)


def dense(x):
    lead = x.shape[1:-1]
    n = len(lead)
    y = x.reshape((2,) + lead + (BLOCKS, LANES))
    y = y.transpose(tuple(range(1, n + 1)) + (n + 1, 0, n + 2))
    return y.reshape(lead + (ROWS, LANES))


def undense(y):
    lead = y.shape[:-2]
    n = len(lead)
    y = y.reshape(lead + (BLOCKS, 2, LANES))
    y = y.transpose((n + 1,) + tuple(range(n)) + (n, n + 2))
    return y.reshape((2,) + lead + (BLOCKS * LANES,))


def row_iota():
    return lax.broadcasted_iota(jnp.int32, (HALF, LANES), 0)


def pick_lanes(x, index):
    return jnp.take_along_axis(x, index, axis=1, mode="promise_in_bounds")


def pick_rows(x, index):
    return jnp.take_along_axis(x, index, axis=0, mode="promise_in_bounds")


def fill_table(half, value, var, table):
    parity = row_iota() & 1
    for q in range(4):
        table[var, 4 * half + q] = pick_rows(value, parity + 2 * q)


def pick(table, var, lane, masks):
    got = pick_lanes(table[var, 0], lane)
    for block in range(1, len(masks)):
        got = jnp.where(masks[block], pick_lanes(table[var, block], lane), got)
    return got


def split(index, blocks):
    high = lax.shift_right_logical(index, 7)
    return index & (LANES - 1), [high == block for block in range(blocks)]


def send_blocks(table, sends, rows, outs):
    for slot in range(SLOTS):
        rows[2 * slot : 2 * slot + 2, :] = jnp.broadcast_to(sends[slot : slot + 1, :], (2, LANES))
    lane, masks = split(rows[...], BLOCKS)
    parity = row_iota() & 1
    for var in range(NV):
        got = pick(table, var, lane, masks)
        for slot in range(SLOTS):
            outs[slot][var] = pick_rows(got, parity + 2 * slot)


def prep_kernel(adj, sends, out0, out1, out2, out3, copies, table, rows):
    for var in range(NV):
        for half in range(2):
            value = adj[var, half * HALF : (half + 1) * HALF, :]
            fill_table(half, value, var, table)
            for peer in range(8):
                at = var * ROWS + half * HALF
                copies[peer, at : at + HALF, :] = value
    send_blocks(table, sends, rows, (out0, out1, out2, out3))


def sweep_kernel(last, *refs):
    count, cur, every, h0, h1, h2, h3, jac, dinv, grad, vol, cols = refs[:12]
    halos = (h0, h1, h2, h3)
    if last:
        out, table, wide = refs[12:]
    else:
        sends, out, out0, out1, out2, out3, copies, table, wide, rows = refs[12:]
    me = lax.axis_index("inst")
    row = row_iota()
    parity = row & 1
    odd = parity == 1
    for var in range(NV):
        for half in range(2):
            fill_table(half, cur[var, half * HALF : (half + 1) * HALF, :], var, table)
    for k in range(NBR):
        for block in range(BLOCKS):
            one = cols[k : k + 1, block * LANES : (block + 1) * LANES]
            wide[k, 2 * block : 2 * block + 2, :] = jnp.broadcast_to(one, (2, LANES))
    fresh = []
    for half in range(2):
        here = slice(half * HALF, (half + 1) * HALF)
        coupling = [jnp.zeros((HALF, LANES), jnp.float32) for _ in range(NV)]
        for k in range(NBR):
            index = wide[k, here, :]
            if k < NEAR:
                lane, masks = split(index, BLOCKS)
            else:
                lane, masks = split(index - BLOCKS * LANES, SLOTS)
            for var in range(NV):
                if k < NEAR:
                    got = pick(table, var, lane, masks)
                else:
                    got = pick_lanes(halos[0][var], lane)
                    for slot in range(1, SLOTS):
                        got = jnp.where(masks[slot], pick_lanes(halos[slot][var], lane), got)
                for i in range(NV):
                    coupling[i] = coupling[i] + jac[k, i, var, here, :] * got
        volume = pick_rows(vol[...], lax.shift_right_logical(row, 1) + 4 * half)
        rest = []
        for var in range(NV):
            same = jnp.zeros((HALF, LANES), jnp.float32)
            cross = jnp.zeros((HALF, LANES), jnp.float32)
            for r in range(8):
                other = lax.rem(me + r, 8)
                at = var * ROWS + half * HALF
                value = every[other, at : at + HALF, :]
                if r:
                    same = same + spectral(2 * r) * value
                factor = jnp.where(odd, spectral(2 * r + 1), spectral(2 * r - 1))
                cross = cross + factor.astype(jnp.float32) * value
            timewise = same + pick_rows(cross, row ^ 1)
            rest.append(grad[var, here, :] - coupling[var] - volume * timewise)
        cell = (4 * half + lax.shift_right_logical(row, 1)) * LANES
        cell = cell + lax.broadcasted_iota(jnp.int32, (HALF, LANES), 1)
        live = (cell < count[0]).astype(jnp.float32)
        for i in range(NV):
            total = dinv[i, 0, here, :] * rest[0]
            for var in range(1, NV):
                total = total + dinv[i, var, here, :] * rest[var]
            total = live * total
            out[i, here, :] = total
            if not last:
                fresh.append((half, total, i))
                at = i * ROWS + half * HALF
                for peer in range(8):
                    copies[peer, at : at + HALF, :] = total
    if not last:
        for half, total, i in fresh:
            fill_table(half, total, i, table)
        send_blocks(table, sends, rows, (out0, out1, out2, out3))


VMEM = pl.BlockSpec(memory_space=pltpu.VMEM)
SMEM = pl.BlockSpec(memory_space=pltpu.SMEM)
PARAMS = pltpu.CompilerParams(vmem_limit_bytes=8 * 1024 * 1024)
TABLE = pltpu.VMEM((NV, BLOCKS, HALF, LANES), jnp.float32)
WIDE = pltpu.VMEM((NBR, ROWS, LANES), jnp.int32)
SENT = jax.ShapeDtypeStruct((NV, HALF, LANES), jnp.float32)
CURRENT = jax.ShapeDtypeStruct((NV, ROWS, LANES), jnp.float32)
COPIES = jax.ShapeDtypeStruct((8, NV * ROWS, LANES), jnp.float32)
ROW_INDEX = pltpu.VMEM((HALF, LANES), jnp.int32)


def exchange(blocks, copies):
    arrived = []
    for block, offset in zip(blocks, OFFSETS):
        count = lax.axis_size("dom")
        pairs = [(source, (source + offset) % count) for source in range(count)]
        arrived.append(lax.ppermute(block, "dom", pairs))
    return arrived, lax.all_to_all(copies, "inst", 0, 0)


def on_device(adjoint, gradient, jac_blocks, diag_inverse, volume, columns, send_rows, counts):
    cur, grad, jac, dinv = dense(adjoint), dense(gradient), dense(jac_blocks), dense(diag_inverse)
    vol = volume.reshape(BLOCKS, LANES)
    *blocks, copies = pl.pallas_call(
        prep_kernel,
        out_shape=(SENT,) * SLOTS + (COPIES,),
        in_specs=[VMEM] * 2,
        out_specs=(VMEM,) * 5,
        scratch_shapes=[TABLE, ROW_INDEX],
        compiler_params=PARAMS,
        name="prep",
    )(cur, send_rows)
    arrived, every = exchange(blocks, copies)
    cur, *blocks, copies = pl.pallas_call(
        functools.partial(sweep_kernel, False),
        out_shape=(CURRENT,) + (SENT,) * SLOTS + (COPIES,),
        in_specs=[SMEM] + [VMEM] * 12,
        out_specs=(VMEM,) * 6,
        scratch_shapes=[TABLE, WIDE, ROW_INDEX],
        compiler_params=PARAMS,
        name="sweep_one",
    )(counts, cur, every, *arrived, jac, dinv, grad, vol, columns, send_rows)
    arrived, every = exchange(blocks, copies)
    cur = pl.pallas_call(
        functools.partial(sweep_kernel, True),
        out_shape=CURRENT,
        in_specs=[SMEM] + [VMEM] * 11,
        out_specs=VMEM,
        scratch_shapes=[TABLE, WIDE],
        compiler_params=PARAMS,
        name="sweep_two",
    )(counts, cur, every, *arrived, jac, dinv, grad, vol, columns)
    return undense(cur)


def solution(mesh):
    in_specs = (
        P("inst", None, "dom"),
        P("inst", None, "dom"),
        P("inst", None, None, None, "dom"),
        P("inst", None, None, "dom"),
        P("dom"),
        P(None, "dom"),
        P("dom", None),
        P("dom"),
    )
    out_specs = P("inst", None, "dom")
    return jax.shard_map(
        on_device, mesh=mesh, in_specs=in_specs, out_specs=out_specs, check_vma=False
    )
```

time: 483 us -> 76 us (0.16)
  the two profiles are of different devices: /device:TPU:1 before, /device:TPU:118 now
where the time goes in v1:
time: 76 us; the launch traced here: 75 us
  starting transfers between devices  50.1 us (66%)
  waiting for transfers between devices  13.4 us (18%)
  local copies, waits for them, and re-layouts  7.38 us (10%)
  Pallas kernels  3.29 us (4%)
  between operations  0.81 us (1%)
    ppermute x8, starting transfers between devices, exchange(): arrived.append(lax.ppermute(block, 'dom', pairs))  26.2 us
    all_to_all x2, starting transfers between devices, exchange(): return (arrived, lax.all_to_all(copies, 'inst', 0, 0))  23.9 us
    ppermute x8, waiting for transfers between devices, exchange(): arrived.append(lax.ppermute(block, 'dom', pairs))  13.4 us
    unnamed x28, local copies, waits for them, and re-layouts  7.38 us
  transfers between devices with their start and end apart: 10, of which 2 were waited for; matrix products, arithmetic and copies ran while one was open for 0% of the time, Pallas kernels for 0%

profile of v1, /device:TPU:118, one launch (start us, length us, event | category | flops | bytes accessed | tf_op | source)
XLA Modules:
  0.0 75.0 jit_solution(9346413447998851706)
XLA Ops:
  0.0 0.0 copy-start.4
  0.0 0.8 %copy-done.4 = f32[2,5,1024]{2,0,1:T(2,128)S(1)} copy-done((f32[2,5,1024]{2,0,1:T(2,128)S(1)}, f32[2,5,1024]{2,0,1:T(2,128)}, u32[]{:S(2)}) %copy-start.4) | copy-done | bytes 40984
  0.8 0.0 copy-start.12
  0.8 0.7 copy-done.12
  1.5 0.8 %prep.1 = (f32[5,8,128]{2,1,0:T(8,128)S(1)}, f32[5,8,128]{2,1,0:T(8,128)S(1)}, f32[5,8,128]{2,1,0:T(8,128)S(1)}, f32[5,8,128]{2,1,0:T(8,128)S(1)}, f32[8,80,128]{2,1,0:T(8,128)}) custom-call(f32[5,16,128]{2,1,0:T(8,128)S(1)} %bitcast.30, s32[4,128]{1,0:T(4,128)S(1)} %copy-done.12), custom_call_target="tpu_custom_call" | custom-call | tf_op jit(solution)/shard_map/prep/pallas_call | solution.py:194
  2.2 16.7 %all-to-all-start = ((f32[8,80,128]{2,1,0:T(8,128)}), f32[8,80,128]{2,1,0:T(8,128)S(1)}, u32[]{:S(2)}, u32[]{:S(2)}) async-start(f32[8,80,128]{2,1,0:T(8,128)} %get-tuple-element.16), calls=%async_computation | async-start | bytes 655360 | tf_op jit(solution)/shard_map/all_to_all | solution.py:188
  18.9 1.9 %collective-permute-start = (f32[5,8,128]{2,1,0:T(8,128)S(1)}, f32[5,8,128]{2,1,0:T(8,128)S(1)}, u32[]{:S(2)}, u32[]{:S(2)}) collective-permute-start(f32[5,8,128]{2,1,0:T(8,128)S(1)} %get-tuple-element.17), channel_id=1, source_target_pairs={{0,8},{8,16},{16,24},{24,32},{32,40},{40,48},{48,56},{56,64},{64,7... | collective-permute-start | bytes 61448 | tf_op jit(solution)/shard_map/ppermute | solution.py:187
  20.8 3.6 %collective-permute-start.1 = (f32[5,8,128]{2,1,0:T(8,128)S(1)}, f32[5,8,128]{2,1,0:T(8,128)S(1)}, u32[]{:S(2)}, u32[]{:S(2)}) collective-permute-start(f32[5,8,128]{2,1,0:T(8,128)S(1)} %get-tuple-element.18), channel_id=1, source_target_pairs={{0,1016},{8,0},{16,8},{24,16},{32,24},{40,32},{48,40},{56,48},{64,... | collective-permute-start | bytes 61448 | tf_op jit(solution)/shard_map/ppermute | solution.py:187
  24.5 6.3 %collective-permute-start.2 = (f32[5,8,128]{2,1,0:T(8,128)S(1)}, f32[5,8,128]{2,1,0:T(8,128)S(1)}, u32[]{:S(2)}, u32[]{:S(2)}) collective-permute-start(f32[5,8,128]{2,1,0:T(8,128)S(1)} %get-tuple-element.19), channel_id=1, source_target_pairs={{0,16},{8,24},{16,32},{24,40},{32,48},{40,56},{48,64},{56,72},{64,... | collective-permute-start | bytes 61448 | tf_op jit(solution)/shard_map/ppermute | solution.py:187
  30.8 1.9 %collective-permute-start.3 = (f32[5,8,128]{2,1,0:T(8,128)S(1)}, f32[5,8,128]{2,1,0:T(8,128)S(1)}, u32[]{:S(2)}, u32[]{:S(2)}) collective-permute-start(f32[5,8,128]{2,1,0:T(8,128)S(1)} %get-tuple-element.20), channel_id=1, source_target_pairs={{0,1008},{8,1016},{16,0},{24,8},{32,16},{40,24},{48,32},{56,40},{6... | collective-permute-start | bytes 61448 | tf_op jit(solution)/shard_map/ppermute | solution.py:187
  33.4 0.0 collective-permute-done.refs_3_
  33.4 0.0 collective-permute-done.1.refs_4_
  33.4 0.0 collective-permute-done.2.refs_5_
  33.4 6.4 %collective-permute-done.3.refs_6_ = f32[5,8,128]{2,1,0:T(8,128)S(1)} collective-permute-done((f32[5,8,128]{2,1,0:T(8,128)S(1)}, f32[5,8,128]{2,1,0:T(8,128)S(1)}, u32[]{:S(2)}, u32[]{:S(2)}) %collective-permute-start.3) | collective-permute-done | bytes 20512 | tf_op jit(solution)/shard_map/ppermute | solution.py:187
  39.8 0.0 all-to-all-done.refs_2_
  39.8 0.0 copy-start
  39.8 1.3 %copy-done = f32[2,6,5,5,1024]{4,0,3,2,1:T(2,128)S(1)} copy-done((f32[2,6,5,5,1024]{4,0,3,2,1:T(2,128)S(1)}, f32[2,6,5,5,1024]{4,0,3,2,1:T(2,128)}, u32[]{:S(2)}) %copy-start) | copy-done | bytes 1228824
  41.1 0.0 copy-start.2
  41.1 0.9 %copy-done.2 = f32[2,5,5,1024]{3,0,2,1:T(2,128)S(1)} copy-done((f32[2,5,5,1024]{3,0,2,1:T(2,128)S(1)}, f32[2,5,5,1024]{3,0,2,1:T(2,128)}, u32[]{:S(2)}) %copy-start.2) | copy-done | bytes 204824
  42.0 0.0 copy-start.5
  42.0 0.8 %copy-done.5 = f32[2,5,1024]{2,0,1:T(2,128)S(1)} copy-done((f32[2,5,1024]{2,0,1:T(2,128)S(1)}, f32[2,5,1024]{2,0,1:T(2,128)}, u32[]{:S(2)}) %copy-start.5) | copy-done | bytes 40984
  42.8 0.0 copy-start.6
  42.8 0.8 %copy-done.6 = f32[2,5,1024]{2,0,1:T(2,128)S(1)} copy-done((f32[2,5,1024]{2,0,1:T(2,128)S(1)}, f32[2,5,1024]{2,0,1:T(2,128)}, u32[]{:S(2)}) %copy-start.6) | copy-done | bytes 40984
  43.6 0.0 copy-start.8
  43.6 0.8 %copy-done.8 = s32[6,1024]{1,0:T(8,128)S(1)} copy-done((s32[6,1024]{1,0:T(8,128)S(1)}, s32[6,1024]{1,0:T(8,128)}, u32[]{:S(2)}) %copy-start.8) | copy-done | bytes 24600
  44.3 0.0 copy-start.10
  44.3 0.7 copy-done.10
  45.0 0.0 copy-start.13
  45.0 0.7 copy-done.13
  45.7 0.0 copy-start.1
  45.7 0.0 copy-start.3
  45.7 0.0 copy-start.7
  45.7 0.0 copy-start.9
  45.7 0.0 copy-start.11
  45.7 1.3 %sweep_one.1 = (f32[5,16,128]{2,1,0:T(8,128)S(1)}, f32[5,8,128]{2,1,0:T(8,128)S(1)}, f32[5,8,128]{2,1,0:T(8,128)S(1)}, f32[5,8,128]{2,1,0:T(8,128)S(1)}, f32[5,8...) custom-call(s32[1]{0:T(128)S(6)} %copy.14.refs_0_, f32[5,16,128]{2,1,0:T(8,128)S(1)} %bitcast.31, ...), custom_call_target="tpu_custom_call" | custom-call | tf_op jit(solution)/shard_map/sweep_one/pallas_call | solution.py:204
  47.1 7.2 %all-to-all-start.1 = ((f32[8,80,128]{2,1,0:T(8,128)}), f32[8,80,128]{2,1,0:T(8,128)S(1)}, u32[]{:S(2)}, u32[]{:S(2)}) async-start(f32[8,80,128]{2,1,0:T(8,128)} %get-tuple-element.22), calls=%async_computation.1 | async-start | bytes 655360 | tf_op jit(solution)/shard_map/all_to_all | solution.py:188
  54.3 1.9 %collective-permute-start.4 = (f32[5,8,128]{2,1,0:T(8,128)S(1)}, f32[5,8,128]{2,1,0:T(8,128)S(1)}, u32[]{:S(2)}, u32[]{:S(2)}) collective-permute-start(f32[5,8,128]{2,1,0:T(8,128)S(1)} %get-tuple-element.23), channel_id=1, source_target_pairs={{0,8},{8,16},{16,24},{24,32},{32,40},{40,48},{48,56},{56,64},{64,7... | collective-permute-start | bytes 61448 | tf_op jit(solution)/shard_map/ppermute | solution.py:187
  56.2 3.6 %collective-permute-start.5 = (f32[5,8,128]{2,1,0:T(8,128)S(1)}, f32[5,8,128]{2,1,0:T(8,128)S(1)}, u32[]{:S(2)}, u32[]{:S(2)}) collective-permute-start(f32[5,8,128]{2,1,0:T(8,128)S(1)} %get-tuple-element.24), channel_id=1, source_target_pairs={{0,1016},{8,0},{16,8},{24,16},{32,24},{40,32},{48,40},{56,48},{64,... | collective-permute-start | bytes 61448 | tf_op jit(solution)/shard_map/ppermute | solution.py:187
  59.9 5.0 %collective-permute-start.6 = (f32[5,8,128]{2,1,0:T(8,128)S(1)}, f32[5,8,128]{2,1,0:T(8,128)S(1)}, u32[]{:S(2)}, u32[]{:S(2)}) collective-permute-start(f32[5,8,128]{2,1,0:T(8,128)S(1)} %get-tuple-element.25), channel_id=1, source_target_pairs={{0,16},{8,24},{16,32},{24,40},{32,48},{40,56},{48,64},{56,72},{64,... | collective-permute-start | bytes 61448 | tf_op jit(solution)/shard_map/ppermute | solution.py:187
  64.8 1.9 %collective-permute-start.7 = (f32[5,8,128]{2,1,0:T(8,128)S(1)}, f32[5,8,128]{2,1,0:T(8,128)S(1)}, u32[]{:S(2)}, u32[]{:S(2)}) collective-permute-start(f32[5,8,128]{2,1,0:T(8,128)S(1)} %get-tuple-element.26), channel_id=1, source_target_pairs={{0,1008},{8,1016},{16,0},{24,8},{32,16},{40,24},{48,32},{56,40},{6... | collective-permute-start | bytes 61448 | tf_op jit(solution)/shard_map/ppermute | solution.py:187
  66.7 0.0 collective-permute-done.4.refs_3_
  66.8 0.0 collective-permute-done.5.refs_4_
  66.8 0.0 collective-permute-done.6.refs_5_
  66.8 7.0 %collective-permute-done.7.refs_6_ = f32[5,8,128]{2,1,0:T(8,128)S(1)} collective-permute-done((f32[5,8,128]{2,1,0:T(8,128)S(1)}, f32[5,8,128]{2,1,0:T(8,128)S(1)}, u32[]{:S(2)}, u32[]{:S(2)}) %collective-permute-start.7) | collective-permute-done | bytes 20512 | tf_op jit(solution)/shard_map/ppermute | solution.py:187
  73.8 0.0 all-to-all-done.1.refs_2_
  73.8 0.0 copy-done.1
  73.8 0.0 copy-done.3
  73.8 0.0 copy-done.7
  73.8 0.0 copy-done.9
  73.8 0.0 copy-done.11
  73.9 1.2 %sweep_two.1 = f32[5,16,128]{2,1,0:T(8,128)} custom-call(s32[1]{0:T(128)S(6)} %copy.14.refs_0_, f32[5,16,128]{2,1,0:T(8,128)S(1)} %get-tuple-element.21.refs_1_, f32[8,80,128]{2,1,0:T(8,128)S(1)} %all-to-all-done.1.refs_2_, f32[5,8,128]{2,1,0:T(8,128)S(1)} %collective-permute-done.4.refs_3_, f32[5,8,128]{2,1,0:T(8,128)S(1)} %collective-permute-done.5.refs_4_, ...), custom_call_target="tpu_custom_call" | custom-call | tf_op jit(solution)/shard_map/sweep_two/pallas_call | solution.py:214
Async XLA Ops:
  0.0 0.8 %copy-start.4 = (f32[2,5,1024]{2,0,1:T(2,128)S(1)}, f32[2,5,1024]{2,0,1:T(2,128)}, u32[]{:S(2)}) copy-start(f32[2,5,1024]{2,0,1:T(2,128)} %param.8) | copy-start | bytes 122884
  0.8 0.7 copy-start.12
  2.2 37.6 %all-to-all-start = ((f32[8,80,128]{2,1,0:T(8,128)}), f32[8,80,128]{2,1,0:T(8,128)S(1)}, u32[]{:S(2)}, u32[]{:S(2)}) async-start(f32[8,80,128]{2,1,0:T(8,128)} %get-tuple-element.16), calls=%async_computation | async-start | bytes 655360 | tf_op jit(solution)/shard_map/all_to_all | solution.py:188
  18.9 14.5 %collective-permute-start = (f32[5,8,128]{2,1,0:T(8,128)S(1)}, f32[5,8,128]{2,1,0:T(8,128)S(1)}, u32[]{:S(2)}, u32[]{:S(2)}) collective-permute-start(f32[5,8,128]{2,1,0:T(8,128)S(1)} %get-tuple-element.17), channel_id=1, source_target_pairs={{0,8},{8,16},{16,24},{24,32},{32,40},{40,48},{48,56},{56,64},{64,7... | collective-permute-start | bytes 61448 | tf_op jit(solution)/shard_map/ppermute | solution.py:187
  20.8 12.6 %collective-permute-start.1 = (f32[5,8,128]{2,1,0:T(8,128)S(1)}, f32[5,8,128]{2,1,0:T(8,128)S(1)}, u32[]{:S(2)}, u32[]{:S(2)}) collective-permute-start(f32[5,8,128]{2,1,0:T(8,128)S(1)} %get-tuple-element.18), channel_id=1, source_target_pairs={{0,1016},{8,0},{16,8},{24,16},{32,24},{40,32},{48,40},{56,48},{64,... | collective-permute-start | bytes 61448 | tf_op jit(solution)/shard_map/ppermute | solution.py:187
  24.5 8.9 %collective-permute-start.2 = (f32[5,8,128]{2,1,0:T(8,128)S(1)}, f32[5,8,128]{2,1,0:T(8,128)S(1)}, u32[]{:S(2)}, u32[]{:S(2)}) collective-permute-start(f32[5,8,128]{2,1,0:T(8,128)S(1)} %get-tuple-element.19), channel_id=1, source_target_pairs={{0,16},{8,24},{16,32},{24,40},{32,48},{40,56},{48,64},{56,72},{64,... | collective-permute-start | bytes 61448 | tf_op jit(solution)/shard_map/ppermute | solution.py:187
  30.8 9.0 %collective-permute-start.3 = (f32[5,8,128]{2,1,0:T(8,128)S(1)}, f32[5,8,128]{2,1,0:T(8,128)S(1)}, u32[]{:S(2)}, u32[]{:S(2)}) collective-permute-start(f32[5,8,128]{2,1,0:T(8,128)S(1)} %get-tuple-element.20), channel_id=1, source_target_pairs={{0,1008},{8,1016},{16,0},{24,8},{32,16},{40,24},{48,32},{56,40},{6... | collective-permute-start | bytes 61448 | tf_op jit(solution)/shard_map/ppermute | solution.py:187
  39.8 1.3 %copy-start = (f32[2,6,5,5,1024]{4,0,3,2,1:T(2,128)S(1)}, f32[2,6,5,5,1024]{4,0,3,2,1:T(2,128)}, u32[]{:S(2)}) copy-start(f32[2,6,5,5,1024]{4,0,3,2,1:T(2,128)} %param.10) | copy-start | bytes 3686404
  41.1 0.9 %copy-start.2 = (f32[2,5,5,1024]{3,0,2,1:T(2,128)S(1)}, f32[2,5,5,1024]{3,0,2,1:T(2,128)}, u32[]{:S(2)}) copy-start(f32[2,5,5,1024]{3,0,2,1:T(2,128)} %param.11) | copy-start | bytes 614404
  42.0 0.8 %copy-start.5 = (f32[2,5,1024]{2,0,1:T(2,128)S(1)}, f32[2,5,1024]{2,0,1:T(2,128)}, u32[]{:S(2)}) copy-start(f32[2,5,1024]{2,0,1:T(2,128)} %param.8) | copy-start | bytes 122884
  42.8 0.8 %copy-start.6 = (f32[2,5,1024]{2,0,1:T(2,128)S(1)}, f32[2,5,1024]{2,0,1:T(2,128)}, u32[]{:S(2)}) copy-start(f32[2,5,1024]{2,0,1:T(2,128)} %param.9) | copy-start | bytes 122884
  43.6 0.8 %copy-start.8 = (s32[6,1024]{1,0:T(8,128)S(1)}, s32[6,1024]{1,0:T(8,128)}, u32[]{:S(2)}) copy-start(s32[6,1024]{1,0:T(8,128)} %refs_11_.3) | copy-start | bytes 73732
  44.3 0.7 copy-start.10
  45.0 0.7 copy-start.13
  45.7 28.1 %copy-start.1 = (f32[2,6,5,5,1024]{4,0,3,2,1:T(2,128)S(1)}, f32[2,6,5,5,1024]{4,0,3,2,1:T(2,128)}, u32[]{:S(2)}) copy-start(f32[2,6,5,5,1024]{4,0,3,2,1:T(2,128)} %param.10) | copy-start | bytes 3686404
  45.7 28.1 %copy-start.3 = (f32[2,5,5,1024]{3,0,2,1:T(2,128)S(1)}, f32[2,5,5,1024]{3,0,2,1:T(2,128)}, u32[]{:S(2)}) copy-start(f32[2,5,5,1024]{3,0,2,1:T(2,128)} %param.11) | copy-start | bytes 614404
  45.7 28.1 %copy-start.7 = (f32[2,5,1024]{2,0,1:T(2,128)S(1)}, f32[2,5,1024]{2,0,1:T(2,128)}, u32[]{:S(2)}) copy-start(f32[2,5,1024]{2,0,1:T(2,128)} %param.9) | copy-start | bytes 122884
  45.7 28.1 %copy-start.9 = (s32[6,1024]{1,0:T(8,128)S(1)}, s32[6,1024]{1,0:T(8,128)}, u32[]{:S(2)}) copy-start(s32[6,1024]{1,0:T(8,128)} %refs_11_.3) | copy-start | bytes 73732
  45.7 28.1 %copy-start.11 = (f32[1024]{0:T(1024)S(1)}, f32[1024]{0:T(1024)}, u32[]{:S(2)}) copy-start(f32[1024]{0:T(1024)} %param.12) | copy-start | bytes 12292
  47.1 26.7 %all-to-all-start.1 = ((f32[8,80,128]{2,1,0:T(8,128)}), f32[8,80,128]{2,1,0:T(8,128)S(1)}, u32[]{:S(2)}, u32[]{:S(2)}) async-start(f32[8,80,128]{2,1,0:T(8,128)} %get-tuple-element.22), calls=%async_computation.1 | async-start | bytes 655360 | tf_op jit(solution)/shard_map/all_to_all | solution.py:188
  54.3 12.5 %collective-permute-start.4 = (f32[5,8,128]{2,1,0:T(8,128)S(1)}, f32[5,8,128]{2,1,0:T(8,128)S(1)}, u32[]{:S(2)}, u32[]{:S(2)}) collective-permute-start(f32[5,8,128]{2,1,0:T(8,128)S(1)} %get-tuple-element.23), channel_id=1, source_target_pairs={{0,8},{8,16},{16,24},{24,32},{32,40},{40,48},{48,56},{56,64},{64,7... | collective-permute-start | bytes 61448 | tf_op jit(solution)/shard_map/ppermute | solution.py:187
  56.2 10.6 %collective-permute-start.5 = (f32[5,8,128]{2,1,0:T(8,128)S(1)}, f32[5,8,128]{2,1,0:T(8,128)S(1)}, u32[]{:S(2)}, u32[]{:S(2)}) collective-permute-start(f32[5,8,128]{2,1,0:T(8,128)S(1)} %get-tuple-element.24), channel_id=1, source_target_pairs={{0,1016},{8,0},{16,8},{24,16},{32,24},{40,32},{48,40},{56,48},{64,... | collective-permute-start | bytes 61448 | tf_op jit(solution)/shard_map/ppermute | solution.py:187
  59.9 6.9 %collective-permute-start.6 = (f32[5,8,128]{2,1,0:T(8,128)S(1)}, f32[5,8,128]{2,1,0:T(8,128)S(1)}, u32[]{:S(2)}, u32[]{:S(2)}) collective-permute-start(f32[5,8,128]{2,1,0:T(8,128)S(1)} %get-tuple-element.25), channel_id=1, source_target_pairs={{0,16},{8,24},{16,32},{24,40},{32,48},{40,56},{48,64},{56,72},{64,... | collective-permute-start | bytes 61448 | tf_op jit(solution)/shard_map/ppermute | solution.py:187
  64.8 9.0 %collective-permute-start.7 = (f32[5,8,128]{2,1,0:T(8,128)S(1)}, f32[5,8,128]{2,1,0:T(8,128)S(1)}, u32[]{:S(2)}, u32[]{:S(2)}) collective-permute-start(f32[5,8,128]{2,1,0:T(8,128)S(1)} %get-tuple-element.26), channel_id=1, source_target_pairs={{0,1008},{8,1016},{16,0},{24,8},{32,16},{40,24},{48,32},{56,40},{6... | collective-permute-start | bytes 61448 | tf_op jit(solution)/shard_map/ppermute | solution.py:187

commit v2 on v1

v2 whole, which is shorter than its diff:
```python
import functools
import math

import jax
import jax.numpy as jnp
from jax import lax
from jax.experimental import pallas as pl
from jax.experimental.pallas import tpu as pltpu
from jax.sharding import PartitionSpec as P

NI = 16
NV = 5
NBR = 6
NEAR = 4
SLOTS = 4
LANES = 128
ROWS = 16
HALF = 8
BLOCKS = 8


def spectral(diff):
    diff = diff % NI
    if diff == 0:
        return 0.0
    angle = math.pi * diff / NI
    return 0.5 * (-1) ** diff * math.cos(angle) / math.sin(angle)


def dense(x):
    lead = x.shape[1:-1]
    n = len(lead)
    y = x.reshape((2,) + lead + (BLOCKS, LANES))
    y = y.transpose(tuple(range(1, n + 1)) + (n + 1, 0, n + 2))
    return y.reshape(lead + (ROWS, LANES))


def undense(y):
    lead = y.shape[:-2]
    n = len(lead)
    y = y.reshape(lead + (BLOCKS, 2, LANES))
    y = y.transpose((n + 1,) + tuple(range(n)) + (n, n + 2))
    return y.reshape((2,) + lead + (BLOCKS * LANES,))


def row_iota():
    return lax.broadcasted_iota(jnp.int32, (HALF, LANES), 0)


def pick_lanes(x, index):
    return jnp.take_along_axis(x, index, axis=1, mode="promise_in_bounds")


def pick_rows(x, index):
    return jnp.take_along_axis(x, index, axis=0, mode="promise_in_bounds")


def fill_table(half, value, var, table):
    parity = row_iota() & 1
    for q in range(4):
        table[var, 4 * half + q] = pick_rows(value, parity + 2 * q)


def pick(table, var, lane, masks):
    got = pick_lanes(table[var, 0], lane)
    for block in range(1, len(masks)):
        got = jnp.where(masks[block], pick_lanes(table[var, block], lane), got)
    return got


def split(index, blocks):
    high = lax.shift_right_logical(index, 7)
    return index & (LANES - 1), [high == block for block in range(blocks)]


def send_blocks(table, rows, swap, own):
    lane, masks = split(rows, BLOCKS)
    parity = row_iota() & 1
    for var in range(NV):
        got = pick(table, var, lane, masks)
        for slot in range(SLOTS):
            out = (swap, swap, own, own)[slot]
            out[slot % 2, var] = pick_rows(got, parity + 2 * slot)


def prep_kernel(adj_hbm, sends_hbm, swap, own, copies, table, rows, adj, sends, sems):
    loads = [
        pltpu.make_async_copy(adj_hbm, adj, sems.at[0]),
        pltpu.make_async_copy(sends_hbm, sends, sems.at[1]),
    ]
    for load in loads:
        load.start()
    for load in loads:
        load.wait()
    for var in range(NV):
        for half in range(2):
            value = adj[var, half * HALF : (half + 1) * HALF, :]
            fill_table(half, value, var, table)
            for peer in range(8):
                at = var * ROWS + half * HALF
                copies[peer, at : at + HALF, :] = value
    for slot in range(SLOTS):
        rows[2 * slot : 2 * slot + 2, :] = jnp.broadcast_to(sends[slot : slot + 1, :], (2, LANES))
    send_blocks(table, rows[...], swap, own)


def pass_on(own, came, plus, minus):
    for var in range(NV):
        plus[0, var] = own[0, var]
        plus[1, var] = came[0, var]
        minus[0, var] = own[1, var]
        minus[1, var] = came[1, var]


def near_picks(table, wide, picked):
    for half in range(2):
        here = slice(half * HALF, (half + 1) * HALF)
        for k in range(NEAR):
            lane, masks = split(wide[k, here, :], BLOCKS)
            for var in range(NV):
                picked[k, var, here, :] = pick(table, var, lane, masks)


def near_sum(jac, picked, near):
    for half in range(2):
        here = slice(half * HALF, (half + 1) * HALF)
        total = [None] * NV
        for k in range(NEAR):
            for var in range(NV):
                got = picked[k, var, here, :]
                for i in range(NV):
                    term = jac[k, i, var, here, :] * got
                    total[i] = term if total[i] is None else total[i] + term
        for i in range(NV):
            near[i, here, :] = total[i]


def near_first(
    table, came, own, cols_hbm, jac_hbm, dinv_hbm, grad_hbm, vol_hbm, count,
    plus, minus, near, wide, jac, dinv, grad, volume, live,
    picked, cols, vol, sems,
):
    pairs = (
        (cols_hbm, cols),
        (jac_hbm, jac),
        (vol_hbm, vol),
        (dinv_hbm, dinv),
        (grad_hbm, grad),
    )
    loads = [pltpu.make_async_copy(a, b, sems.at[n]) for n, (a, b) in enumerate(pairs)]
    for load in loads:
        load.start()
    pass_on(own, came, plus, minus)
    loads[0].wait()
    for k in range(NBR):
        for block in range(BLOCKS):
            one = cols[k : k + 1, block * LANES : (block + 1) * LANES]
            wide[k, 2 * block : 2 * block + 2, :] = jnp.broadcast_to(one, (2, LANES))
    near_picks(table, wide, picked)
    for load in loads[1:]:
        load.wait()
    row = row_iota()
    for half in range(2):
        here = slice(half * HALF, (half + 1) * HALF)
        block = lax.shift_right_logical(row, 1) + 4 * half
        volume[here, :] = pick_rows(vol[...], block)
        cell = block * LANES + lax.broadcasted_iota(jnp.int32, (HALF, LANES), 1)
        live[here, :] = (cell < count[0]).astype(jnp.float32)
    near_sum(jac, picked, near)


def near_second(table, came, own, wide, jac, plus, minus, near, picked):
    pass_on(own, came, plus, minus)
    near_picks(table, wide, picked)
    near_sum(jac, picked, near)


def finish_kernel(last, *refs):
    every, came, above, below, near, wide, jac, dinv, grad, volume, live = refs[:11]
    if last:
        out, halos = refs[11:]
    else:
        rows, swap, own, copies, table, halos = refs[11:]
    me = lax.axis_index("inst")
    first = (lax.axis_index("dom") & 1) == 0
    row = row_iota()
    odd = (row & 1) == 1
    for var in range(NV):
        halos[0, var] = jnp.where(first, above[1, var], came[0, var])
        halos[1, var] = jnp.where(first, came[1, var], below[1, var])
        halos[2, var] = above[0, var]
        halos[3, var] = below[0, var]
    for half in range(2):
        here = slice(half * HALF, (half + 1) * HALF)
        coupling = [near[i, here, :] for i in range(NV)]
        for k in range(NEAR, NBR):
            lane, masks = split(wide[k, here, :] - BLOCKS * LANES, SLOTS)
            for var in range(NV):
                got = pick_lanes(halos[0, var], lane)
                for slot in range(1, SLOTS):
                    got = jnp.where(masks[slot], pick_lanes(halos[slot, var], lane), got)
                for i in range(NV):
                    coupling[i] = coupling[i] + jac[k, i, var, here, :] * got
        rest = []
        for var in range(NV):
            same = jnp.zeros((HALF, LANES), jnp.float32)
            cross = jnp.zeros((HALF, LANES), jnp.float32)
            for r in range(8):
                other = lax.rem(me + r, 8)
                at = var * ROWS + half * HALF
                value = every[other, at : at + HALF, :]
                if r:
                    same = same + spectral(2 * r) * value
                factor = jnp.where(odd, spectral(2 * r + 1), spectral(2 * r - 1))
                cross = cross + factor.astype(jnp.float32) * value
            timewise = same + pick_rows(cross, row ^ 1)
            rest.append(grad[var, here, :] - coupling[var] - volume[here, :] * timewise)
        for i in range(NV):
            total = dinv[i, 0, here, :] * rest[0]
            for var in range(1, NV):
                total = total + dinv[i, var, here, :] * rest[var]
            total = live[here, :] * total
            if last:
                out[i, here, :] = total
            else:
                fill_table(half, total, i, table)
                at = i * ROWS + half * HALF
                for peer in range(8):
                    copies[peer, at : at + HALF, :] = total
    if not last:
        send_blocks(table, rows[...], swap, own)


VMEM = pl.BlockSpec(memory_space=pltpu.VMEM)
HBM = pl.BlockSpec(memory_space=pltpu.HBM)
SMEM = pl.BlockSpec(memory_space=pltpu.SMEM)
PARAMS = pltpu.CompilerParams(vmem_limit_bytes=8 * 1024 * 1024)


def f32(*shape):
    return jax.ShapeDtypeStruct(shape, jnp.float32)


def i32(*shape):
    return jax.ShapeDtypeStruct(shape, jnp.int32)


TABLE = f32(NV, BLOCKS, HALF, LANES)
PAIR = f32(2, NV, HALF, LANES)
CURRENT = f32(NV, ROWS, LANES)
COPIES = f32(8, NV * ROWS, LANES)
WIDE = i32(NBR, ROWS, LANES)
ROW_INDEX = i32(HALF, LANES)
JAC = f32(NBR, NV, NV, ROWS, LANES)
DINV = f32(NV, NV, ROWS, LANES)
CELL = f32(ROWS, LANES)
PICKED = pltpu.VMEM((NEAR, NV, ROWS, LANES), jnp.float32)
HALOS = pltpu.VMEM((SLOTS, NV, HALF, LANES), jnp.float32)


def call(kernel, name, args, outs, scratch, hbm=(), smem=()):
    specs = [HBM if n in hbm else SMEM if n in smem else VMEM for n in range(len(args))]
    args = [
        pltpu.with_memory_space_constraint(arg, pltpu.HBM) if n in hbm else arg
        for n, arg in enumerate(args)
    ]
    return pl.pallas_call(
        kernel,
        out_shape=outs,
        in_specs=specs,
        out_specs=jax.tree.map(lambda _: VMEM, outs),
        scratch_shapes=scratch,
        compiler_params=PARAMS,
        name=name,
    )(*args)


def swapped(value):
    count = lax.axis_size("dom")
    return lax.ppermute(value, "dom", [(source, source ^ 1) for source in range(count)])


def shifted(value, steps):
    count = lax.axis_size("dom")
    pairs = [(source, (source + steps) % count) for source in range(count)]
    return lax.ppermute(value, "dom", pairs)


def on_device(adjoint, gradient, jac_blocks, diag_inverse, volume, columns, send_rows, counts):
    swap, own, copies, table, rows = call(
        prep_kernel,
        "prep",
        (dense(adjoint), send_rows),
        (PAIR, PAIR, COPIES, TABLE, ROW_INDEX),
        [
            pltpu.VMEM(CURRENT.shape, jnp.float32),
            pltpu.VMEM((SLOTS, LANES), jnp.int32),
            pltpu.SemaphoreType.DMA((2,)),
        ],
        hbm=(0, 1),
    )
    came = swapped(swap)
    every = lax.all_to_all(copies, "inst", 0, 0)
    raw = (
        columns,
        dense(jac_blocks),
        dense(diag_inverse),
        dense(gradient),
        volume.reshape(BLOCKS, LANES),
        counts,
    )
    plus, minus, near, wide, jac, dinv, grad, vol, live = call(
        near_first,
        "near_first",
        (table, came, own) + raw,
        (PAIR, PAIR, CURRENT, WIDE, JAC, DINV, CURRENT, CELL, CELL),
        [
            PICKED,
            pltpu.VMEM((NBR, BLOCKS * LANES), jnp.int32),
            pltpu.VMEM((BLOCKS, LANES), jnp.float32),
            pltpu.SemaphoreType.DMA((5,)),
        ],
        hbm=range(3, 8),
        smem=(8,),
    )
    kept = (wide, jac, dinv, grad, vol, live)
    swap, own, copies, table = call(
        functools.partial(finish_kernel, False),
        "finish_first",
        (every, came, shifted(plus, 2), shifted(minus, -2), near) + kept + (rows,),
        (PAIR, PAIR, COPIES, TABLE),
        [HALOS],
    )
    came = swapped(swap)
    every = lax.all_to_all(copies, "inst", 0, 0)
    plus, minus, near = call(
        near_second,
        "near_second",
        (table, came, own, wide, jac),
        (PAIR, PAIR, CURRENT),
        [PICKED],
    )
    out = call(
        functools.partial(finish_kernel, True),
        "finish_second",
        (every, came, shifted(plus, 2), shifted(minus, -2), near) + kept,
        CURRENT,
        [HALOS],
    )
    return undense(out)


def solution(mesh):
    in_specs = (
        P("inst", None, "dom"),
        P("inst", None, "dom"),
        P("inst", None, None, None, "dom"),
        P("inst", None, None, "dom"),
        P("dom"),
        P(None, "dom"),
        P("dom", None),
        P("dom"),
    )
    out_specs = P("inst", None, "dom")
    return jax.shard_map(
        on_device, mesh=mesh, in_specs=in_specs, out_specs=out_specs, check_vma=False
    )
```

time: 76 us -> 59.4 us (0.78)
  the two profiles are of different devices: /device:TPU:118 before, /device:TPU:1 now
where the time goes in v2:
time: 59.4 us; the launch traced here: 58.8 us
  starting transfers between devices  49.7 us (84%)
  Pallas kernels  5.18 us (9%)
  waiting for transfers between devices  3.2 us (5%)
  between operations  0.74 us (1%)
    all_to_all x2, starting transfers between devices, on_device(): every = lax.all_to_all(copies, 'inst', 0, 0)  24.2 us
    ppermute x4, starting transfers between devices, shifted(): return lax.ppermute(value, 'dom', pairs)  19.3 us
    ppermute x2, starting transfers between devices, swapped(): lax.ppermute(value, 'dom', [(source, source ^ 1) for source in range(coun...  6.23 us
    pallas_call x5, Pallas kernels, call(): pl.pallas_call(kernel, out_shape=outs, in_specs=specs, out_specs=jax.tree...  5.18 us
    ppermute x4, waiting for transfers between devices, shifted(): return lax.ppermute(value, 'dom', pairs)  2.14 us
  transfers between devices with their start and end apart: 8, of which 4 were waited for; matrix products, arithmetic and copies ran while one was open for 0% of the time, Pallas kernels for 3%

profile of v2, /device:TPU:1, one launch (start us, length us, event | category | flops | bytes accessed | tf_op | source)
XLA Modules:
  0.0 58.8 jit_solution(2425949491059406123)
XLA Ops:
  0.0 1.5 %prep.1 = (f32[2,5,8,128]{3,2,1,0:T(8,128)S(1)}, f32[2,5,8,128]{3,2,1,0:T(8,128)S(1)}, f32[8,80,128]{2,1,0:T(8,128)}, f32[5,8,8,128]{3,2,1,0:T(8,128)S(1)}, s32[8,128]{1,0:T(8,128)S(1)}) custom-call(f32[5,16,128]{2,1,0:T(8,128)} %bitcast.28, s32[4,128]{1,0:T(4,128)} %sends_hbm.1), custom_call_target="tpu_custom_call" | custom-call | tf_op jit(solution)/shard_map/prep/pallas_call | solution.py:267
  1.6 17.2 %all-to-all-start = ((f32[8,80,128]{2,1,0:T(8,128)}), f32[8,80,128]{2,1,0:T(8,128)S(1)}, u32[]{:S(2)}, u32[]{:S(2)}) async-start(f32[8,80,128]{2,1,0:T(8,128)} %get-tuple-element.26), calls=%async_computation | async-start | bytes 655360 | tf_op jit(solution)/shard_map/all_to_all | solution.py:303
  18.8 2.9 %collective-permute-start = (f32[2,5,8,128]{3,2,1,0:T(8,128)S(1)}, f32[2,5,8,128]{3,2,1,0:T(8,128)S(1)}, u32[]{:S(2)}, u32[]{:S(2)}) collective-permute-start(f32[2,5,8,128]{3,2,1,0:T(8,128)S(1)} %get-tuple-element.27), channel_id=1, source_target_pairs={{0,8},{8,0},{16,24},{24,16},{32,40},{40,32},{48,56},{56,48},{64,72... | collective-permute-start | bytes 122888 | tf_op jit(solution)/shard_map/ppermute | solution.py:280
  22.3 0.2 collective-permute-done.came.refs_1_
  22.5 1.5 %near_first.1 = (f32[2,5,8,128]{3,2,1,0:T(8,128)S(1)}, f32[2,5,8,128]{3,2,1,0:T(8,128)S(1)}, f32[5,16,128]{2,1,0:T(8,128)S(1)}, s32[6,16,128]{2,1,0:T(8,128)S(1)...) custom-call(f32[5,8,8,128]{3,2,1,0:T(8,128)S(1)} %get-tuple-element., ...), custom_call_target="tpu_custom_call" | custom-call | tf_op jit(solution)/shard_map/near_first/pallas_call | solution.py:267
  24.0 3.3 %collective-permute-start.1 = (f32[2,5,8,128]{3,2,1,0:T(8,128)S(1)}, f32[2,5,8,128]{3,2,1,0:T(8,128)S(1)}, u32[]{:S(2)}, u32[]{:S(2)}) collective-permute-start(f32[2,5,8,128]{3,2,1,0:T(8,128)S(1)} %get-tuple-element.30), channel_id=1, source_target_pairs={{0,16},{8,24},{16,32},{24,40},{32,48},{40,56},{48,64},{56,72},{64,... | collective-permute-start | bytes 122888 | tf_op jit(solution)/shard_map/ppermute | solution.py:286
  27.3 6.8 %collective-permute-start.2 = (f32[2,5,8,128]{3,2,1,0:T(8,128)S(1)}, f32[2,5,8,128]{3,2,1,0:T(8,128)S(1)}, u32[]{:S(2)}, u32[]{:S(2)}) collective-permute-start(f32[2,5,8,128]{3,2,1,0:T(8,128)S(1)} %get-tuple-element.31), channel_id=1, source_target_pairs={{0,1008},{8,1016},{16,0},{24,8},{32,16},{40,24},{48,32},{56,40},{6... | collective-permute-start | bytes 122888 | tf_op jit(solution)/shard_map/ppermute | solution.py:286
  34.1 0.0 collective-permute-done.1.refs_2_
  34.1 1.1 %collective-permute-done.2.refs_3_ = f32[2,5,8,128]{3,2,1,0:T(8,128)S(1)} collective-permute-done((f32[2,5,8,128]{3,2,1,0:T(8,128)S(1)}, f32[2,5,8,128]{3,2,1,0:T(8,128)S(1)}, u32[]{:S(2)}, u32[]{:S(2)}) %collective-permute-start.2) | collective-permute-done | bytes 40992 | tf_op jit(solution)/shard_map/ppermute | solution.py:286
  35.2 0.0 all-to-all-done.refs_0_
  35.2 0.9 %finish_first.1 = (f32[2,5,8,128]{3,2,1,0:T(8,128)S(1)}, f32[2,5,8,128]{3,2,1,0:T(8,128)S(1)}, f32[8,80,128]{2,1,0:T(8,128)}, f32[5,8,8,128]{3,2,1,0:T(8,128)S(1)}) custom-call(f32[8,80,128]{2,1,0:T(8,128)S(1)} %all-to-all-done.refs_0_, f32[2,5,8,128]{3,2,1,0:T(8,128)S(1)} %collective-permute-done.came.refs_1_, ...), custom_call_target="tpu_custom_call" | custom-call | tf_op jit(solution)/shard_map/finish_first/pallas_call | solution.py:267
  36.1 6.9 %all-to-all-start.1 = ((f32[8,80,128]{2,1,0:T(8,128)}), f32[8,80,128]{2,1,0:T(8,128)S(1)}, u32[]{:S(2)}, u32[]{:S(2)}) async-start(f32[8,80,128]{2,1,0:T(8,128)} %get-tuple-element.40), calls=%async_computation.1 | async-start | bytes 655360 | tf_op jit(solution)/shard_map/all_to_all | solution.py:335
  43.1 3.4 %collective-permute-start.3 = (f32[2,5,8,128]{3,2,1,0:T(8,128)S(1)}, f32[2,5,8,128]{3,2,1,0:T(8,128)S(1)}, u32[]{:S(2)}, u32[]{:S(2)}) collective-permute-start(f32[2,5,8,128]{3,2,1,0:T(8,128)S(1)} %get-tuple-element.41), channel_id=1, source_target_pairs={{0,8},{8,0},{16,24},{24,16},{32,40},{40,32},{48,56},{56,48},{64,72... | collective-permute-start | bytes 122888 | tf_op jit(solution)/shard_map/ppermute | solution.py:280
  46.4 0.8 %collective-permute-done.3.came.refs_1_ = f32[2,5,8,128]{3,2,1,0:T(8,128)S(1)} collective-permute-done((f32[2,5,8,128]{3,2,1,0:T(8,128)S(1)}, f32[2,5,8,128]{3,2,1,0:T(8,128)S(1)}, u32[]{:S(2)}, u32[]{:S(2)}) %collective-permute-start.3) | collective-permute-done | bytes 40992 | tf_op jit(solution)/shard_map/ppermute | solution.py:280
  47.3 0.4 near_second.1
  47.7 1.9 %collective-permute-start.4 = (f32[2,5,8,128]{3,2,1,0:T(8,128)S(1)}, f32[2,5,8,128]{3,2,1,0:T(8,128)S(1)}, u32[]{:S(2)}, u32[]{:S(2)}) collective-permute-start(f32[2,5,8,128]{3,2,1,0:T(8,128)S(1)} %get-tuple-element.44), channel_id=1, source_target_pairs={{0,16},{8,24},{16,32},{24,40},{32,48},{40,56},{48,64},{56,72},{64,... | collective-permute-start | bytes 122888 | tf_op jit(solution)/shard_map/ppermute | solution.py:286
  49.7 7.3 %collective-permute-start.5 = (f32[2,5,8,128]{3,2,1,0:T(8,128)S(1)}, f32[2,5,8,128]{3,2,1,0:T(8,128)S(1)}, u32[]{:S(2)}, u32[]{:S(2)}) collective-permute-start(f32[2,5,8,128]{3,2,1,0:T(8,128)S(1)} %get-tuple-element.45), channel_id=1, source_target_pairs={{0,1008},{8,1016},{16,0},{24,8},{32,16},{40,24},{48,32},{56,40},{6... | collective-permute-start | bytes 122888 | tf_op jit(solution)/shard_map/ppermute | solution.py:286
  56.9 0.0 collective-permute-done.4.refs_2_
  57.0 1.1 %collective-permute-done.5.refs_3_ = f32[2,5,8,128]{3,2,1,0:T(8,128)S(1)} collective-permute-done((f32[2,5,8,128]{3,2,1,0:T(8,128)S(1)}, f32[2,5,8,128]{3,2,1,0:T(8,128)S(1)}, u32[]{:S(2)}, u32[]{:S(2)}) %collective-permute-start.5) | collective-permute-done | bytes 40992 | tf_op jit(solution)/shard_map/ppermute | solution.py:286
  58.0 0.0 all-to-all-done.1.refs_0_
  58.0 0.8 %finish_second.1 = f32[5,16,128]{2,1,0:T(8,128)} custom-call(f32[8,80,128]{2,1,0:T(8,128)S(1)} %all-to-all-done.1.refs_0_, f32[2,5,8,128]{3,2,1,0:T(8,128)S(1)} %collective-permute-done.3.came.refs_1_, f32[2,5,8,128]{3,2,1,0:T(8,128)S(1)} %collective-permute-done.4.refs_2_, f32[2,5,8,128]{3,2,1,0:T(8,128)S(1)} %collective-permute-done.5.refs_3_, ...), custom_call_target="tpu_custom_call" | custom-call | tf_op jit(solution)/shard_map/finish_second/pallas_call | solution.py:267
Async XLA Ops:
  1.6 33.7 %all-to-all-start = ((f32[8,80,128]{2,1,0:T(8,128)}), f32[8,80,128]{2,1,0:T(8,128)S(1)}, u32[]{:S(2)}, u32[]{:S(2)}) async-start(f32[8,80,128]{2,1,0:T(8,128)} %get-tuple-element.26), calls=%async_computation | async-start | bytes 655360 | tf_op jit(solution)/shard_map/all_to_all | solution.py:303
  18.8 3.7 %collective-permute-start = (f32[2,5,8,128]{3,2,1,0:T(8,128)S(1)}, f32[2,5,8,128]{3,2,1,0:T(8,128)S(1)}, u32[]{:S(2)}, u32[]{:S(2)}) collective-permute-start(f32[2,5,8,128]{3,2,1,0:T(8,128)S(1)} %get-tuple-element.27), channel_id=1, source_target_pairs={{0,8},{8,0},{16,24},{24,16},{32,40},{40,32},{48,56},{56,48},{64,72... | collective-permute-start | bytes 122888 | tf_op jit(solution)/shard_map/ppermute | solution.py:280
  24.0 10.1 %collective-permute-start.1 = (f32[2,5,8,128]{3,2,1,0:T(8,128)S(1)}, f32[2,5,8,128]{3,2,1,0:T(8,128)S(1)}, u32[]{:S(2)}, u32[]{:S(2)}) collective-permute-start(f32[2,5,8,128]{3,2,1,0:T(8,128)S(1)} %get-tuple-element.30), channel_id=1, source_target_pairs={{0,16},{8,24},{16,32},{24,40},{32,48},{40,56},{48,64},{56,72},{64,... | collective-permute-start | bytes 122888 | tf_op jit(solution)/shard_map/ppermute | solution.py:286
  27.3 7.9 %collective-permute-start.2 = (f32[2,5,8,128]{3,2,1,0:T(8,128)S(1)}, f32[2,5,8,128]{3,2,1,0:T(8,128)S(1)}, u32[]{:S(2)}, u32[]{:S(2)}) collective-permute-start(f32[2,5,8,128]{3,2,1,0:T(8,128)S(1)} %get-tuple-element.31), channel_id=1, source_target_pairs={{0,1008},{8,1016},{16,0},{24,8},{32,16},{40,24},{48,32},{56,40},{6... | collective-permute-start | bytes 122888 | tf_op jit(solution)/shard_map/ppermute | solution.py:286
  36.1 21.9 %all-to-all-start.1 = ((f32[8,80,128]{2,1,0:T(8,128)}), f32[8,80,128]{2,1,0:T(8,128)S(1)}, u32[]{:S(2)}, u32[]{:S(2)}) async-start(f32[8,80,128]{2,1,0:T(8,128)} %get-tuple-element.40), calls=%async_computation.1 | async-start | bytes 655360 | tf_op jit(solution)/shard_map/all_to_all | solution.py:335
  43.1 4.2 %collective-permute-start.3 = (f32[2,5,8,128]{3,2,1,0:T(8,128)S(1)}, f32[2,5,8,128]{3,2,1,0:T(8,128)S(1)}, u32[]{:S(2)}, u32[]{:S(2)}) collective-permute-start(f32[2,5,8,128]{3,2,1,0:T(8,128)S(1)} %get-tuple-element.41), channel_id=1, source_target_pairs={{0,8},{8,0},{16,24},{24,16},{32,40},{40,32},{48,56},{56,48},{64,72... | collective-permute-start | bytes 122888 | tf_op jit(solution)/shard_map/ppermute | solution.py:280
  47.7 9.2 %collective-permute-start.4 = (f32[2,5,8,128]{3,2,1,0:T(8,128)S(1)}, f32[2,5,8,128]{3,2,1,0:T(8,128)S(1)}, u32[]{:S(2)}, u32[]{:S(2)}) collective-permute-start(f32[2,5,8,128]{3,2,1,0:T(8,128)S(1)} %get-tuple-element.44), channel_id=1, source_target_pairs={{0,16},{8,24},{16,32},{24,40},{32,48},{40,56},{48,64},{56,72},{64,... | collective-permute-start | bytes 122888 | tf_op jit(solution)/shard_map/ppermute | solution.py:286
  49.7 8.4 %collective-permute-start.5 = (f32[2,5,8,128]{3,2,1,0:T(8,128)S(1)}, f32[2,5,8,128]{3,2,1,0:T(8,128)S(1)}, u32[]{:S(2)}, u32[]{:S(2)}) collective-permute-start(f32[2,5,8,128]{3,2,1,0:T(8,128)S(1)} %get-tuple-element.45), channel_id=1, source_target_pairs={{0,1008},{8,1016},{16,0},{24,8},{32,16},{40,24},{48,32},{56,40},{6... | collective-permute-start | bytes 122888 | tf_op jit(solution)/shard_map/ppermute | solution.py:286

commit v3 on v2

--- a/solution.py
+++ b/solution.py
@@ -104,7 +104,7 @@
     send_blocks(table, rows[...], swap, own)
 
 
-def pass_on(own, came, plus, minus):
+def join_kernel(own, came, plus, minus):
     for var in range(NV):
         plus[0, var] = own[0, var]
         plus[1, var] = came[0, var]
@@ -112,16 +112,33 @@
         minus[1, var] = came[1, var]
 
 
-def near_picks(table, wide, picked):
+def timewise(every, me, var, half):
+    row = row_iota()
+    odd = (row & 1) == 1
+    at = var * ROWS + half * HALF
+    same = jnp.zeros((HALF, LANES), jnp.float32)
+    cross = jnp.zeros((HALF, LANES), jnp.float32)
+    for r in range(8):
+        value = every[lax.rem(me + r, 8), at : at + HALF, :]
+        if r:
+            same = same + spectral(2 * r) * value
+        factor = jnp.where(odd, spectral(2 * r + 1), spectral(2 * r - 1))
+        cross = cross + factor.astype(jnp.float32) * value
+    return same + pick_rows(cross, row ^ 1)
+
+
+def inner(table, every, wide, jac, picked, grad, volume, rest, loads):
+    me = lax.axis_index("inst")
     for half in range(2):
         here = slice(half * HALF, (half + 1) * HALF)
         for k in range(NEAR):
             lane, masks = split(wide[k, here, :], BLOCKS)
             for var in range(NV):
                 picked[k, var, here, :] = pick(table, var, lane, masks)
-
-
-def near_sum(jac, picked, near):
+        for var in range(NV):
+            rest[var, here, :] = timewise(every, me, var, half)
+    for load in loads:
+        load.wait()
     for half in range(2):
         here = slice(half * HALF, (half + 1) * HALF)
         total = [None] * NV
@@ -132,12 +149,12 @@
                     term = jac[k, i, var, here, :] * got
                     total[i] = term if total[i] is None else total[i] + term
         for i in range(NV):
-            near[i, here, :] = total[i]
-
-
-def near_first(
-    table, came, own, cols_hbm, jac_hbm, dinv_hbm, grad_hbm, vol_hbm, count,
-    plus, minus, near, wide, jac, dinv, grad, volume, live,
+            rest[i, here, :] = grad[i, here, :] - total[i] - volume(half) * rest[i, here, :]
+
+
+def inner_first(
+    table, every, cols_hbm, jac_hbm, dinv_hbm, grad_hbm, vol_hbm, count,
+    rest, wide, jac, dinv, grad, volume, live,
     picked, cols, vol, sems,
 ):
     pairs = (
@@ -150,41 +167,39 @@
     loads = [pltpu.make_async_copy(a, b, sems.at[n]) for n, (a, b) in enumerate(pairs)]
     for load in loads:
         load.start()
-    pass_on(own, came, plus, minus)
+    row = row_iota()
+    for half in range(2):
+        cell = (lax.shift_right_logical(row, 1) + 4 * half) * LANES
+        cell = cell + lax.broadcasted_iota(jnp.int32, (HALF, LANES), 1)
+        live[half * HALF : (half + 1) * HALF, :] = (cell < count[0]).astype(jnp.float32)
     loads[0].wait()
     for k in range(NBR):
         for block in range(BLOCKS):
             one = cols[k : k + 1, block * LANES : (block + 1) * LANES]
             wide[k, 2 * block : 2 * block + 2, :] = jnp.broadcast_to(one, (2, LANES))
-    near_picks(table, wide, picked)
-    for load in loads[1:]:
-        load.wait()
-    row = row_iota()
-    for half in range(2):
-        here = slice(half * HALF, (half + 1) * HALF)
-        block = lax.shift_right_logical(row, 1) + 4 * half
-        volume[here, :] = pick_rows(vol[...], block)
-        cell = block * LANES + lax.broadcasted_iota(jnp.int32, (HALF, LANES), 1)
-        live[here, :] = (cell < count[0]).astype(jnp.float32)
-    near_sum(jac, picked, near)
-
-
-def near_second(table, came, own, wide, jac, plus, minus, near, picked):
-    pass_on(own, came, plus, minus)
-    near_picks(table, wide, picked)
-    near_sum(jac, picked, near)
+
+    def spread(half):
+        value = pick_rows(vol[...], lax.shift_right_logical(row, 1) + 4 * half)
+        volume[half * HALF : (half + 1) * HALF, :] = value
+        return value
+
+    inner(table, every, wide, jac, picked, grad, spread, rest, loads[1:])
+
+
+def inner_second(table, every, wide, jac, grad, volume, rest, picked):
+    def here(half):
+        return volume[half * HALF : (half + 1) * HALF, :]
+
+    inner(table, every, wide, jac, picked, grad, here, rest, ())
 
 
 def finish_kernel(last, *refs):
-    every, came, above, below, near, wide, jac, dinv, grad, volume, live = refs[:11]
+    rest, came, above, below, wide, jac, dinv, live = refs[:8]
     if last:
-        out, halos = refs[11:]
+        out, halos = refs[8:]
     else:
-        rows, swap, own, copies, table, halos = refs[11:]
-    me = lax.axis_index("inst")
+        rows, swap, own, copies, table, halos = refs[8:]
     first = (lax.axis_index("dom") & 1) == 0
-    row = row_iota()
-    odd = (row & 1) == 1
     for var in range(NV):
         halos[0, var] = jnp.where(first, above[1, var], came[0, var])
         halos[1, var] = jnp.where(first, came[1, var], below[1, var])
@@ -192,7 +207,7 @@
         halos[3, var] = below[0, var]
     for half in range(2):
         here = slice(half * HALF, (half + 1) * HALF)
-        coupling = [near[i, here, :] for i in range(NV)]
+        left = [rest[i, here, :] for i in range(NV)]
         for k in range(NEAR, NBR):
             lane, masks = split(wide[k, here, :] - BLOCKS * LANES, SLOTS)
             for var in range(NV):
@@ -200,25 +215,11 @@
                 for slot in range(1, SLOTS):
                     got = jnp.where(masks[slot], pick_lanes(halos[slot, var], lane), got)
                 for i in range(NV):
-                    coupling[i] = coupling[i] + jac[k, i, var, here, :] * got
-        rest = []
-        for var in range(NV):
-            same = jnp.zeros((HALF, LANES), jnp.float32)
-            cross = jnp.zeros((HALF, LANES), jnp.float32)
-            for r in range(8):
-                other = lax.rem(me + r, 8)
-                at = var * ROWS + half * HALF
-                value = every[other, at : at + HALF, :]
-                if r:
-                    same = same + spectral(2 * r) * value
-                factor = jnp.where(odd, spectral(2 * r + 1), spectral(2 * r - 1))
-                cross = cross + factor.astype(jnp.float32) * value
-            timewise = same + pick_rows(cross, row ^ 1)
-            rest.append(grad[var, here, :] - coupling[var] - volume[here, :] * timewise)
+                    left[i] = left[i] - jac[k, i, var, here, :] * got
         for i in range(NV):
-            total = dinv[i, 0, here, :] * rest[0]
+            total = dinv[i, 0, here, :] * left[0]
             for var in range(1, NV):
-                total = total + dinv[i, var, here, :] * rest[var]
+                total = total + dinv[i, var, here, :] * left[var]
             total = live[here, :] * total
             if last:
                 out[i, here, :] = total
@@ -234,6 +235,7 @@
 VMEM = pl.BlockSpec(memory_space=pltpu.VMEM)
 HBM = pl.BlockSpec(memory_space=pltpu.HBM)
 SMEM = pl.BlockSpec(memory_space=pltpu.SMEM)
+COST = pl.CostEstimate(flops=1_000_000, bytes_accessed=4_000_000, transcendentals=0)
 PARAMS = pltpu.CompilerParams(vmem_limit_bytes=8 * 1024 * 1024)
 
 
@@ -258,7 +260,7 @@
 HALOS = pltpu.VMEM((SLOTS, NV, HALF, LANES), jnp.float32)
 
 
-def call(kernel, name, args, outs, scratch, hbm=(), smem=()):
+def call(kernel, name, args, outs, scratch=(), hbm=(), smem=(), cost=None):
     specs = [HBM if n in hbm else SMEM if n in smem else VMEM for n in range(len(args))]
     args = [
         pltpu.with_memory_space_constraint(arg, pltpu.HBM) if n in hbm else arg
@@ -271,6 +273,7 @@
         out_specs=jax.tree.map(lambda _: VMEM, outs),
         scratch_shapes=scratch,
         compiler_params=PARAMS,
+        cost_estimate=cost,
         name=name,
     )(*args)
 
@@ -301,6 +304,8 @@
     )
     came = swapped(swap)
     every = lax.all_to_all(copies, "inst", 0, 0)
+    plus, minus = call(join_kernel, "join_first", (own, came), (PAIR, PAIR))
+    above, below = shifted(plus, 2), shifted(minus, -2)
     raw = (
         columns,
         dense(jac_blocks),
@@ -309,41 +314,44 @@
         volume.reshape(BLOCKS, LANES),
         counts,
     )
-    plus, minus, near, wide, jac, dinv, grad, vol, live = call(
-        near_first,
-        "near_first",
-        (table, came, own) + raw,
-        (PAIR, PAIR, CURRENT, WIDE, JAC, DINV, CURRENT, CELL, CELL),
+    rest, wide, jac, dinv, grad, vol, live = call(
+        inner_first,
+        "inner_first",
+        (table, every) + raw,
+        (CURRENT, WIDE, JAC, DINV, CURRENT, CELL, CELL),
         [
             PICKED,
             pltpu.VMEM((NBR, BLOCKS * LANES), jnp.int32),
             pltpu.VMEM((BLOCKS, LANES), jnp.float32),
             pltpu.SemaphoreType.DMA((5,)),
         ],
-        hbm=range(3, 8),
-        smem=(8,),
-    )
-    kept = (wide, jac, dinv, grad, vol, live)
+        hbm=range(2, 7),
+        smem=(7,),
+        cost=COST,
+    )
     swap, own, copies, table = call(
         functools.partial(finish_kernel, False),
         "finish_first",
-        (every, came, shifted(plus, 2), shifted(minus, -2), near) + kept + (rows,),
+        (rest, came, above, below, wide, jac, dinv, live, rows),
         (PAIR, PAIR, COPIES, TABLE),
         [HALOS],
     )
     came = swapped(swap)
     every = lax.all_to_all(copies, "inst", 0, 0)
-    plus, minus, near = call(
-        near_second,
-        "near_second",
-        (table, came, own, wide, jac),
-        (PAIR, PAIR, CURRENT),
+    plus, minus = call(join_kernel, "join_second", (own, came), (PAIR, PAIR))
+    above, below = shifted(plus, 2), shifted(minus, -2)
+    rest = call(
+        inner_second,
+        "inner_second",
+        (table, every, wide, jac, grad, vol),
+        CURRENT,
         [PICKED],
+        cost=COST,
     )
     out = call(
         functools.partial(finish_kernel, True),
         "finish_second",
-        (every, came, shifted(plus, 2), shifted(minus, -2), near) + kept,
+        (rest, came, above, below, wide, jac, dinv, live),
         CURRENT,
         [HALOS],
     )

time: 59.4 us -> 57.5 us (0.968)
  starting transfers between devices: 49.7 us -> 48.6 us
  waiting for transfers between devices: 3.2 us -> 2.32 us
    ppermute x4, waiting for transfers between devices: 2.14 us -> 0.61 us  [shifted(): return lax.ppermute(value, 'dom', pairs)]
    ppermute x2, waiting for transfers between devices: 1.05 us -> 1.7 us  [swapped(): lax.ppermute(value, 'dom', [(source, source ^ 1) for source in range(coun...]
    pallas_call x5 -> x7, Pallas kernels: 5.18 us -> 5.22 us  [call(): pl.pallas_call(kernel, out_shape=outs, in_specs=specs, out_specs=jax.tree...]
  transfers between devices with their start and end apart: 8 -> 8, of which waited for: 4 -> 3; matrix products, arithmetic and copies ran while one was open for 0% -> 0% of each run, Pallas kernels for 3% -> 3%
where the time goes in v3:
time: 57.5 us; the launch traced here: 56.9 us
  starting transfers between devices  48.6 us (85%)
  Pallas kernels  5.22 us (9%)
  waiting for transfers between devices  2.32 us (4%)
  between operations  0.76 us (1%)
    all_to_all x2, starting transfers between devices, on_device(): every = lax.all_to_all(copies, 'inst', 0, 0)  24.2 us
    ppermute x4, starting transfers between devices, shifted(): return lax.ppermute(value, 'dom', pairs)  18.8 us
    ppermute x2, starting transfers between devices, swapped(): lax.ppermute(value, 'dom', [(source, source ^ 1) for source in range(coun...  5.66 us
    pallas_call x7, Pallas kernels, call(): pl.pallas_call(kernel, out_shape=outs, in_specs=specs, out_specs=jax.tree...  5.22 us
    ppermute x2, waiting for transfers between devices, swapped(): lax.ppermute(value, 'dom', [(source, source ^ 1) for source in range(coun...  1.7 us
  transfers between devices with their start and end apart: 8, of which 3 were waited for; matrix products, arithmetic and copies ran while one was open for 0% of the time, Pallas kernels for 3%

profile of v3, /device:TPU:1, one launch (start us, length us, event | category | flops | bytes accessed | tf_op | source)
XLA Modules:
  0.0 56.9 jit_solution(6424497063655935769)
XLA Ops:
  0.0 1.6 %prep.1 = (f32[2,5,8,128]{3,2,1,0:T(8,128)S(1)}, f32[2,5,8,128]{3,2,1,0:T(8,128)S(1)}, f32[8,80,128]{2,1,0:T(8,128)}, f32[5,8,8,128]{3,2,1,0:T(8,128)S(1)}, s32[8,128]{1,0:T(8,128)S(1)}) custom-call(f32[5,16,128]{2,1,0:T(8,128)} %bitcast.28, s32[4,128]{1,0:T(4,128)} %sends_hbm.1), custom_call_target="tpu_custom_call" | custom-call | tf_op jit(solution)/shard_map/prep/pallas_call | solution.py:269
  1.6 17.2 %all-to-all-start = ((f32[8,80,128]{2,1,0:T(8,128)}), f32[8,80,128]{2,1,0:T(8,128)S(1)}, u32[]{:S(2)}, u32[]{:S(2)}) async-start(f32[8,80,128]{2,1,0:T(8,128)} %get-tuple-element.26), calls=%async_computation | async-start | bytes 655360 | tf_op jit(solution)/shard_map/all_to_all | solution.py:306
  18.8 2.9 %collective-permute-start = (f32[2,5,8,128]{3,2,1,0:T(8,128)S(1)}, f32[2,5,8,128]{3,2,1,0:T(8,128)S(1)}, u32[]{:S(2)}, u32[]{:S(2)}) collective-permute-start(f32[2,5,8,128]{3,2,1,0:T(8,128)S(1)} %get-tuple-element.28), channel_id=1, source_target_pairs={{0,8},{8,0},{16,24},{24,16},{32,40},{40,32},{48,56},{56,48},{64,72... | collective-permute-start | bytes 122888 | tf_op jit(solution)/shard_map/ppermute | solution.py:283
  21.7 0.8 %collective-permute-done.came.refs_1_ = f32[2,5,8,128]{3,2,1,0:T(8,128)S(1)} collective-permute-done((f32[2,5,8,128]{3,2,1,0:T(8,128)S(1)}, f32[2,5,8,128]{3,2,1,0:T(8,128)S(1)}, u32[]{:S(2)}, u32[]{:S(2)}) %collective-permute-start) | collective-permute-done | bytes 40992 | tf_op jit(solution)/shard_map/ppermute | solution.py:283
  22.5 3.3 %collective-permute-start.1 = (f32[2,5,8,128]{3,2,1,0:T(8,128)S(1)}, f32[2,5,8,128]{3,2,1,0:T(8,128)S(1)}, u32[]{:S(2)}, u32[]{:S(2)}) collective-permute-start(f32[2,5,8,128]{3,2,1,0:T(8,128)S(1)} %get-tuple-element.30), channel_id=1, source_target_pairs={{0,16},{8,24},{16,32},{24,40},{32,48},{40,56},{48,64},{56,72},{64,... | collective-permute-start | bytes 122888 | tf_op jit(solution)/shard_map/ppermute | solution.py:289
  25.8 6.8 %collective-permute-start.2 = (f32[2,5,8,128]{3,2,1,0:T(8,128)S(1)}, f32[2,5,8,128]{3,2,1,0:T(8,128)S(1)}, u32[]{:S(2)}, u32[]{:S(2)}) collective-permute-start(f32[2,5,8,128]{3,2,1,0:T(8,128)S(1)} %get-tuple-element.31), channel_id=1, source_target_pairs={{0,1008},{8,1016},{16,0},{24,8},{32,16},{40,24},{48,32},{56,40},{6... | collective-permute-start | bytes 122888 | tf_op jit(solution)/shard_map/ppermute | solution.py:289
  33.3 0.0 all-to-all-done.every
  33.3 1.5 %inner_first.1 = (f32[5,16,128]{2,1,0:T(8,128)S(1)}, s32[6,16,128]{2,1,0:T(8,128)S(1)}, f32[6,5,5,16,128]{4,3,2,1,0:T(8,128)S(1)}, f32[5,5,16,128]{3,2,1,0:T(8,1...) custom-call(f32[5,8,8,128]{3,2,1,0:T(8,128)S(1)} %get-tuple-element.25.table, ...), custom_call_target="tpu_custom_call" | custom-call | flops 1000000 | bytes 4000000 | tf_op jit(solution)/shard_map/inner_first/pallas_call | solution.py:269
  34.8 0.0 collective-permute-done.1.refs_2_
  34.8 0.0 collective-permute-done.2.refs_3_
  34.8 0.9 %finish_first.1 = (f32[2,5,8,128]{3,2,1,0:T(8,128)S(1)}, f32[2,5,8,128]{3,2,1,0:T(8,128)S(1)}, f32[8,80,128]{2,1,0:T(8,128)}, f32[5,8,8,128]{3,2,1,0:T(8,128)S(1)}) custom-call(f32[5,16,128]{2,1,0:T(8,128)S(1)} %get-tuple-element.27.refs_0_, f32[2,5,8,128]{3,2,1,0:T(8,128)S(1)} %collective-permute-done.came.refs_1_, ...), custom_call_target="tpu_custom_call" | custom-call | tf_op jit(solution)/shard_map/finish_first/pallas_call | solution.py:269
  35.7 6.9 %all-to-all-start.1 = ((f32[8,80,128]{2,1,0:T(8,128)}), f32[8,80,128]{2,1,0:T(8,128)S(1)}, u32[]{:S(2)}, u32[]{:S(2)}) async-start(f32[8,80,128]{2,1,0:T(8,128)} %get-tuple-element.38), calls=%async_computation.1 | async-start | bytes 655360 | tf_op jit(solution)/shard_map/all_to_all | solution.py:340
  42.7 2.8 %collective-permute-start.3 = (f32[2,5,8,128]{3,2,1,0:T(8,128)S(1)}, f32[2,5,8,128]{3,2,1,0:T(8,128)S(1)}, u32[]{:S(2)}, u32[]{:S(2)}) collective-permute-start(f32[2,5,8,128]{3,2,1,0:T(8,128)S(1)} %get-tuple-element.41), channel_id=1, source_target_pairs={{0,8},{8,0},{16,24},{24,16},{32,40},{40,32},{48,56},{56,48},{64,72... | collective-permute-start | bytes 122888 | tf_op jit(solution)/shard_map/ppermute | solution.py:283
  45.5 0.8 %collective-permute-done.3.came.refs_1_ = f32[2,5,8,128]{3,2,1,0:T(8,128)S(1)} collective-permute-done((f32[2,5,8,128]{3,2,1,0:T(8,128)S(1)}, f32[2,5,8,128]{3,2,1,0:T(8,128)S(1)}, u32[]{:S(2)}, u32[]{:S(2)}) %collective-permute-start.3) | collective-permute-done | bytes 40992 | tf_op jit(solution)/shard_map/ppermute | solution.py:283
  46.3 1.9 %collective-permute-start.4 = (f32[2,5,8,128]{3,2,1,0:T(8,128)S(1)}, f32[2,5,8,128]{3,2,1,0:T(8,128)S(1)}, u32[]{:S(2)}, u32[]{:S(2)}) collective-permute-start(f32[2,5,8,128]{3,2,1,0:T(8,128)S(1)} %get-tuple-element.43), channel_id=1, source_target_pairs={{0,16},{8,24},{16,32},{24,40},{32,48},{40,56},{48,64},{56,72},{64,... | collective-permute-start | bytes 122888 | tf_op jit(solution)/shard_map/ppermute | solution.py:289
  48.3 6.7 %collective-permute-start.5 = (f32[2,5,8,128]{3,2,1,0:T(8,128)S(1)}, f32[2,5,8,128]{3,2,1,0:T(8,128)S(1)}, u32[]{:S(2)}, u32[]{:S(2)}) collective-permute-start(f32[2,5,8,128]{3,2,1,0:T(8,128)S(1)} %get-tuple-element.44), channel_id=1, source_target_pairs={{0,1008},{8,1016},{16,0},{24,8},{32,16},{40,24},{48,32},{56,40},{6... | collective-permute-start | bytes 122888 | tf_op jit(solution)/shard_map/ppermute | solution.py:289
  55.0 0.0 all-to-all-done.1.every
  55.0 0.4 inner_second.1.refs_0_
  55.5 0.0 collective-permute-done.4.refs_2_
  55.5 0.6 %collective-permute-done.5.refs_3_ = f32[2,5,8,128]{3,2,1,0:T(8,128)S(1)} collective-permute-done((f32[2,5,8,128]{3,2,1,0:T(8,128)S(1)}, f32[2,5,8,128]{3,2,1,0:T(8,128)S(1)}, u32[]{:S(2)}, u32[]{:S(2)}) %collective-permute-start.5) | collective-permute-done | bytes 40992 | tf_op jit(solution)/shard_map/ppermute | solution.py:289
  56.1 0.8 %finish_second.1 = f32[5,16,128]{2,1,0:T(8,128)} custom-call(f32[5,16,128]{2,1,0:T(8,128)S(1)} %inner_second.1.refs_0_, f32[2,5,8,128]{3,2,1,0:T(8,128)S(1)} %collective-permute-done.3.came.refs_1_, f32[2,5,8,128]{3,2,1,0:T(8,128)S(1)} %collective-permute-done.4.refs_2_, f32[2,5,8,128]{3,2,1,0:T(8,128)S(1)} %collective-permute-done.5.refs_3_, ...), custom_call_target="tpu_custom_call" | custom-call | tf_op jit(solution)/shard_map/finish_second/pallas_call | solution.py:269
  (2 shorter events, 0.0 us)
Async XLA Ops:
  1.6 31.7 %all-to-all-start = ((f32[8,80,128]{2,1,0:T(8,128)}), f32[8,80,128]{2,1,0:T(8,128)S(1)}, u32[]{:S(2)}, u32[]{:S(2)}) async-start(f32[8,80,128]{2,1,0:T(8,128)} %get-tuple-element.26), calls=%async_computation | async-start | bytes 655360 | tf_op jit(solution)/shard_map/all_to_all | solution.py:306
  18.8 3.7 %collective-permute-start = (f32[2,5,8,128]{3,2,1,0:T(8,128)S(1)}, f32[2,5,8,128]{3,2,1,0:T(8,128)S(1)}, u32[]{:S(2)}, u32[]{:S(2)}) collective-permute-start(f32[2,5,8,128]{3,2,1,0:T(8,128)S(1)} %get-tuple-element.28), channel_id=1, source_target_pairs={{0,8},{8,0},{16,24},{24,16},{32,40},{40,32},{48,56},{56,48},{64,72... | collective-permute-start | bytes 122888 | tf_op jit(solution)/shard_map/ppermute | solution.py:283
  22.5 12.3 %collective-permute-start.1 = (f32[2,5,8,128]{3,2,1,0:T(8,128)S(1)}, f32[2,5,8,128]{3,2,1,0:T(8,128)S(1)}, u32[]{:S(2)}, u32[]{:S(2)}) collective-permute-start(f32[2,5,8,128]{3,2,1,0:T(8,128)S(1)} %get-tuple-element.30), channel_id=1, source_target_pairs={{0,16},{8,24},{16,32},{24,40},{32,48},{40,56},{48,64},{56,72},{64,... | collective-permute-start | bytes 122888 | tf_op jit(solution)/shard_map/ppermute | solution.py:289
  25.8 9.0 %collective-permute-start.2 = (f32[2,5,8,128]{3,2,1,0:T(8,128)S(1)}, f32[2,5,8,128]{3,2,1,0:T(8,128)S(1)}, u32[]{:S(2)}, u32[]{:S(2)}) collective-permute-start(f32[2,5,8,128]{3,2,1,0:T(8,128)S(1)} %get-tuple-element.31), channel_id=1, source_target_pairs={{0,1008},{8,1016},{16,0},{24,8},{32,16},{40,24},{48,32},{56,40},{6... | collective-permute-start | bytes 122888 | tf_op jit(solution)/shard_map/ppermute | solution.py:289
  35.7 19.3 %all-to-all-start.1 = ((f32[8,80,128]{2,1,0:T(8,128)}), f32[8,80,128]{2,1,0:T(8,128)S(1)}, u32[]{:S(2)}, u32[]{:S(2)}) async-start(f32[8,80,128]{2,1,0:T(8,128)} %get-tuple-element.38), calls=%async_computation.1 | async-start | bytes 655360 | tf_op jit(solution)/shard_map/all_to_all | solution.py:340
  42.7 3.7 %collective-permute-start.3 = (f32[2,5,8,128]{3,2,1,0:T(8,128)S(1)}, f32[2,5,8,128]{3,2,1,0:T(8,128)S(1)}, u32[]{:S(2)}, u32[]{:S(2)}) collective-permute-start(f32[2,5,8,128]{3,2,1,0:T(8,128)S(1)} %get-tuple-element.41), channel_id=1, source_target_pairs={{0,8},{8,0},{16,24},{24,16},{32,40},{40,32},{48,56},{56,48},{64,72... | collective-permute-start | bytes 122888 | tf_op jit(solution)/shard_map/ppermute | solution.py:283
  46.3 9.1 %collective-permute-start.4 = (f32[2,5,8,128]{3,2,1,0:T(8,128)S(1)}, f32[2,5,8,128]{3,2,1,0:T(8,128)S(1)}, u32[]{:S(2)}, u32[]{:S(2)}) collective-permute-start(f32[2,5,8,128]{3,2,1,0:T(8,128)S(1)} %get-tuple-element.43), channel_id=1, source_target_pairs={{0,16},{8,24},{16,32},{24,40},{32,48},{40,56},{48,64},{56,72},{64,... | collective-permute-start | bytes 122888 | tf_op jit(solution)/shard_map/ppermute | solution.py:289
  48.3 7.8 %collective-permute-start.5 = (f32[2,5,8,128]{3,2,1,0:T(8,128)S(1)}, f32[2,5,8,128]{3,2,1,0:T(8,128)S(1)}, u32[]{:S(2)}, u32[]{:S(2)}) collective-permute-start(f32[2,5,8,128]{3,2,1,0:T(8,128)S(1)} %get-tuple-element.44), channel_id=1, source_target_pairs={{0,1008},{8,1016},{16,0},{24,8},{32,16},{40,24},{48,32},{56,40},{6... | collective-permute-start | bytes 122888 | tf_op jit(solution)/shard_map/ppermute | solution.py:289

commit v4 on v3

--- a/solution.py
+++ b/solution.py
@@ -88,20 +88,21 @@
         pltpu.make_async_copy(adj_hbm, adj, sems.at[0]),
         pltpu.make_async_copy(sends_hbm, sends, sems.at[1]),
     ]
-    for load in loads:
-        load.start()
+    repeats = [
+        pltpu.make_async_copy(adj_hbm, copies.at[peer], sems.at[2 + peer]) for peer in range(8)
+    ]
+    for copy in loads + repeats:
+        copy.start()
     for load in loads:
         load.wait()
     for var in range(NV):
         for half in range(2):
-            value = adj[var, half * HALF : (half + 1) * HALF, :]
-            fill_table(half, value, var, table)
-            for peer in range(8):
-                at = var * ROWS + half * HALF
-                copies[peer, at : at + HALF, :] = value
+            fill_table(half, adj[var, half * HALF : (half + 1) * HALF, :], var, table)
     for slot in range(SLOTS):
         rows[2 * slot : 2 * slot + 2, :] = jnp.broadcast_to(sends[slot : slot + 1, :], (2, LANES))
     send_blocks(table, rows[...], swap, own)
+    for copy in repeats:
+        copy.wait()
 
 
 def join_kernel(own, came, plus, minus):
@@ -115,11 +116,11 @@
 def timewise(every, me, var, half):
     row = row_iota()
     odd = (row & 1) == 1
-    at = var * ROWS + half * HALF
+    here = slice(half * HALF, (half + 1) * HALF)
     same = jnp.zeros((HALF, LANES), jnp.float32)
     cross = jnp.zeros((HALF, LANES), jnp.float32)
     for r in range(8):
-        value = every[lax.rem(me + r, 8), at : at + HALF, :]
+        value = every[lax.rem(me + r, 8), var, here, :]
         if r:
             same = same + spectral(2 * r) * value
         factor = jnp.where(odd, spectral(2 * r + 1), spectral(2 * r - 1))
@@ -196,9 +197,10 @@
 def finish_kernel(last, *refs):
     rest, came, above, below, wide, jac, dinv, live = refs[:8]
     if last:
-        out, halos = refs[8:]
+        out, halos, fresh, sems = refs[8:]
     else:
-        rows, swap, own, copies, table, halos = refs[8:]
+        rows, swap, own, copies, table, halos, fresh, sems = refs[8:]
+    writes = []
     first = (lax.axis_index("dom") & 1) == 0
     for var in range(NV):
         halos[0, var] = jnp.where(first, above[1, var], came[0, var])
@@ -221,15 +223,25 @@
             for var in range(1, NV):
                 total = total + dinv[i, var, here, :] * left[var]
             total = live[here, :] * total
+            fresh[i, here, :] = total
+            if not last:
+                fill_table(half, total, i, table)
+        if last:
+            targets = [out]
+        elif half == 1:
+            targets = [copies.at[peer] for peer in range(8)]
+        else:
+            targets = []
+        for target in targets:
+            source = fresh
             if last:
-                out[i, here, :] = total
-            else:
-                fill_table(half, total, i, table)
-                at = i * ROWS + half * HALF
-                for peer in range(8):
-                    copies[peer, at : at + HALF, :] = total
+                source, target = (ref.at[:, pl.ds(half * HALF, HALF), :] for ref in (fresh, target))
+            writes.append(pltpu.make_async_copy(source, target, sems.at[len(writes)]))
+            writes[-1].start()
     if not last:
         send_blocks(table, rows[...], swap, own)
+    for write in writes:
+        write.wait()
 
 
 VMEM = pl.BlockSpec(memory_space=pltpu.VMEM)
@@ -250,17 +262,18 @@
 TABLE = f32(NV, BLOCKS, HALF, LANES)
 PAIR = f32(2, NV, HALF, LANES)
 CURRENT = f32(NV, ROWS, LANES)
-COPIES = f32(8, NV * ROWS, LANES)
+COPIES = f32(8, NV, ROWS, LANES)
 WIDE = i32(NBR, ROWS, LANES)
 ROW_INDEX = i32(HALF, LANES)
 JAC = f32(NBR, NV, NV, ROWS, LANES)
 DINV = f32(NV, NV, ROWS, LANES)
 CELL = f32(ROWS, LANES)
 PICKED = pltpu.VMEM((NEAR, NV, ROWS, LANES), jnp.float32)
+FRESH = pltpu.VMEM((NV, ROWS, LANES), jnp.float32)
 HALOS = pltpu.VMEM((SLOTS, NV, HALF, LANES), jnp.float32)
 
 
-def call(kernel, name, args, outs, scratch=(), hbm=(), smem=(), cost=None):
+def call(kernel, name, args, outs, scratch=(), hbm=(), smem=(), hbm_out=(), cost=None):
     specs = [HBM if n in hbm else SMEM if n in smem else VMEM for n in range(len(args))]
     args = [
         pltpu.with_memory_space_constraint(arg, pltpu.HBM) if n in hbm else arg
@@ -270,7 +283,7 @@
         kernel,
         out_shape=outs,
         in_specs=specs,
-        out_specs=jax.tree.map(lambda _: VMEM, outs),
+        out_specs=jax.tree.map(lambda out: HBM if out in hbm_out else VMEM, outs),
         scratch_shapes=scratch,
         compiler_params=PARAMS,
         cost_estimate=cost,
@@ -298,9 +311,10 @@
         [
             pltpu.VMEM(CURRENT.shape, jnp.float32),
             pltpu.VMEM((SLOTS, LANES), jnp.int32),
-            pltpu.SemaphoreType.DMA((2,)),
+            pltpu.SemaphoreType.DMA((10,)),
         ],
         hbm=(0, 1),
+        hbm_out=(COPIES,),
     )
     came = swapped(swap)
     every = lax.all_to_all(copies, "inst", 0, 0)
@@ -334,7 +348,8 @@
         "finish_first",
         (rest, came, above, below, wide, jac, dinv, live, rows),
         (PAIR, PAIR, COPIES, TABLE),
-        [HALOS],
+        [HALOS, FRESH, pltpu.SemaphoreType.DMA((8,))],
+        hbm_out=(COPIES,),
     )
     came = swapped(swap)
     every = lax.all_to_all(copies, "inst", 0, 0)
@@ -353,7 +368,8 @@
         "finish_second",
         (rest, came, above, below, wide, jac, dinv, live),
         CURRENT,
-        [HALOS],
+        [HALOS, FRESH, pltpu.SemaphoreType.DMA((2,))],
+        hbm_out=(CURRENT,),
     )
     return undense(out)
 

time: 57.5 us -> 67.2 us (1.17)
  Pallas kernels: 5.22 us -> 14.8 us
    pallas_call x7, Pallas kernels: 5.22 us -> 14.8 us  [call(): pl.pallas_call(kernel, out_shape=outs, in_specs=specs, out_specs=jax.tree...]
where the time goes in v4:
time: 67.2 us; the launch traced here: 66.5 us
  starting transfers between devices  48.6 us (72%)
  Pallas kernels  14.8 us (22%)
  waiting for transfers between devices  2.32 us (3%)
  between operations  0.77 us (1%)
    all_to_all x2, starting transfers between devices, on_device(): every = lax.all_to_all(copies, 'inst', 0, 0)  24.2 us
    ppermute x4, starting transfers between devices, shifted(): return lax.ppermute(value, 'dom', pairs)  18.8 us
    pallas_call x7, Pallas kernels, call(): pl.pallas_call(kernel, out_shape=outs, in_specs=specs, out_specs=jax.tree...  14.8 us
    ppermute x2, starting transfers between devices, swapped(): lax.ppermute(value, 'dom', [(source, source ^ 1) for source in range(coun...  5.66 us
    ppermute x2, waiting for transfers between devices, swapped(): lax.ppermute(value, 'dom', [(source, source ^ 1) for source in range(coun...  1.7 us
  transfers between devices with their start and end apart: 8, of which 3 were waited for; matrix products, arithmetic and copies ran while one was open for 0% of the time, Pallas kernels for 3%

profile of v4, /device:TPU:1, one launch (start us, length us, event | category | flops | bytes accessed | tf_op | source)
XLA Modules:
  0.0 66.5 jit_solution(7967872863737938702)
XLA Ops:
  0.0 11.1 %prep.1 = (f32[2,5,8,128]{3,2,1,0:T(8,128)S(1)}, f32[2,5,8,128]{3,2,1,0:T(8,128)S(1)}, f32[8,5,16,128]{3,2,1,0:T(8,128)}, f32[5,8,8,128]{3,2,1,0:T(8,128)S(1)}, s32[8,128]{1,0:T(8,128)S(1)}) custom-call(f32[5,16,128]{2,1,0:T(8,128)} %bitcast.28, s32[4,128]{1,0:T(4,128)} %sends_hbm.1), custom_call_target="tpu_custom_call" | custom-call | tf_op jit(solution)/shard_map/prep/pallas_call | solution.py:282
  11.1 17.2 %all-to-all-start = ((f32[8,5,16,128]{3,2,1,0:T(8,128)}), f32[8,5,16,128]{3,2,1,0:T(8,128)S(1)}, u32[]{:S(2)}, u32[]{:S(2)}) async-start(f32[8,5,16,128]{3,2,1,0:T(8,128)} %get-tuple-element.26), calls=%async_computation | async-start | bytes 655360 | tf_op jit(solution)/shard_map/all_to_all | solution.py:320
  28.4 2.9 %collective-permute-start = (f32[2,5,8,128]{3,2,1,0:T(8,128)S(1)}, f32[2,5,8,128]{3,2,1,0:T(8,128)S(1)}, u32[]{:S(2)}, u32[]{:S(2)}) collective-permute-start(f32[2,5,8,128]{3,2,1,0:T(8,128)S(1)} %get-tuple-element.28), channel_id=1, source_target_pairs={{0,8},{8,0},{16,24},{24,16},{32,40},{40,32},{48,56},{56,48},{64,72... | collective-permute-start | bytes 122888 | tf_op jit(solution)/shard_map/ppermute | solution.py:296
  31.2 0.8 %collective-permute-done.came.refs_1_ = f32[2,5,8,128]{3,2,1,0:T(8,128)S(1)} collective-permute-done((f32[2,5,8,128]{3,2,1,0:T(8,128)S(1)}, f32[2,5,8,128]{3,2,1,0:T(8,128)S(1)}, u32[]{:S(2)}, u32[]{:S(2)}) %collective-permute-start) | collective-permute-done | bytes 40992 | tf_op jit(solution)/shard_map/ppermute | solution.py:296
  32.1 3.3 %collective-permute-start.1 = (f32[2,5,8,128]{3,2,1,0:T(8,128)S(1)}, f32[2,5,8,128]{3,2,1,0:T(8,128)S(1)}, u32[]{:S(2)}, u32[]{:S(2)}) collective-permute-start(f32[2,5,8,128]{3,2,1,0:T(8,128)S(1)} %get-tuple-element.30), channel_id=1, source_target_pairs={{0,16},{8,24},{16,32},{24,40},{32,48},{40,56},{48,64},{56,72},{64,... | collective-permute-start | bytes 122888 | tf_op jit(solution)/shard_map/ppermute | solution.py:302
  35.4 6.8 %collective-permute-start.2 = (f32[2,5,8,128]{3,2,1,0:T(8,128)S(1)}, f32[2,5,8,128]{3,2,1,0:T(8,128)S(1)}, u32[]{:S(2)}, u32[]{:S(2)}) collective-permute-start(f32[2,5,8,128]{3,2,1,0:T(8,128)S(1)} %get-tuple-element.31), channel_id=1, source_target_pairs={{0,1008},{8,1016},{16,0},{24,8},{32,16},{40,24},{48,32},{56,40},{6... | collective-permute-start | bytes 122888 | tf_op jit(solution)/shard_map/ppermute | solution.py:302
  42.9 0.0 all-to-all-done.every
  42.9 1.5 %inner_first.1 = (f32[5,16,128]{2,1,0:T(8,128)S(1)}, s32[6,16,128]{2,1,0:T(8,128)S(1)}, f32[6,5,5,16,128]{4,3,2,1,0:T(8,128)S(1)}, f32[5,5,16,128]{3,2,1,0:T(8,1...) custom-call(f32[5,8,8,128]{3,2,1,0:T(8,128)S(1)} %get-tuple-element.25.table, ...), custom_call_target="tpu_custom_call" | custom-call | flops 1000000 | bytes 4000000 | tf_op jit(solution)/shard_map/inner_first/pallas_call | solution.py:282
  44.4 0.0 collective-permute-done.1.refs_2_
  44.4 0.0 collective-permute-done.2.refs_3_
  44.4 1.0 %finish_first.1 = (f32[2,5,8,128]{3,2,1,0:T(8,128)S(1)}, f32[2,5,8,128]{3,2,1,0:T(8,128)S(1)}, f32[8,5,16,128]{3,2,1,0:T(8,128)}, f32[5,8,8,128]{3,2,1,0:T(8,128)S(1)}) custom-call(f32[5,16,128]{2,1,0:T(8,128)S(1)} %get-tuple-element.27.refs_0_, f32[2,5,8,128]{3,2,1,0:T(8,128)S(1)} %collective-permute-done.came.refs_1_, ...), custom_call_target="tpu_custom_call" | custom-call | tf_op jit(solution)/shard_map/finish_first/pallas_call | solution.py:282
  45.4 6.9 %all-to-all-start.1 = ((f32[8,5,16,128]{3,2,1,0:T(8,128)}), f32[8,5,16,128]{3,2,1,0:T(8,128)S(1)}, u32[]{:S(2)}, u32[]{:S(2)}) async-start(f32[8,5,16,128]{3,2,1,0:T(8,128)} %get-tuple-element.38), calls=%async_computation.1 | async-start | bytes 655360 | tf_op jit(solution)/shard_map/all_to_all | solution.py:355
  52.3 2.8 %collective-permute-start.3 = (f32[2,5,8,128]{3,2,1,0:T(8,128)S(1)}, f32[2,5,8,128]{3,2,1,0:T(8,128)S(1)}, u32[]{:S(2)}, u32[]{:S(2)}) collective-permute-start(f32[2,5,8,128]{3,2,1,0:T(8,128)S(1)} %get-tuple-element.41), channel_id=1, source_target_pairs={{0,8},{8,0},{16,24},{24,16},{32,40},{40,32},{48,56},{56,48},{64,72... | collective-permute-start | bytes 122888 | tf_op jit(solution)/shard_map/ppermute | solution.py:296
  55.1 0.8 %collective-permute-done.3.came.refs_1_ = f32[2,5,8,128]{3,2,1,0:T(8,128)S(1)} collective-permute-done((f32[2,5,8,128]{3,2,1,0:T(8,128)S(1)}, f32[2,5,8,128]{3,2,1,0:T(8,128)S(1)}, u32[]{:S(2)}, u32[]{:S(2)}) %collective-permute-start.3) | collective-permute-done | bytes 40992 | tf_op jit(solution)/shard_map/ppermute | solution.py:296
  56.0 1.9 %collective-permute-start.4 = (f32[2,5,8,128]{3,2,1,0:T(8,128)S(1)}, f32[2,5,8,128]{3,2,1,0:T(8,128)S(1)}, u32[]{:S(2)}, u32[]{:S(2)}) collective-permute-start(f32[2,5,8,128]{3,2,1,0:T(8,128)S(1)} %get-tuple-element.43), channel_id=1, source_target_pairs={{0,16},{8,24},{16,32},{24,40},{32,48},{40,56},{48,64},{56,72},{64,... | collective-permute-start | bytes 122888 | tf_op jit(solution)/shard_map/ppermute | solution.py:302
  57.9 6.7 %collective-permute-start.5 = (f32[2,5,8,128]{3,2,1,0:T(8,128)S(1)}, f32[2,5,8,128]{3,2,1,0:T(8,128)S(1)}, u32[]{:S(2)}, u32[]{:S(2)}) collective-permute-start(f32[2,5,8,128]{3,2,1,0:T(8,128)S(1)} %get-tuple-element.44), channel_id=1, source_target_pairs={{0,1008},{8,1016},{16,0},{24,8},{32,16},{40,24},{48,32},{56,40},{6... | collective-permute-start | bytes 122888 | tf_op jit(solution)/shard_map/ppermute | solution.py:302
  64.7 0.0 all-to-all-done.1.every
  64.7 0.4 inner_second.1.refs_0_
  65.1 0.0 collective-permute-done.4.refs_2_
  65.1 0.6 collective-permute-done.5.refs_3_
  65.7 0.8 %finish_second.1 = f32[5,16,128]{2,1,0:T(8,128)} custom-call(f32[5,16,128]{2,1,0:T(8,128)S(1)} %inner_second.1.refs_0_, f32[2,5,8,128]{3,2,1,0:T(8,128)S(1)} %collective-permute-done.3.came.refs_1_, f32[2,5,8,128]{3,2,1,0:T(8,128)S(1)} %collective-permute-done.4.refs_2_, f32[2,5,8,128]{3,2,1,0:T(8,128)S(1)} %collective-permute-done.5.refs_3_, ...), custom_call_target="tpu_custom_call" | custom-call | tf_op jit(solution)/shard_map/finish_second/pallas_call | solution.py:282
  (2 shorter events, 0.0 us)
Async XLA Ops:
  11.1 31.7 %all-to-all-start = ((f32[8,5,16,128]{3,2,1,0:T(8,128)}), f32[8,5,16,128]{3,2,1,0:T(8,128)S(1)}, u32[]{:S(2)}, u32[]{:S(2)}) async-start(f32[8,5,16,128]{3,2,1,0:T(8,128)} %get-tuple-element.26), calls=%async_computation | async-start | bytes 655360 | tf_op jit(solution)/shard_map/all_to_all | solution.py:320
  28.4 3.7 %collective-permute-start = (f32[2,5,8,128]{3,2,1,0:T(8,128)S(1)}, f32[2,5,8,128]{3,2,1,0:T(8,128)S(1)}, u32[]{:S(2)}, u32[]{:S(2)}) collective-permute-start(f32[2,5,8,128]{3,2,1,0:T(8,128)S(1)} %get-tuple-element.28), channel_id=1, source_target_pairs={{0,8},{8,0},{16,24},{24,16},{32,40},{40,32},{48,56},{56,48},{64,72... | collective-permute-start | bytes 122888 | tf_op jit(solution)/shard_map/ppermute | solution.py:296
  32.1 12.3 %collective-permute-start.1 = (f32[2,5,8,128]{3,2,1,0:T(8,128)S(1)}, f32[2,5,8,128]{3,2,1,0:T(8,128)S(1)}, u32[]{:S(2)}, u32[]{:S(2)}) collective-permute-start(f32[2,5,8,128]{3,2,1,0:T(8,128)S(1)} %get-tuple-element.30), channel_id=1, source_target_pairs={{0,16},{8,24},{16,32},{24,40},{32,48},{40,56},{48,64},{56,72},{64,... | collective-permute-start | bytes 122888 | tf_op jit(solution)/shard_map/ppermute | solution.py:302
  35.4 9.0 %collective-permute-start.2 = (f32[2,5,8,128]{3,2,1,0:T(8,128)S(1)}, f32[2,5,8,128]{3,2,1,0:T(8,128)S(1)}, u32[]{:S(2)}, u32[]{:S(2)}) collective-permute-start(f32[2,5,8,128]{3,2,1,0:T(8,128)S(1)} %get-tuple-element.31), channel_id=1, source_target_pairs={{0,1008},{8,1016},{16,0},{24,8},{32,16},{40,24},{48,32},{56,40},{6... | collective-permute-start | bytes 122888 | tf_op jit(solution)/shard_map/ppermute | solution.py:302
  45.4 19.3 %all-to-all-start.1 = ((f32[8,5,16,128]{3,2,1,0:T(8,128)}), f32[8,5,16,128]{3,2,1,0:T(8,128)S(1)}, u32[]{:S(2)}, u32[]{:S(2)}) async-start(f32[8,5,16,128]{3,2,1,0:T(8,128)} %get-tuple-element.38), calls=%async_computation.1 | async-start | bytes 655360 | tf_op jit(solution)/shard_map/all_to_all | solution.py:355
  52.3 3.7 %collective-permute-start.3 = (f32[2,5,8,128]{3,2,1,0:T(8,128)S(1)}, f32[2,5,8,128]{3,2,1,0:T(8,128)S(1)}, u32[]{:S(2)}, u32[]{:S(2)}) collective-permute-start(f32[2,5,8,128]{3,2,1,0:T(8,128)S(1)} %get-tuple-element.41), channel_id=1, source_target_pairs={{0,8},{8,0},{16,24},{24,16},{32,40},{40,32},{48,56},{56,48},{64,72... | collective-permute-start | bytes 122888 | tf_op jit(solution)/shard_map/ppermute | solution.py:296
  56.0 9.1 %collective-permute-start.4 = (f32[2,5,8,128]{3,2,1,0:T(8,128)S(1)}, f32[2,5,8,128]{3,2,1,0:T(8,128)S(1)}, u32[]{:S(2)}, u32[]{:S(2)}) collective-permute-start(f32[2,5,8,128]{3,2,1,0:T(8,128)S(1)} %get-tuple-element.43), channel_id=1, source_target_pairs={{0,16},{8,24},{16,32},{24,40},{32,48},{40,56},{48,64},{56,72},{64,... | collective-permute-start | bytes 122888 | tf_op jit(solution)/shard_map/ppermute | solution.py:302
  57.9 7.8 %collective-permute-start.5 = (f32[2,5,8,128]{3,2,1,0:T(8,128)S(1)}, f32[2,5,8,128]{3,2,1,0:T(8,128)S(1)}, u32[]{:S(2)}, u32[]{:S(2)}) collective-permute-start(f32[2,5,8,128]{3,2,1,0:T(8,128)S(1)} %get-tuple-element.44), channel_id=1, source_target_pairs={{0,1008},{8,1016},{16,0},{24,8},{32,16},{40,24},{48,32},{56,40},{6... | collective-permute-start | bytes 122888 | tf_op jit(solution)/shard_map/ppermute | solution.py:302

commit v5 on v3

--- a/solution.py
+++ b/solution.py
@@ -83,15 +83,24 @@
             out[slot % 2, var] = pick_rows(got, parity + 2 * slot)
 
 
-def prep_kernel(adj_hbm, sends_hbm, swap, own, copies, table, rows, adj, sends, sems):
-    loads = [
-        pltpu.make_async_copy(adj_hbm, adj, sems.at[0]),
-        pltpu.make_async_copy(sends_hbm, sends, sems.at[1]),
-    ]
+def prep_kernel(
+    adj_hbm, sends_hbm, cols_hbm, jac_hbm, dinv_hbm, grad_hbm, vol_hbm,
+    swap, own, copies, table, rows, cols, jac, dinv, grad, vol,
+    adj, sends, sems,
+):
+    pairs = (
+        (adj_hbm, adj),
+        (sends_hbm, sends),
+        (cols_hbm, cols),
+        (jac_hbm, jac),
+        (dinv_hbm, dinv),
+        (grad_hbm, grad),
+        (vol_hbm, vol),
+    )
+    loads = [pltpu.make_async_copy(a, b, sems.at[n]) for n, (a, b) in enumerate(pairs)]
     for load in loads:
         load.start()
-    for load in loads:
-        load.wait()
+    loads[0].wait()
     for var in range(NV):
         for half in range(2):
             value = adj[var, half * HALF : (half + 1) * HALF, :]
@@ -99,17 +108,53 @@
             for peer in range(8):
                 at = var * ROWS + half * HALF
                 copies[peer, at : at + HALF, :] = value
+    loads[1].wait()
     for slot in range(SLOTS):
         rows[2 * slot : 2 * slot + 2, :] = jnp.broadcast_to(sends[slot : slot + 1, :], (2, LANES))
     send_blocks(table, rows[...], swap, own)
-
-
-def join_kernel(own, came, plus, minus):
+    for load in loads[2:]:
+        load.wait()
+
+
+def join_kernel(own, came, _, plus, minus):
     for var in range(NV):
         plus[0, var] = own[0, var]
         plus[1, var] = came[0, var]
         minus[0, var] = own[1, var]
         minus[1, var] = came[1, var]
+
+
+def near_sum(table, wide, jac, grad, rest):
+    for half in range(2):
+        here = slice(half * HALF, (half + 1) * HALF)
+        left = [grad[i, here, :] for i in range(NV)]
+        for k in range(NEAR):
+            lane, masks = split(wide[k, here, :], BLOCKS)
+            for var in range(NV):
+                got = pick(table, var, lane, masks)
+                for i in range(NV):
+                    left[i] = left[i] - jac[k, i, var, here, :] * got
+        for i in range(NV):
+            rest[i, here, :] = left[i]
+
+
+def near_first(table, cols, jac, grad, vol, count, rest, wide, volume, live):
+    row = row_iota()
+    for half in range(2):
+        here = slice(half * HALF, (half + 1) * HALF)
+        block = lax.shift_right_logical(row, 1) + 4 * half
+        volume[here, :] = pick_rows(vol[...], block)
+        cell = block * LANES + lax.broadcasted_iota(jnp.int32, (HALF, LANES), 1)
+        live[here, :] = (cell < count[0]).astype(jnp.float32)
+    for k in range(NBR):
+        for block in range(BLOCKS):
+            one = cols[k : k + 1, block * LANES : (block + 1) * LANES]
+            wide[k, 2 * block : 2 * block + 2, :] = jnp.broadcast_to(one, (2, LANES))
+    near_sum(table, wide, jac, grad, rest)
+
+
+def near_second(table, wide, jac, grad, rest):
+    near_sum(table, wide, jac, grad, rest)
 
 
 def timewise(every, me, var, half):
@@ -127,78 +172,13 @@
     return same + pick_rows(cross, row ^ 1)
 
 
-def inner(table, every, wide, jac, picked, grad, volume, rest, loads):
+def finish_kernel(last, *refs):
+    every, rest, came, above, below, wide, jac, dinv, volume, live = refs[:10]
+    if last:
+        out, halos = refs[10:]
+    else:
+        rows, swap, own, copies, table, halos = refs[10:]
     me = lax.axis_index("inst")
-    for half in range(2):
-        here = slice(half * HALF, (half + 1) * HALF)
-        for k in range(NEAR):
-            lane, masks = split(wide[k, here, :], BLOCKS)
-            for var in range(NV):
-                picked[k, var, here, :] = pick(table, var, lane, masks)
-        for var in range(NV):
-            rest[var, here, :] = timewise(every, me, var, half)
-    for load in loads:
-        load.wait()
-    for half in range(2):
-        here = slice(half * HALF, (half + 1) * HALF)
-        total = [None] * NV
-        for k in range(NEAR):
-            for var in range(NV):
-                got = picked[k, var, here, :]
-                for i in range(NV):
-                    term = jac[k, i, var, here, :] * got
-                    total[i] = term if total[i] is None else total[i] + term
-        for i in range(NV):
-            rest[i, here, :] = grad[i, here, :] - total[i] - volume(half) * rest[i, here, :]
-
-
-def inner_first(
-    table, every, cols_hbm, jac_hbm, dinv_hbm, grad_hbm, vol_hbm, count,
-    rest, wide, jac, dinv, grad, volume, live,
-    picked, cols, vol, sems,
-):
-    pairs = (
-        (cols_hbm, cols),
-        (jac_hbm, jac),
-        (vol_hbm, vol),
-        (dinv_hbm, dinv),
-        (grad_hbm, grad),
-    )
-    loads = [pltpu.make_async_copy(a, b, sems.at[n]) for n, (a, b) in enumerate(pairs)]
-    for load in loads:
-        load.start()
-    row = row_iota()
-    for half in range(2):
-        cell = (lax.shift_right_logical(row, 1) + 4 * half) * LANES
-        cell = cell + lax.broadcasted_iota(jnp.int32, (HALF, LANES), 1)
-        live[half * HALF : (half + 1) * HALF, :] = (cell < count[0]).astype(jnp.float32)
-    loads[0].wait()
-    for k in range(NBR):
-        for block in range(BLOCKS):
-            one = cols[k : k + 1, block * LANES : (block + 1) * LANES]
-            wide[k, 2 * block : 2 * block + 2, :] = jnp.broadcast_to(one, (2, LANES))
-
-    def spread(half):
-        value = pick_rows(vol[...], lax.shift_right_logical(row, 1) + 4 * half)
-        volume[half * HALF : (half + 1) * HALF, :] = value
-        return value
-
-    inner(table, every, wide, jac, picked, grad, spread, rest, loads[1:])
-
-
-def inner_second(table, every, wide, jac, grad, volume, rest, picked):
-    def here(half):
-        return volume[half * HALF : (half + 1) * HALF, :]
-
-    inner(table, every, wide, jac, picked, grad, here, rest, ())
-
-
-def finish_kernel(last, *refs):
-    rest, came, above, below, wide, jac, dinv, live = refs[:8]
-    if last:
-        out, halos = refs[8:]
-    else:
-        rows, swap, own, copies, table, halos = refs[8:]
     first = (lax.axis_index("dom") & 1) == 0
     for var in range(NV):
         halos[0, var] = jnp.where(first, above[1, var], came[0, var])
@@ -207,7 +187,9 @@
         halos[3, var] = below[0, var]
     for half in range(2):
         here = slice(half * HALF, (half + 1) * HALF)
-        left = [rest[i, here, :] for i in range(NV)]
+        left = [
+            rest[i, here, :] - volume[here, :] * timewise(every, me, i, half) for i in range(NV)
+        ]
         for k in range(NEAR, NBR):
             lane, masks = split(wide[k, here, :] - BLOCKS * LANES, SLOTS)
             for var in range(NV):
@@ -256,7 +238,8 @@
 JAC = f32(NBR, NV, NV, ROWS, LANES)
 DINV = f32(NV, NV, ROWS, LANES)
 CELL = f32(ROWS, LANES)
-PICKED = pltpu.VMEM((NEAR, NV, ROWS, LANES), jnp.float32)
+COLS = i32(NBR, BLOCKS * LANES)
+VOL = f32(BLOCKS, LANES)
 HALOS = pltpu.VMEM((SLOTS, NV, HALF, LANES), jnp.float32)
 
 
@@ -290,68 +273,55 @@
 
 
 def on_device(adjoint, gradient, jac_blocks, diag_inverse, volume, columns, send_rows, counts):
-    swap, own, copies, table, rows = call(
+    swap, own, copies, table, rows, cols, jac, dinv, grad, vol = call(
         prep_kernel,
         "prep",
-        (dense(adjoint), send_rows),
-        (PAIR, PAIR, COPIES, TABLE, ROW_INDEX),
+        (
+            dense(adjoint),
+            send_rows,
+            columns,
+            dense(jac_blocks),
+            dense(diag_inverse),
+            dense(gradient),
+            volume.reshape(BLOCKS, LANES),
+        ),
+        (PAIR, PAIR, COPIES, TABLE, ROW_INDEX, COLS, JAC, DINV, CURRENT, VOL),
         [
             pltpu.VMEM(CURRENT.shape, jnp.float32),
             pltpu.VMEM((SLOTS, LANES), jnp.int32),
-            pltpu.SemaphoreType.DMA((2,)),
+            pltpu.SemaphoreType.DMA((7,)),
         ],
-        hbm=(0, 1),
+        hbm=range(7),
     )
     came = swapped(swap)
     every = lax.all_to_all(copies, "inst", 0, 0)
-    plus, minus = call(join_kernel, "join_first", (own, came), (PAIR, PAIR))
+    rest, wide, vol, live = call(
+        near_first,
+        "near_first",
+        (table, cols, jac, grad, vol, counts),
+        (CURRENT, WIDE, CELL, CELL),
+        smem=(5,),
+        cost=COST,
+    )
+    plus, minus = call(join_kernel, "join_first", (own, came, rest), (PAIR, PAIR))
     above, below = shifted(plus, 2), shifted(minus, -2)
-    raw = (
-        columns,
-        dense(jac_blocks),
-        dense(diag_inverse),
-        dense(gradient),
-        volume.reshape(BLOCKS, LANES),
-        counts,
-    )
-    rest, wide, jac, dinv, grad, vol, live = call(
-        inner_first,
-        "inner_first",
-        (table, every) + raw,
-        (CURRENT, WIDE, JAC, DINV, CURRENT, CELL, CELL),
-        [
-            PICKED,
-            pltpu.VMEM((NBR, BLOCKS * LANES), jnp.int32),
-            pltpu.VMEM((BLOCKS, LANES), jnp.float32),
-            pltpu.SemaphoreType.DMA((5,)),
-        ],
-        hbm=range(2, 7),
-        smem=(7,),
-        cost=COST,
-    )
+    kept = (wide, jac, dinv, vol, live)
     swap, own, copies, table = call(
         functools.partial(finish_kernel, False),
         "finish_first",
-        (rest, came, above, below, wide, jac, dinv, live, rows),
+        (every, rest, came, above, below) + kept + (rows,),
         (PAIR, PAIR, COPIES, TABLE),
         [HALOS],
     )
     came = swapped(swap)
     every = lax.all_to_all(copies, "inst", 0, 0)
-    plus, minus = call(join_kernel, "join_second", (own, came), (PAIR, PAIR))
+    rest = call(near_second, "near_second", (table, wide, jac, grad), CURRENT, cost=COST)
+    plus, minus = call(join_kernel, "join_second", (own, came, rest), (PAIR, PAIR))
     above, below = shifted(plus, 2), shifted(minus, -2)
-    rest = call(
-        inner_second,
-        "inner_second",
-        (table, every, wide, jac, grad, vol),
-        CURRENT,
-        [PICKED],
-        cost=COST,
-    )
     out = call(
         functools.partial(finish_kernel, True),
         "finish_second",
-        (rest, came, above, below, wide, jac, dinv, live),
+        (every, rest, came, above, below) + kept,
         CURRENT,
         [HALOS],
     )

time: 57.5 us -> 58 us (level)
  starting transfers between devices: 48.6 us -> 49.4 us
    ppermute x4, waiting for transfers between devices: 0.61 us -> 2.14 us  [shifted(): return lax.ppermute(value, 'dom', pairs)]
    ppermute x2, waiting for transfers between devices: 1.7 us -> 0.4 us  [swapped(): lax.ppermute(value, 'dom', [(source, source ^ 1) for source in range(coun...]
  transfers between devices with their start and end apart: 8 -> 8, of which waited for: 3 -> 3; matrix products, arithmetic and copies ran while one was open for 0% -> 0% of each run, Pallas kernels for 3% -> 2%
where the time goes in v5:
time: 58 us; the launch traced here: 57.5 us
  starting transfers between devices  49.4 us (85%)
  Pallas kernels  4.8 us (8%)
  waiting for transfers between devices  2.55 us (4%)
  between operations  0.75 us (1%)
    all_to_all x2, starting transfers between devices, on_device(): every = lax.all_to_all(copies, 'inst', 0, 0)  24.2 us
    ppermute x4, starting transfers between devices, shifted(): return lax.ppermute(value, 'dom', pairs)  19.3 us
    ppermute x2, starting transfers between devices, swapped(): lax.ppermute(value, 'dom', [(source, source ^ 1) for source in range(coun...  5.94 us
    pallas_call x7, Pallas kernels, call(): pl.pallas_call(kernel, out_shape=outs, in_specs=specs, out_specs=jax.tree...  4.8 us
    ppermute x4, waiting for transfers between devices, shifted(): return lax.ppermute(value, 'dom', pairs)  2.14 us
  transfers between devices with their start and end apart: 8, of which 3 were waited for; matrix products, arithmetic and copies ran while one was open for 0% of the time, Pallas kernels for 2%

profile of v5, /device:TPU:1, one launch (start us, length us, event | category | flops | bytes accessed | tf_op | source)
XLA Modules:
  0.0 57.5 jit_solution(6719456649842322087)
XLA Ops:
  0.0 2.2 %prep.1 = (f32[2,5,8,128]{3,2,1,0:T(8,128)S(1)}, f32[2,5,8,128]{3,2,1,0:T(8,128)S(1)}, f32[8,80,128]{2,1,0:T(8,128)}, f32[5,8,8,128]{3,2,1,0:T(8,128)S(1)}, s32[...) custom-call(f32[5,16,128]{2,1,0:T(8,128)} %bitcast.28, ...), custom_call_target="tpu_custom_call" | custom-call | tf_op jit(solution)/shard_map/prep/pallas_call | solution.py:252
  2.2 17.2 %all-to-all-start = ((f32[8,80,128]{2,1,0:T(8,128)}), f32[8,80,128]{2,1,0:T(8,128)S(1)}, u32[]{:S(2)}, u32[]{:S(2)}) async-start(f32[8,80,128]{2,1,0:T(8,128)} %get-tuple-element.27), calls=%async_computation | async-start | bytes 655360 | tf_op jit(solution)/shard_map/all_to_all | solution.py:297
  19.4 2.9 %collective-permute-start = (f32[2,5,8,128]{3,2,1,0:T(8,128)S(1)}, f32[2,5,8,128]{3,2,1,0:T(8,128)S(1)}, u32[]{:S(2)}, u32[]{:S(2)}) collective-permute-start(f32[2,5,8,128]{3,2,1,0:T(8,128)S(1)} %get-tuple-element.34), channel_id=1, source_target_pairs={{0,8},{8,0},{16,24},{24,16},{32,40},{40,32},{48,56},{56,48},{64,72... | collective-permute-start | bytes 122888 | tf_op jit(solution)/shard_map/ppermute | solution.py:266
  22.9 0.5 near_first.1
  23.4 0.0 collective-permute-done.came.refs_2_
  23.4 3.3 %collective-permute-start.1 = (f32[2,5,8,128]{3,2,1,0:T(8,128)S(1)}, f32[2,5,8,128]{3,2,1,0:T(8,128)S(1)}, u32[]{:S(2)}, u32[]{:S(2)}) collective-permute-start(f32[2,5,8,128]{3,2,1,0:T(8,128)S(1)} %get-tuple-element.36), channel_id=1, source_target_pairs={{0,16},{8,24},{16,32},{24,40},{32,48},{40,56},{48,64},{56,72},{64,... | collective-permute-start | bytes 122888 | tf_op jit(solution)/shard_map/ppermute | solution.py:272
  26.7 6.8 %collective-permute-start.2 = (f32[2,5,8,128]{3,2,1,0:T(8,128)S(1)}, f32[2,5,8,128]{3,2,1,0:T(8,128)S(1)}, u32[]{:S(2)}, u32[]{:S(2)}) collective-permute-start(f32[2,5,8,128]{3,2,1,0:T(8,128)S(1)} %get-tuple-element.37), channel_id=1, source_target_pairs={{0,1008},{8,1016},{16,0},{24,8},{32,16},{40,24},{48,32},{56,40},{6... | collective-permute-start | bytes 122888 | tf_op jit(solution)/shard_map/ppermute | solution.py:272
  33.6 0.0 collective-permute-done.1.refs_3_
  33.6 1.1 %collective-permute-done.2.refs_4_ = f32[2,5,8,128]{3,2,1,0:T(8,128)S(1)} collective-permute-done((f32[2,5,8,128]{3,2,1,0:T(8,128)S(1)}, f32[2,5,8,128]{3,2,1,0:T(8,128)S(1)}, u32[]{:S(2)}, u32[]{:S(2)}) %collective-permute-start.2) | collective-permute-done | bytes 40992 | tf_op jit(solution)/shard_map/ppermute | solution.py:272
  34.6 0.0 all-to-all-done.refs_0_
  34.6 0.9 %finish_first.1 = (f32[2,5,8,128]{3,2,1,0:T(8,128)S(1)}, f32[2,5,8,128]{3,2,1,0:T(8,128)S(1)}, f32[8,80,128]{2,1,0:T(8,128)}, f32[5,8,8,128]{3,2,1,0:T(8,128)S(1)}) custom-call(f32[8,80,128]{2,1,0:T(8,128)S(1)} %all-to-all-done.refs_0_, f32[5,16,128]{2,1,0:T(8,128)S(1)} %get-tuple-element.33._.refs_1_, ...), custom_call_target="tpu_custom_call" | custom-call | tf_op jit(solution)/shard_map/finish_first/pallas_call | solution.py:252
  35.6 6.9 %all-to-all-start.1 = ((f32[8,80,128]{2,1,0:T(8,128)}), f32[8,80,128]{2,1,0:T(8,128)S(1)}, u32[]{:S(2)}, u32[]{:S(2)}) async-start(f32[8,80,128]{2,1,0:T(8,128)} %get-tuple-element.43), calls=%async_computation.1 | async-start | bytes 655360 | tf_op jit(solution)/shard_map/all_to_all | solution.py:317
  42.5 3.1 %collective-permute-start.3 = (f32[2,5,8,128]{3,2,1,0:T(8,128)S(1)}, f32[2,5,8,128]{3,2,1,0:T(8,128)S(1)}, u32[]{:S(2)}, u32[]{:S(2)}) collective-permute-start(f32[2,5,8,128]{3,2,1,0:T(8,128)S(1)} %get-tuple-element.45), channel_id=1, source_target_pairs={{0,8},{8,0},{16,24},{24,16},{32,40},{40,32},{48,56},{56,48},{64,72... | collective-permute-start | bytes 122888 | tf_op jit(solution)/shard_map/ppermute | solution.py:266
  45.6 0.4 near_second.1._.refs_1_
  46.0 0.4 collective-permute-done.3.came.refs_2_
  46.4 1.9 %collective-permute-start.4 = (f32[2,5,8,128]{3,2,1,0:T(8,128)S(1)}, f32[2,5,8,128]{3,2,1,0:T(8,128)S(1)}, u32[]{:S(2)}, u32[]{:S(2)}) collective-permute-start(f32[2,5,8,128]{3,2,1,0:T(8,128)S(1)} %get-tuple-element.47), channel_id=1, source_target_pairs={{0,16},{8,24},{16,32},{24,40},{32,48},{40,56},{48,64},{56,72},{64,... | collective-permute-start | bytes 122888 | tf_op jit(solution)/shard_map/ppermute | solution.py:272
  48.4 7.3 %collective-permute-start.5 = (f32[2,5,8,128]{3,2,1,0:T(8,128)S(1)}, f32[2,5,8,128]{3,2,1,0:T(8,128)S(1)}, u32[]{:S(2)}, u32[]{:S(2)}) collective-permute-start(f32[2,5,8,128]{3,2,1,0:T(8,128)S(1)} %get-tuple-element.48), channel_id=1, source_target_pairs={{0,1008},{8,1016},{16,0},{24,8},{32,16},{40,24},{48,32},{56,40},{6... | collective-permute-start | bytes 122888 | tf_op jit(solution)/shard_map/ppermute | solution.py:272
  55.6 0.0 collective-permute-done.4.refs_3_
  55.6 1.1 %collective-permute-done.5.refs_4_ = f32[2,5,8,128]{3,2,1,0:T(8,128)S(1)} collective-permute-done((f32[2,5,8,128]{3,2,1,0:T(8,128)S(1)}, f32[2,5,8,128]{3,2,1,0:T(8,128)S(1)}, u32[]{:S(2)}, u32[]{:S(2)}) %collective-permute-start.5) | collective-permute-done | bytes 40992 | tf_op jit(solution)/shard_map/ppermute | solution.py:272
  56.7 0.0 all-to-all-done.1.refs_0_
  56.7 0.8 %finish_second.1 = f32[5,16,128]{2,1,0:T(8,128)} custom-call(f32[8,80,128]{2,1,0:T(8,128)S(1)} %all-to-all-done.1.refs_0_, f32[5,16,128]{2,1,0:T(8,128)S(1)} %near_second.1._.refs_1_, f32[2,5,8,128]{3,2,1,0:T(8,128)S(1)} %collective-permute-done.3.came.refs_2_, f32[2,5,8,128]{3,2,1,0:T(8,128)S(1)} %collective-permute-done.4.refs_3_, ...), custom_call_target="tpu_custom_call" | custom-call | tf_op jit(solution)/shard_map/finish_second/pallas_call | solution.py:252
  (2 shorter events, 0.0 us)
Async XLA Ops:
  2.2 32.5 %all-to-all-start = ((f32[8,80,128]{2,1,0:T(8,128)}), f32[8,80,128]{2,1,0:T(8,128)S(1)}, u32[]{:S(2)}, u32[]{:S(2)}) async-start(f32[8,80,128]{2,1,0:T(8,128)} %get-tuple-element.27), calls=%async_computation | async-start | bytes 655360 | tf_op jit(solution)/shard_map/all_to_all | solution.py:297
  19.4 4.0 %collective-permute-start = (f32[2,5,8,128]{3,2,1,0:T(8,128)S(1)}, f32[2,5,8,128]{3,2,1,0:T(8,128)S(1)}, u32[]{:S(2)}, u32[]{:S(2)}) collective-permute-start(f32[2,5,8,128]{3,2,1,0:T(8,128)S(1)} %get-tuple-element.34), channel_id=1, source_target_pairs={{0,8},{8,0},{16,24},{24,16},{32,40},{40,32},{48,56},{56,48},{64,72... | collective-permute-start | bytes 122888 | tf_op jit(solution)/shard_map/ppermute | solution.py:266
  23.4 10.1 %collective-permute-start.1 = (f32[2,5,8,128]{3,2,1,0:T(8,128)S(1)}, f32[2,5,8,128]{3,2,1,0:T(8,128)S(1)}, u32[]{:S(2)}, u32[]{:S(2)}) collective-permute-start(f32[2,5,8,128]{3,2,1,0:T(8,128)S(1)} %get-tuple-element.36), channel_id=1, source_target_pairs={{0,16},{8,24},{16,32},{24,40},{32,48},{40,56},{48,64},{56,72},{64,... | collective-permute-start | bytes 122888 | tf_op jit(solution)/shard_map/ppermute | solution.py:272
  26.7 7.9 %collective-permute-start.2 = (f32[2,5,8,128]{3,2,1,0:T(8,128)S(1)}, f32[2,5,8,128]{3,2,1,0:T(8,128)S(1)}, u32[]{:S(2)}, u32[]{:S(2)}) collective-permute-start(f32[2,5,8,128]{3,2,1,0:T(8,128)S(1)} %get-tuple-element.37), channel_id=1, source_target_pairs={{0,1008},{8,1016},{16,0},{24,8},{32,16},{40,24},{48,32},{56,40},{6... | collective-permute-start | bytes 122888 | tf_op jit(solution)/shard_map/ppermute | solution.py:272
  35.6 21.2 %all-to-all-start.1 = ((f32[8,80,128]{2,1,0:T(8,128)}), f32[8,80,128]{2,1,0:T(8,128)S(1)}, u32[]{:S(2)}, u32[]{:S(2)}) async-start(f32[8,80,128]{2,1,0:T(8,128)} %get-tuple-element.43), calls=%async_computation.1 | async-start | bytes 655360 | tf_op jit(solution)/shard_map/all_to_all | solution.py:317
  42.5 3.9 %collective-permute-start.3 = (f32[2,5,8,128]{3,2,1,0:T(8,128)S(1)}, f32[2,5,8,128]{3,2,1,0:T(8,128)S(1)}, u32[]{:S(2)}, u32[]{:S(2)}) collective-permute-start(f32[2,5,8,128]{3,2,1,0:T(8,128)S(1)} %get-tuple-element.45), channel_id=1, source_target_pairs={{0,8},{8,0},{16,24},{24,16},{32,40},{40,32},{48,56},{56,48},{64,72... | collective-permute-start | bytes 122888 | tf_op jit(solution)/shard_map/ppermute | solution.py:266
  46.4 9.2 %collective-permute-start.4 = (f32[2,5,8,128]{3,2,1,0:T(8,128)S(1)}, f32[2,5,8,128]{3,2,1,0:T(8,128)S(1)}, u32[]{:S(2)}, u32[]{:S(2)}) collective-permute-start(f32[2,5,8,128]{3,2,1,0:T(8,128)S(1)} %get-tuple-element.47), channel_id=1, source_target_pairs={{0,16},{8,24},{16,32},{24,40},{32,48},{40,56},{48,64},{56,72},{64,... | collective-permute-start | bytes 122888 | tf_op jit(solution)/shard_map/ppermute | solution.py:272
  48.4 8.4 %collective-permute-start.5 = (f32[2,5,8,128]{3,2,1,0:T(8,128)S(1)}, f32[2,5,8,128]{3,2,1,0:T(8,128)S(1)}, u32[]{:S(2)}, u32[]{:S(2)}) collective-permute-start(f32[2,5,8,128]{3,2,1,0:T(8,128)S(1)} %get-tuple-element.48), channel_id=1, source_target_pairs={{0,1008},{8,1016},{16,0},{24,8},{32,16},{40,24},{48,32},{56,40},{6... | collective-permute-start | bytes 122888 | tf_op jit(solution)/shard_map/ppermute | solution.py:272

commit v6 on v5

--- a/solution.py
+++ b/solution.py
@@ -84,16 +84,15 @@
 
 
 def prep_kernel(
-    adj_hbm, sends_hbm, cols_hbm, jac_hbm, dinv_hbm, grad_hbm, vol_hbm,
-    swap, own, copies, table, rows, cols, jac, dinv, grad, vol,
+    adj_hbm, sends_hbm, cols_hbm, jac_hbm, grad_hbm, vol_hbm,
+    swap, own, copies, table, rows, cols, jac, grad, vol,
     adj, sends, sems,
 ):
     pairs = (
         (adj_hbm, adj),
         (sends_hbm, sends),
         (cols_hbm, cols),
-        (jac_hbm, jac),
-        (dinv_hbm, dinv),
+        (jac_hbm.at[0:2], jac),
         (grad_hbm, grad),
         (vol_hbm, vol),
     )
@@ -124,12 +123,12 @@
         minus[1, var] = came[1, var]
 
 
-def near_sum(table, wide, jac, grad, rest):
+def near_sum(table, wide, jac, start, before, rest):
     for half in range(2):
         here = slice(half * HALF, (half + 1) * HALF)
-        left = [grad[i, here, :] for i in range(NV)]
-        for k in range(NEAR):
-            lane, masks = split(wide[k, here, :], BLOCKS)
+        left = [before[i, here, :] for i in range(NV)]
+        for k in range(2):
+            lane, masks = split(wide[start + k, here, :], BLOCKS)
             for var in range(NV):
                 got = pick(table, var, lane, masks)
                 for i in range(NV):
@@ -138,7 +137,11 @@
             rest[i, here, :] = left[i]
 
 
-def near_first(table, cols, jac, grad, vol, count, rest, wide, volume, live):
+def near_first(
+    table, cols, jac, jac_hbm, grad, vol, count, rest, wide, jac_two, volume, live, sem
+):
+    load = pltpu.make_async_copy(jac_hbm.at[2:4], jac_two, sem.at[0])
+    load.start()
     row = row_iota()
     for half in range(2):
         here = slice(half * HALF, (half + 1) * HALF)
@@ -150,11 +153,25 @@
         for block in range(BLOCKS):
             one = cols[k : k + 1, block * LANES : (block + 1) * LANES]
             wide[k, 2 * block : 2 * block + 2, :] = jnp.broadcast_to(one, (2, LANES))
-    near_sum(table, wide, jac, grad, rest)
-
-
-def near_second(table, wide, jac, grad, rest):
-    near_sum(table, wide, jac, grad, rest)
+    near_sum(table, wide, jac, 0, grad, rest)
+    load.wait()
+    near_sum(table, wide, jac_two, 2, rest, rest)
+
+
+def near_second(table, wide, jac, jac_two, grad, rest):
+    near_sum(table, wide, jac, 0, grad, rest)
+    near_sum(table, wide, jac_two, 2, rest, rest)
+
+
+def load_kernel(_, jac_hbm, dinv_hbm, jac, dinv, sems):
+    loads = [
+        pltpu.make_async_copy(jac_hbm.at[4:6], jac, sems.at[0]),
+        pltpu.make_async_copy(dinv_hbm, dinv, sems.at[1]),
+    ]
+    for load in loads:
+        load.start()
+    for load in loads:
+        load.wait()
 
 
 def timewise(every, me, var, half):
@@ -197,7 +214,7 @@
                 for slot in range(1, SLOTS):
                     got = jnp.where(masks[slot], pick_lanes(halos[slot, var], lane), got)
                 for i in range(NV):
-                    left[i] = left[i] - jac[k, i, var, here, :] * got
+                    left[i] = left[i] - jac[k - NEAR, i, var, here, :] * got
         for i in range(NV):
             total = dinv[i, 0, here, :] * left[0]
             for var in range(1, NV):
@@ -235,7 +252,7 @@
 COPIES = f32(8, NV * ROWS, LANES)
 WIDE = i32(NBR, ROWS, LANES)
 ROW_INDEX = i32(HALF, LANES)
-JAC = f32(NBR, NV, NV, ROWS, LANES)
+JAC = f32(2, NV, NV, ROWS, LANES)
 DINV = f32(NV, NV, ROWS, LANES)
 CELL = f32(ROWS, LANES)
 COLS = i32(NBR, BLOCKS * LANES)
@@ -273,39 +290,50 @@
 
 
 def on_device(adjoint, gradient, jac_blocks, diag_inverse, volume, columns, send_rows, counts):
-    swap, own, copies, table, rows, cols, jac, dinv, grad, vol = call(
+    jac_hbm = dense(jac_blocks)
+    swap, own, copies, table, rows, cols, jac, grad, vol = call(
         prep_kernel,
         "prep",
         (
             dense(adjoint),
             send_rows,
             columns,
-            dense(jac_blocks),
-            dense(diag_inverse),
+            jac_hbm,
             dense(gradient),
             volume.reshape(BLOCKS, LANES),
         ),
-        (PAIR, PAIR, COPIES, TABLE, ROW_INDEX, COLS, JAC, DINV, CURRENT, VOL),
+        (PAIR, PAIR, COPIES, TABLE, ROW_INDEX, COLS, JAC, CURRENT, VOL),
         [
             pltpu.VMEM(CURRENT.shape, jnp.float32),
             pltpu.VMEM((SLOTS, LANES), jnp.int32),
-            pltpu.SemaphoreType.DMA((7,)),
+            pltpu.SemaphoreType.DMA((6,)),
         ],
-        hbm=range(7),
+        hbm=range(6),
     )
     came = swapped(swap)
     every = lax.all_to_all(copies, "inst", 0, 0)
-    rest, wide, vol, live = call(
+    rest, wide, jac_two, vol, live = call(
         near_first,
         "near_first",
-        (table, cols, jac, grad, vol, counts),
-        (CURRENT, WIDE, CELL, CELL),
-        smem=(5,),
+        (table, cols, jac, jac_hbm, grad, vol, counts),
+        (CURRENT, WIDE, JAC, CELL, CELL),
+        [pltpu.SemaphoreType.DMA((1,))],
+        hbm=(3,),
+        smem=(6,),
         cost=COST,
     )
     plus, minus = call(join_kernel, "join_first", (own, came, rest), (PAIR, PAIR))
     above, below = shifted(plus, 2), shifted(minus, -2)
-    kept = (wide, jac, dinv, vol, live)
+    far, dinv = call(
+        load_kernel,
+        "load_rest",
+        (plus, jac_hbm, dense(diag_inverse)),
+        (JAC, DINV),
+        [pltpu.SemaphoreType.DMA((2,))],
+        hbm=(1, 2),
+        cost=COST,
+    )
+    kept = (wide, far, dinv, vol, live)
     swap, own, copies, table = call(
         functools.partial(finish_kernel, False),
         "finish_first",
@@ -315,7 +343,7 @@
     )
     came = swapped(swap)
     every = lax.all_to_all(copies, "inst", 0, 0)
-    rest = call(near_second, "near_second", (table, wide, jac, grad), CURRENT, cost=COST)
+    rest = call(near_second, "near_second", (table, wide, jac, jac_two, grad), CURRENT, cost=COST)
     plus, minus = call(join_kernel, "join_second", (own, came, rest), (PAIR, PAIR))
     above, below = shifted(plus, 2), shifted(minus, -2)
     out = call(

time: 58 us -> 63.6 us (1.097)
  waiting for transfers between devices: 2.55 us -> 6.51 us
  Pallas kernels: 4.8 us -> 6.39 us
    ppermute x4, waiting for transfers between devices: 2.14 us -> 6.12 us  [shifted(): return lax.ppermute(value, 'dom', pairs)]
    pallas_call x7 -> x8, Pallas kernels: 4.8 us -> 6.39 us  [call(): pl.pallas_call(kernel, out_shape=outs, in_specs=specs, out_specs=jax.tree...]
  transfers between devices with their start and end apart: 8 -> 8, of which waited for: 3 -> 3; matrix products, arithmetic and copies ran while one was open for 0% -> 0% of each run, Pallas kernels for 2% -> 5%
where the time goes in v6:
time: 63.6 us; the launch traced here: 63 us
  starting transfers between devices  49.4 us (78%)
  waiting for transfers between devices  6.51 us (10%)
  Pallas kernels  6.39 us (10%)
  between operations  0.76 us (1%)
    all_to_all x2, starting transfers between devices, on_device(): every = lax.all_to_all(copies, 'inst', 0, 0)  24.2 us
    ppermute x4, starting transfers between devices, shifted(): return lax.ppermute(value, 'dom', pairs)  18.7 us
    ppermute x2, starting transfers between devices, swapped(): lax.ppermute(value, 'dom', [(source, source ^ 1) for source in range(coun...  6.47 us
    pallas_call x8, Pallas kernels, call(): pl.pallas_call(kernel, out_shape=outs, in_specs=specs, out_specs=jax.tree...  6.39 us
    ppermute x4, waiting for transfers between devices, shifted(): return lax.ppermute(value, 'dom', pairs)  6.12 us
  transfers between devices with their start and end apart: 8, of which 3 were waited for; matrix products, arithmetic and copies ran while one was open for 0% of the time, Pallas kernels for 5%

profile of v6, /device:TPU:1, one launch (start us, length us, event | category | flops | bytes accessed | tf_op | source)
XLA Modules:
  0.0 63.0 jit_solution(15833760107414132092)
XLA Ops:
  0.0 1.8 %prep.1 = (f32[2,5,8,128]{3,2,1,0:T(8,128)S(1)}, f32[2,5,8,128]{3,2,1,0:T(8,128)S(1)}, f32[8,80,128]{2,1,0:T(8,128)}, f32[5,8,8,128]{3,2,1,0:T(8,128)S(1)}, s32[...) custom-call(f32[5,16,128]{2,1,0:T(8,128)} %bitcast.30, ...), custom_call_target="tpu_custom_call" | custom-call | tf_op jit(solution)/shard_map/prep/pallas_call | solution.py:269
  1.8 17.2 %all-to-all-start = ((f32[8,80,128]{2,1,0:T(8,128)}), f32[8,80,128]{2,1,0:T(8,128)S(1)}, u32[]{:S(2)}, u32[]{:S(2)}) async-start(f32[8,80,128]{2,1,0:T(8,128)} %get-tuple-element.29), calls=%async_computation | async-start | bytes 655360 | tf_op jit(solution)/shard_map/all_to_all | solution.py:314
  19.1 2.9 %collective-permute-start = (f32[2,5,8,128]{3,2,1,0:T(8,128)S(1)}, f32[2,5,8,128]{3,2,1,0:T(8,128)S(1)}, u32[]{:S(2)}, u32[]{:S(2)}) collective-permute-start(f32[2,5,8,128]{3,2,1,0:T(8,128)S(1)} %get-tuple-element.36), channel_id=1, source_target_pairs={{0,8},{8,0},{16,24},{24,16},{32,40},{40,32},{48,56},{56,48},{64,72... | collective-permute-start | bytes 122888 | tf_op jit(solution)/shard_map/ppermute | solution.py:283
  22.6 1.3 %near_first.1 = (f32[5,16,128]{2,1,0:T(8,128)S(1)}, s32[6,16,128]{2,1,0:T(8,128)S(1)}, f32[2,5,5,16,128]{4,3,2,1,0:T(8,128)S(1)}, f32[16,128]{1,0:T(8,128)S(1)}, f32[16,128]{1,0:T(8,128)S(1)}) custom-call(f32[5,8,8,128]{3,2,1,0:T(8,128)S(1)} %get-tuple-element.30.table, s32[6,1024]{1,0:T(8,128)S(1)} %get-tuple-element.31.cols, ...), custom_call_target="tpu_custom_call" | custom-call | flops 1000000 | bytes 4000000 | tf_op jit(solution)/shard_map/near_first/pallas_call | solution.py:269
  23.9 0.0 collective-permute-done.came.refs_2_
  23.9 8.2 %collective-permute-start.2 = (f32[2,5,8,128]{3,2,1,0:T(8,128)S(1)}, f32[2,5,8,128]{3,2,1,0:T(8,128)S(1)}, u32[]{:S(2)}, u32[]{:S(2)}) collective-permute-start(f32[2,5,8,128]{3,2,1,0:T(8,128)S(1)} %get-tuple-element.39), channel_id=1, source_target_pairs={{0,1008},{8,1016},{16,0},{24,8},{32,16},{40,24},{48,32},{56,40},{6... | collective-permute-start | bytes 122888 | tf_op jit(solution)/shard_map/ppermute | solution.py:289
  32.1 1.9 %collective-permute-start.1 = (f32[2,5,8,128]{3,2,1,0:T(8,128)S(1)}, f32[2,5,8,128]{3,2,1,0:T(8,128)S(1)}, u32[]{:S(2)}, u32[]{:S(2)}) collective-permute-start(f32[2,5,8,128]{3,2,1,0:T(8,128)S(1)} %get-tuple-element.38._), channel_id=1, source_target_pairs={{0,16},{8,24},{16,32},{24,40},{32,48},{40,56},{48,64},{56,72},{64,... | collective-permute-start | bytes 122888 | tf_op jit(solution)/shard_map/ppermute | solution.py:289
  34.1 1.1 %load_rest.1 = (f32[2,5,5,16,128]{4,3,2,1,0:T(8,128)S(1)}, f32[5,5,16,128]{3,2,1,0:T(8,128)S(1)}) custom-call(f32[2,5,8,128]{3,2,1,0:T(8,128)S(1)} %get-tuple-element.38._, f32[6,5,5,16,128]{4,3,2,1,0:T(8,128)} %bitcast.28, f32[5,5,16,128]{3,2,1,0:T(8,128)} %bitcast.29), custom_call_target="tpu_custom_call" | custom-call | flops 1000000 | bytes 4000000 | tf_op jit(solution)/shard_map/load_rest/pallas_call | solution.py:269
  35.1 0.0 collective-permute-done.2.refs_4_
  35.2 5.0 %collective-permute-done.1.refs_3_ = f32[2,5,8,128]{3,2,1,0:T(8,128)S(1)} collective-permute-done((f32[2,5,8,128]{3,2,1,0:T(8,128)S(1)}, f32[2,5,8,128]{3,2,1,0:T(8,128)S(1)}, u32[]{:S(2)}, u32[]{:S(2)}) %collective-permute-start.1) | collective-permute-done | bytes 40992 | tf_op jit(solution)/shard_map/ppermute | solution.py:289
  40.2 0.0 all-to-all-done.refs_0_
  40.2 0.9 %finish_first.1 = (f32[2,5,8,128]{3,2,1,0:T(8,128)S(1)}, f32[2,5,8,128]{3,2,1,0:T(8,128)S(1)}, f32[8,80,128]{2,1,0:T(8,128)}, f32[5,8,8,128]{3,2,1,0:T(8,128)S(1)}) custom-call(f32[8,80,128]{2,1,0:T(8,128)S(1)} %all-to-all-done.refs_0_, f32[5,16,128]{2,1,0:T(8,128)S(1)} %get-tuple-element.35._.refs_1_, ...), custom_call_target="tpu_custom_call" | custom-call | tf_op jit(solution)/shard_map/finish_first/pallas_call | solution.py:269
  41.1 6.9 %all-to-all-start.1 = ((f32[8,80,128]{2,1,0:T(8,128)}), f32[8,80,128]{2,1,0:T(8,128)S(1)}, u32[]{:S(2)}, u32[]{:S(2)}) async-start(f32[8,80,128]{2,1,0:T(8,128)} %get-tuple-element.46), calls=%async_computation.1 | async-start | bytes 655360 | tf_op jit(solution)/shard_map/all_to_all | solution.py:345
  48.0 3.6 %collective-permute-start.3 = (f32[2,5,8,128]{3,2,1,0:T(8,128)S(1)}, f32[2,5,8,128]{3,2,1,0:T(8,128)S(1)}, u32[]{:S(2)}, u32[]{:S(2)}) collective-permute-start(f32[2,5,8,128]{3,2,1,0:T(8,128)S(1)} %get-tuple-element.49), channel_id=1, source_target_pairs={{0,8},{8,0},{16,24},{24,16},{32,40},{40,32},{48,56},{56,48},{64,72... | collective-permute-start | bytes 122888 | tf_op jit(solution)/shard_map/ppermute | solution.py:283
  51.7 0.5 near_second.1._.refs_1_
  52.1 0.4 collective-permute-done.3.came.refs_2_
  52.5 1.9 %collective-permute-start.4 = (f32[2,5,8,128]{3,2,1,0:T(8,128)S(1)}, f32[2,5,8,128]{3,2,1,0:T(8,128)S(1)}, u32[]{:S(2)}, u32[]{:S(2)}) collective-permute-start(f32[2,5,8,128]{3,2,1,0:T(8,128)S(1)} %get-tuple-element.51), channel_id=1, source_target_pairs={{0,16},{8,24},{16,32},{24,40},{32,48},{40,56},{48,64},{56,72},{64,... | collective-permute-start | bytes 122888 | tf_op jit(solution)/shard_map/ppermute | solution.py:289
  54.4 6.7 %collective-permute-start.5 = (f32[2,5,8,128]{3,2,1,0:T(8,128)S(1)}, f32[2,5,8,128]{3,2,1,0:T(8,128)S(1)}, u32[]{:S(2)}, u32[]{:S(2)}) collective-permute-start(f32[2,5,8,128]{3,2,1,0:T(8,128)S(1)} %get-tuple-element.52), channel_id=1, source_target_pairs={{0,1008},{8,1016},{16,0},{24,8},{32,16},{40,24},{48,32},{56,40},{6... | collective-permute-start | bytes 122888 | tf_op jit(solution)/shard_map/ppermute | solution.py:289
  61.1 0.0 collective-permute-done.4.refs_3_
  61.1 1.1 %collective-permute-done.5.refs_4_ = f32[2,5,8,128]{3,2,1,0:T(8,128)S(1)} collective-permute-done((f32[2,5,8,128]{3,2,1,0:T(8,128)S(1)}, f32[2,5,8,128]{3,2,1,0:T(8,128)S(1)}, u32[]{:S(2)}, u32[]{:S(2)}) %collective-permute-start.5) | collective-permute-done | bytes 40992 | tf_op jit(solution)/shard_map/ppermute | solution.py:289
  62.2 0.0 all-to-all-done.1.refs_0_
  62.2 0.8 %finish_second.1 = f32[5,16,128]{2,1,0:T(8,128)} custom-call(f32[8,80,128]{2,1,0:T(8,128)S(1)} %all-to-all-done.1.refs_0_, f32[5,16,128]{2,1,0:T(8,128)S(1)} %near_second.1._.refs_1_, f32[2,5,8,128]{3,2,1,0:T(8,128)S(1)} %collective-permute-done.3.came.refs_2_, f32[2,5,8,128]{3,2,1,0:T(8,128)S(1)} %collective-permute-done.4.refs_3_, ...), custom_call_target="tpu_custom_call" | custom-call | tf_op jit(solution)/shard_map/finish_second/pallas_call | solution.py:269
  (2 shorter events, 0.0 us)
Async XLA Ops:
  1.8 38.4 %all-to-all-start = ((f32[8,80,128]{2,1,0:T(8,128)}), f32[8,80,128]{2,1,0:T(8,128)S(1)}, u32[]{:S(2)}, u32[]{:S(2)}) async-start(f32[8,80,128]{2,1,0:T(8,128)} %get-tuple-element.29), calls=%async_computation | async-start | bytes 655360 | tf_op jit(solution)/shard_map/all_to_all | solution.py:314
  19.1 4.8 %collective-permute-start = (f32[2,5,8,128]{3,2,1,0:T(8,128)S(1)}, f32[2,5,8,128]{3,2,1,0:T(8,128)S(1)}, u32[]{:S(2)}, u32[]{:S(2)}) collective-permute-start(f32[2,5,8,128]{3,2,1,0:T(8,128)S(1)} %get-tuple-element.36), channel_id=1, source_target_pairs={{0,8},{8,0},{16,24},{24,16},{32,40},{40,32},{48,56},{56,48},{64,72... | collective-permute-start | bytes 122888 | tf_op jit(solution)/shard_map/ppermute | solution.py:283
  23.9 11.2 %collective-permute-start.2 = (f32[2,5,8,128]{3,2,1,0:T(8,128)S(1)}, f32[2,5,8,128]{3,2,1,0:T(8,128)S(1)}, u32[]{:S(2)}, u32[]{:S(2)}) collective-permute-start(f32[2,5,8,128]{3,2,1,0:T(8,128)S(1)} %get-tuple-element.39), channel_id=1, source_target_pairs={{0,1008},{8,1016},{16,0},{24,8},{32,16},{40,24},{48,32},{56,40},{6... | collective-permute-start | bytes 122888 | tf_op jit(solution)/shard_map/ppermute | solution.py:289
  32.1 8.1 %collective-permute-start.1 = (f32[2,5,8,128]{3,2,1,0:T(8,128)S(1)}, f32[2,5,8,128]{3,2,1,0:T(8,128)S(1)}, u32[]{:S(2)}, u32[]{:S(2)}) collective-permute-start(f32[2,5,8,128]{3,2,1,0:T(8,128)S(1)} %get-tuple-element.38._), channel_id=1, source_target_pairs={{0,16},{8,24},{16,32},{24,40},{32,48},{40,56},{48,64},{56,72},{64,... | collective-permute-start | bytes 122888 | tf_op jit(solution)/shard_map/ppermute | solution.py:289
  41.1 21.1 %all-to-all-start.1 = ((f32[8,80,128]{2,1,0:T(8,128)}), f32[8,80,128]{2,1,0:T(8,128)S(1)}, u32[]{:S(2)}, u32[]{:S(2)}) async-start(f32[8,80,128]{2,1,0:T(8,128)} %get-tuple-element.46), calls=%async_computation.1 | async-start | bytes 655360 | tf_op jit(solution)/shard_map/all_to_all | solution.py:345
  48.0 4.5 %collective-permute-start.3 = (f32[2,5,8,128]{3,2,1,0:T(8,128)S(1)}, f32[2,5,8,128]{3,2,1,0:T(8,128)S(1)}, u32[]{:S(2)}, u32[]{:S(2)}) collective-permute-start(f32[2,5,8,128]{3,2,1,0:T(8,128)S(1)} %get-tuple-element.49), channel_id=1, source_target_pairs={{0,8},{8,0},{16,24},{24,16},{32,40},{40,32},{48,56},{56,48},{64,72... | collective-permute-start | bytes 122888 | tf_op jit(solution)/shard_map/ppermute | solution.py:283
  52.5 8.6 %collective-permute-start.4 = (f32[2,5,8,128]{3,2,1,0:T(8,128)S(1)}, f32[2,5,8,128]{3,2,1,0:T(8,128)S(1)}, u32[]{:S(2)}, u32[]{:S(2)}) collective-permute-start(f32[2,5,8,128]{3,2,1,0:T(8,128)S(1)} %get-tuple-element.51), channel_id=1, source_target_pairs={{0,16},{8,24},{16,32},{24,40},{32,48},{40,56},{48,64},{56,72},{64,... | collective-permute-start | bytes 122888 | tf_op jit(solution)/shard_map/ppermute | solution.py:289
  54.4 7.8 %collective-permute-start.5 = (f32[2,5,8,128]{3,2,1,0:T(8,128)S(1)}, f32[2,5,8,128]{3,2,1,0:T(8,128)S(1)}, u32[]{:S(2)}, u32[]{:S(2)}) collective-permute-start(f32[2,5,8,128]{3,2,1,0:T(8,128)S(1)} %get-tuple-element.52), channel_id=1, source_target_pairs={{0,1008},{8,1016},{16,0},{24,8},{32,16},{40,24},{48,32},{56,40},{6... | collective-permute-start | bytes 122888 | tf_op jit(solution)/shard_map/ppermute | solution.py:289

commit v7 on v5

--- a/solution.py
+++ b/solution.py
@@ -116,12 +116,18 @@
         load.wait()
 
 
-def join_kernel(own, came, _, plus, minus):
+def even_chip():
+    return (lax.axis_index("dom") & 2) == 0
+
+
+def join_kernel(own, came, _, over_odd, over_even):
+    even = even_chip()
     for var in range(NV):
-        plus[0, var] = own[0, var]
-        plus[1, var] = came[0, var]
-        minus[0, var] = own[1, var]
-        minus[1, var] = came[1, var]
+        plus = own[0, var], came[0, var]
+        minus = own[1, var], came[1, var]
+        for n in range(2):
+            over_odd[n, var] = jnp.where(even, minus[n], plus[n])
+            over_even[n, var] = jnp.where(even, plus[n], minus[n])
 
 
 def near_sum(table, wide, jac, grad, rest):
@@ -173,18 +179,21 @@
 
 
 def finish_kernel(last, *refs):
-    every, rest, came, above, below, wide, jac, dinv, volume, live = refs[:10]
+    every, rest, came, over_odd, over_even, wide, jac, dinv, volume, live = refs[:10]
     if last:
         out, halos = refs[10:]
     else:
         rows, swap, own, copies, table, halos = refs[10:]
     me = lax.axis_index("inst")
     first = (lax.axis_index("dom") & 1) == 0
+    even = even_chip()
     for var in range(NV):
-        halos[0, var] = jnp.where(first, above[1, var], came[0, var])
-        halos[1, var] = jnp.where(first, came[1, var], below[1, var])
-        halos[2, var] = above[0, var]
-        halos[3, var] = below[0, var]
+        above = [jnp.where(even, over_odd[n, var], over_even[n, var]) for n in range(2)]
+        below = [jnp.where(even, over_even[n, var], over_odd[n, var]) for n in range(2)]
+        halos[0, var] = jnp.where(first, above[1], came[0, var])
+        halos[1, var] = jnp.where(first, came[1, var], below[1])
+        halos[2, var] = above[0]
+        halos[3, var] = below[0]
     for half in range(2):
         here = slice(half * HALF, (half + 1) * HALF)
         left = [
@@ -266,9 +275,12 @@
     return lax.ppermute(value, "dom", [(source, source ^ 1) for source in range(count)])
 
 
-def shifted(value, steps):
+def edge(value, odd):
     count = lax.axis_size("dom")
-    pairs = [(source, (source + steps) % count) for source in range(count)]
+    pairs = []
+    for source in range(count):
+        up = (source // 2) % 2 == odd
+        pairs.append((source, (source + (2 if up else -2)) % count))
     return lax.ppermute(value, "dom", pairs)
 
 
@@ -303,25 +315,25 @@
         smem=(5,),
         cost=COST,
     )
-    plus, minus = call(join_kernel, "join_first", (own, came, rest), (PAIR, PAIR))
-    above, below = shifted(plus, 2), shifted(minus, -2)
+    odd, even = call(join_kernel, "join_first", (own, came, rest), (PAIR, PAIR))
+    odd, even = edge(odd, 1), edge(even, 0)
     kept = (wide, jac, dinv, vol, live)
     swap, own, copies, table = call(
         functools.partial(finish_kernel, False),
         "finish_first",
-        (every, rest, came, above, below) + kept + (rows,),
+        (every, rest, came, odd, even) + kept + (rows,),
         (PAIR, PAIR, COPIES, TABLE),
         [HALOS],
     )
     came = swapped(swap)
     every = lax.all_to_all(copies, "inst", 0, 0)
     rest = call(near_second, "near_second", (table, wide, jac, grad), CURRENT, cost=COST)
-    plus, minus = call(join_kernel, "join_second", (own, came, rest), (PAIR, PAIR))
-    above, below = shifted(plus, 2), shifted(minus, -2)
+    odd, even = call(join_kernel, "join_second", (own, came, rest), (PAIR, PAIR))
+    odd, even = edge(odd, 1), edge(even, 0)
     out = call(
         functools.partial(finish_kernel, True),
         "finish_second",
-        (every, rest, came, above, below) + kept,
+        (every, rest, came, odd, even) + kept,
         CURRENT,
         [HALOS],
     )

time: 58 us -> 58.2 us (level)
  waiting for transfers between devices: 2.55 us -> 6.33 us
  starting transfers between devices: 49.4 us -> 45.8 us
    ppermute x4, starting transfers between devices: 19.3 us -> 15.1 us  [edge(): return lax.ppermute(value, 'dom', pairs)]
    ppermute x4, waiting for transfers between devices: 2.14 us -> 5.92 us  [edge(): return lax.ppermute(value, 'dom', pairs)]
    ppermute x2, starting transfers between devices: 5.94 us -> 6.52 us  [swapped(): lax.ppermute(value, 'dom', [(source, source ^ 1) for source in range(coun...]
where the time goes in v7:
time: 58.2 us; the launch traced here: 57.7 us
  starting transfers between devices  45.8 us (79%)
  waiting for transfers between devices  6.33 us (11%)
  Pallas kernels  4.84 us (8%)
  between operations  0.75 us (1%)
    all_to_all x2, starting transfers between devices, on_device(): every = lax.all_to_all(copies, 'inst', 0, 0)  24.2 us
    ppermute x4, starting transfers between devices, edge(): return lax.ppermute(value, 'dom', pairs)  15.1 us
    ppermute x2, starting transfers between devices, swapped(): lax.ppermute(value, 'dom', [(source, source ^ 1) for source in range(coun...  6.52 us
    ppermute x4, waiting for transfers between devices, edge(): return lax.ppermute(value, 'dom', pairs)  5.92 us
    pallas_call x7, Pallas kernels, call(): pl.pallas_call(kernel, out_shape=outs, in_specs=specs, out_specs=jax.tree...  4.84 us
  transfers between devices with their start and end apart: 8, of which 3 were waited for; matrix products, arithmetic and copies ran while one was open for 0% of the time, Pallas kernels for 2%

profile of v7, /device:TPU:1, one launch (start us, length us, event | category | flops | bytes accessed | tf_op | source)
XLA Modules:
  0.0 57.7 jit_solution(15898911168874307870)
XLA Ops:
  0.0 2.2 %prep.1 = (f32[2,5,8,128]{3,2,1,0:T(8,128)S(1)}, f32[2,5,8,128]{3,2,1,0:T(8,128)S(1)}, f32[8,80,128]{2,1,0:T(8,128)}, f32[5,8,8,128]{3,2,1,0:T(8,128)S(1)}, s32[...) custom-call(f32[5,16,128]{2,1,0:T(8,128)} %bitcast.28, ...), custom_call_target="tpu_custom_call" | custom-call | tf_op jit(solution)/shard_map/prep/pallas_call | solution.py:261
  2.2 17.2 %all-to-all-start = ((f32[8,80,128]{2,1,0:T(8,128)}), f32[8,80,128]{2,1,0:T(8,128)S(1)}, u32[]{:S(2)}, u32[]{:S(2)}) async-start(f32[8,80,128]{2,1,0:T(8,128)} %get-tuple-element.27), calls=%async_computation | async-start | bytes 655360 | tf_op jit(solution)/shard_map/all_to_all | solution.py:309
  19.4 2.9 %collective-permute-start = (f32[2,5,8,128]{3,2,1,0:T(8,128)S(1)}, f32[2,5,8,128]{3,2,1,0:T(8,128)S(1)}, u32[]{:S(2)}, u32[]{:S(2)}) collective-permute-start(f32[2,5,8,128]{3,2,1,0:T(8,128)S(1)} %get-tuple-element.34), channel_id=1, source_target_pairs={{0,8},{8,0},{16,24},{24,16},{32,40},{40,32},{48,56},{56,48},{64,72... | collective-permute-start | bytes 122888 | tf_op jit(solution)/shard_map/ppermute | solution.py:275
  22.9 0.5 near_first.1
  23.4 0.0 collective-permute-done.came.refs_2_
  23.4 8.2 %collective-permute-start.1 = (f32[2,5,8,128]{3,2,1,0:T(8,128)S(1)}, f32[2,5,8,128]{3,2,1,0:T(8,128)S(1)}, u32[]{:S(2)}, u32[]{:S(2)}) collective-permute-start(f32[2,5,8,128]{3,2,1,0:T(8,128)S(1)} %get-tuple-element.36), channel_id=1, source_target_pairs={{0,1008},{8,1016},{16,32},{24,40},{32,16},{40,24},{48,64},{56,72},... | collective-permute-start | bytes 122888 | tf_op jit(solution)/shard_map/ppermute | solution.py:284
  31.6 1.9 %collective-permute-start.2 = (f32[2,5,8,128]{3,2,1,0:T(8,128)S(1)}, f32[2,5,8,128]{3,2,1,0:T(8,128)S(1)}, u32[]{:S(2)}, u32[]{:S(2)}) collective-permute-start(f32[2,5,8,128]{3,2,1,0:T(8,128)S(1)} %get-tuple-element.37), channel_id=1, source_target_pairs={{0,16},{8,24},{16,0},{24,8},{32,48},{40,56},{48,32},{56,40},{64,80... | collective-permute-start | bytes 122888 | tf_op jit(solution)/shard_map/ppermute | solution.py:284
  33.6 0.0 collective-permute-done.1.refs_3_
  33.6 2.8 %collective-permute-done.2.refs_4_ = f32[2,5,8,128]{3,2,1,0:T(8,128)S(1)} collective-permute-done((f32[2,5,8,128]{3,2,1,0:T(8,128)S(1)}, f32[2,5,8,128]{3,2,1,0:T(8,128)S(1)}, u32[]{:S(2)}, u32[]{:S(2)}) %collective-permute-start.2) | collective-permute-done | bytes 40992 | tf_op jit(solution)/shard_map/ppermute | solution.py:284
  36.4 0.0 all-to-all-done.refs_0_
  36.4 0.9 %finish_first.1 = (f32[2,5,8,128]{3,2,1,0:T(8,128)S(1)}, f32[2,5,8,128]{3,2,1,0:T(8,128)S(1)}, f32[8,80,128]{2,1,0:T(8,128)}, f32[5,8,8,128]{3,2,1,0:T(8,128)S(1)}) custom-call(f32[8,80,128]{2,1,0:T(8,128)S(1)} %all-to-all-done.refs_0_, f32[5,16,128]{2,1,0:T(8,128)S(1)} %get-tuple-element.33._.refs_1_, ...), custom_call_target="tpu_custom_call" | custom-call | tf_op jit(solution)/shard_map/finish_first/pallas_call | solution.py:261
  37.3 6.9 %all-to-all-start.1 = ((f32[8,80,128]{2,1,0:T(8,128)}), f32[8,80,128]{2,1,0:T(8,128)S(1)}, u32[]{:S(2)}, u32[]{:S(2)}) async-start(f32[8,80,128]{2,1,0:T(8,128)} %get-tuple-element.43), calls=%async_computation.1 | async-start | bytes 655360 | tf_op jit(solution)/shard_map/all_to_all | solution.py:329
  44.2 3.7 %collective-permute-start.3 = (f32[2,5,8,128]{3,2,1,0:T(8,128)S(1)}, f32[2,5,8,128]{3,2,1,0:T(8,128)S(1)}, u32[]{:S(2)}, u32[]{:S(2)}) collective-permute-start(f32[2,5,8,128]{3,2,1,0:T(8,128)S(1)} %get-tuple-element.45), channel_id=1, source_target_pairs={{0,8},{8,0},{16,24},{24,16},{32,40},{40,32},{48,56},{56,48},{64,72... | collective-permute-start | bytes 122888 | tf_op jit(solution)/shard_map/ppermute | solution.py:275
  47.9 0.4 near_second.1._.refs_1_
  48.4 0.4 collective-permute-done.3.came.refs_2_
  48.8 3.0 %collective-permute-start.4 = (f32[2,5,8,128]{3,2,1,0:T(8,128)S(1)}, f32[2,5,8,128]{3,2,1,0:T(8,128)S(1)}, u32[]{:S(2)}, u32[]{:S(2)}) collective-permute-start(f32[2,5,8,128]{3,2,1,0:T(8,128)S(1)} %get-tuple-element.47), channel_id=1, source_target_pairs={{0,1008},{8,1016},{16,32},{24,40},{32,16},{40,24},{48,64},{56,72},... | collective-permute-start | bytes 122888 | tf_op jit(solution)/shard_map/ppermute | solution.py:284
  51.8 1.9 %collective-permute-start.5 = (f32[2,5,8,128]{3,2,1,0:T(8,128)S(1)}, f32[2,5,8,128]{3,2,1,0:T(8,128)S(1)}, u32[]{:S(2)}, u32[]{:S(2)}) collective-permute-start(f32[2,5,8,128]{3,2,1,0:T(8,128)S(1)} %get-tuple-element.48), channel_id=1, source_target_pairs={{0,16},{8,24},{16,0},{24,8},{32,48},{40,56},{48,32},{56,40},{64,80... | collective-permute-start | bytes 122888 | tf_op jit(solution)/shard_map/ppermute | solution.py:284
  53.8 3.1 %collective-permute-done.4.refs_3_ = f32[2,5,8,128]{3,2,1,0:T(8,128)S(1)} collective-permute-done((f32[2,5,8,128]{3,2,1,0:T(8,128)S(1)}, f32[2,5,8,128]{3,2,1,0:T(8,128)S(1)}, u32[]{:S(2)}, u32[]{:S(2)}) %collective-permute-start.4) | collective-permute-done | bytes 40992 | tf_op jit(solution)/shard_map/ppermute | solution.py:284
  56.9 0.0 collective-permute-done.5.refs_4_
  56.9 0.0 all-to-all-done.1.refs_0_
  56.9 0.8 %finish_second.1 = f32[5,16,128]{2,1,0:T(8,128)} custom-call(f32[8,80,128]{2,1,0:T(8,128)S(1)} %all-to-all-done.1.refs_0_, f32[5,16,128]{2,1,0:T(8,128)S(1)} %near_second.1._.refs_1_, f32[2,5,8,128]{3,2,1,0:T(8,128)S(1)} %collective-permute-done.3.came.refs_2_, f32[2,5,8,128]{3,2,1,0:T(8,128)S(1)} %collective-permute-done.4.refs_3_, ...), custom_call_target="tpu_custom_call" | custom-call | tf_op jit(solution)/shard_map/finish_second/pallas_call | solution.py:261
  (2 shorter events, 0.0 us)
Async XLA Ops:
  2.2 34.2 %all-to-all-start = ((f32[8,80,128]{2,1,0:T(8,128)}), f32[8,80,128]{2,1,0:T(8,128)S(1)}, u32[]{:S(2)}, u32[]{:S(2)}) async-start(f32[8,80,128]{2,1,0:T(8,128)} %get-tuple-element.27), calls=%async_computation | async-start | bytes 655360 | tf_op jit(solution)/shard_map/all_to_all | solution.py:309
  19.4 4.0 %collective-permute-start = (f32[2,5,8,128]{3,2,1,0:T(8,128)S(1)}, f32[2,5,8,128]{3,2,1,0:T(8,128)S(1)}, u32[]{:S(2)}, u32[]{:S(2)}) collective-permute-start(f32[2,5,8,128]{3,2,1,0:T(8,128)S(1)} %get-tuple-element.34), channel_id=1, source_target_pairs={{0,8},{8,0},{16,24},{24,16},{32,40},{40,32},{48,56},{56,48},{64,72... | collective-permute-start | bytes 122888 | tf_op jit(solution)/shard_map/ppermute | solution.py:275
  23.4 10.1 %collective-permute-start.1 = (f32[2,5,8,128]{3,2,1,0:T(8,128)S(1)}, f32[2,5,8,128]{3,2,1,0:T(8,128)S(1)}, u32[]{:S(2)}, u32[]{:S(2)}) collective-permute-start(f32[2,5,8,128]{3,2,1,0:T(8,128)S(1)} %get-tuple-element.36), channel_id=1, source_target_pairs={{0,1008},{8,1016},{16,32},{24,40},{32,16},{40,24},{48,64},{56,72},... | collective-permute-start | bytes 122888 | tf_op jit(solution)/shard_map/ppermute | solution.py:284
  31.6 4.7 %collective-permute-start.2 = (f32[2,5,8,128]{3,2,1,0:T(8,128)S(1)}, f32[2,5,8,128]{3,2,1,0:T(8,128)S(1)}, u32[]{:S(2)}, u32[]{:S(2)}) collective-permute-start(f32[2,5,8,128]{3,2,1,0:T(8,128)S(1)} %get-tuple-element.37), channel_id=1, source_target_pairs={{0,16},{8,24},{16,0},{24,8},{32,48},{40,56},{48,32},{56,40},{64,80... | collective-permute-start | bytes 122888 | tf_op jit(solution)/shard_map/ppermute | solution.py:284
  37.3 19.6 %all-to-all-start.1 = ((f32[8,80,128]{2,1,0:T(8,128)}), f32[8,80,128]{2,1,0:T(8,128)S(1)}, u32[]{:S(2)}, u32[]{:S(2)}) async-start(f32[8,80,128]{2,1,0:T(8,128)} %get-tuple-element.43), calls=%async_computation.1 | async-start | bytes 655360 | tf_op jit(solution)/shard_map/all_to_all | solution.py:329
  44.2 4.5 %collective-permute-start.3 = (f32[2,5,8,128]{3,2,1,0:T(8,128)S(1)}, f32[2,5,8,128]{3,2,1,0:T(8,128)S(1)}, u32[]{:S(2)}, u32[]{:S(2)}) collective-permute-start(f32[2,5,8,128]{3,2,1,0:T(8,128)S(1)} %get-tuple-element.45), channel_id=1, source_target_pairs={{0,8},{8,0},{16,24},{24,16},{32,40},{40,32},{48,56},{56,48},{64,72... | collective-permute-start | bytes 122888 | tf_op jit(solution)/shard_map/ppermute | solution.py:275
  48.8 8.1 %collective-permute-start.4 = (f32[2,5,8,128]{3,2,1,0:T(8,128)S(1)}, f32[2,5,8,128]{3,2,1,0:T(8,128)S(1)}, u32[]{:S(2)}, u32[]{:S(2)}) collective-permute-start(f32[2,5,8,128]{3,2,1,0:T(8,128)S(1)} %get-tuple-element.47), channel_id=1, source_target_pairs={{0,1008},{8,1016},{16,32},{24,40},{32,16},{40,24},{48,64},{56,72},... | collective-permute-start | bytes 122888 | tf_op jit(solution)/shard_map/ppermute | solution.py:284
  51.8 5.0 %collective-permute-start.5 = (f32[2,5,8,128]{3,2,1,0:T(8,128)S(1)}, f32[2,5,8,128]{3,2,1,0:T(8,128)S(1)}, u32[]{:S(2)}, u32[]{:S(2)}) collective-permute-start(f32[2,5,8,128]{3,2,1,0:T(8,128)S(1)} %get-tuple-element.48), channel_id=1, source_target_pairs={{0,16},{8,24},{16,0},{24,8},{32,48},{40,56},{48,32},{56,40},{64,80... | collective-permute-start | bytes 122888 | tf_op jit(solution)/shard_map/ppermute | solution.py:284

commit v8 on v7

--- a/solution.py
+++ b/solution.py
@@ -120,14 +120,14 @@
     return (lax.axis_index("dom") & 2) == 0
 
 
-def join_kernel(own, came, _, over_odd, over_even):
+def join_kernel(over_edges, own, came, _, one, two):
     even = even_chip()
     for var in range(NV):
         plus = own[0, var], came[0, var]
         minus = own[1, var], came[1, var]
         for n in range(2):
-            over_odd[n, var] = jnp.where(even, minus[n], plus[n])
-            over_even[n, var] = jnp.where(even, plus[n], minus[n])
+            one[n, var] = jnp.where(even, minus[n], plus[n]) if over_edges else plus[n]
+            two[n, var] = jnp.where(even, plus[n], minus[n]) if over_edges else minus[n]
 
 
 def near_sum(table, wide, jac, grad, rest):
@@ -179,7 +179,7 @@
 
 
 def finish_kernel(last, *refs):
-    every, rest, came, over_odd, over_even, wide, jac, dinv, volume, live = refs[:10]
+    every, rest, came, one, two, wide, jac, dinv, volume, live = refs[:10]
     if last:
         out, halos = refs[10:]
     else:
@@ -188,8 +188,13 @@
     first = (lax.axis_index("dom") & 1) == 0
     even = even_chip()
     for var in range(NV):
-        above = [jnp.where(even, over_odd[n, var], over_even[n, var]) for n in range(2)]
-        below = [jnp.where(even, over_even[n, var], over_odd[n, var]) for n in range(2)]
+        above = [one[n, var] for n in range(2)]
+        below = [two[n, var] for n in range(2)]
+        if last:
+            above, below = (
+                [jnp.where(even, a, b) for a, b in zip(above, below)],
+                [jnp.where(even, b, a) for a, b in zip(above, below)],
+            )
         halos[0, var] = jnp.where(first, above[1], came[0, var])
         halos[1, var] = jnp.where(first, came[1, var], below[1])
         halos[2, var] = above[0]
@@ -275,6 +280,12 @@
     return lax.ppermute(value, "dom", [(source, source ^ 1) for source in range(count)])
 
 
+def shifted(value, steps):
+    count = lax.axis_size("dom")
+    pairs = [(source, (source + steps) % count) for source in range(count)]
+    return lax.ppermute(value, "dom", pairs)
+
+
 def edge(value, odd):
     count = lax.axis_size("dom")
     pairs = []
@@ -315,20 +326,24 @@
         smem=(5,),
         cost=COST,
     )
-    odd, even = call(join_kernel, "join_first", (own, came, rest), (PAIR, PAIR))
-    odd, even = edge(odd, 1), edge(even, 0)
+    plus, minus = call(
+        functools.partial(join_kernel, False), "join_first", (own, came, rest), (PAIR, PAIR)
+    )
+    above, below = shifted(plus, 2), shifted(minus, -2)
     kept = (wide, jac, dinv, vol, live)
     swap, own, copies, table = call(
         functools.partial(finish_kernel, False),
         "finish_first",
-        (every, rest, came, odd, even) + kept + (rows,),
+        (every, rest, came, above, below) + kept + (rows,),
         (PAIR, PAIR, COPIES, TABLE),
         [HALOS],
     )
     came = swapped(swap)
     every = lax.all_to_all(copies, "inst", 0, 0)
     rest = call(near_second, "near_second", (table, wide, jac, grad), CURRENT, cost=COST)
-    odd, even = call(join_kernel, "join_second", (own, came, rest), (PAIR, PAIR))
+    odd, even = call(
+        functools.partial(join_kernel, True), "join_second", (own, came, rest), (PAIR, PAIR)
+    )
     odd, even = edge(odd, 1), edge(even, 0)
     out = call(
         functools.partial(finish_kernel, True),

time: 58.2 us -> 59.8 us (1.027)
  starting transfers between devices: 45.8 us -> 49.4 us
  waiting for transfers between devices: 6.33 us -> 4.29 us
    ppermute x0 -> x2, starting transfers between devices: none -> 10.1 us  [shifted(): return lax.ppermute(value, 'dom', pairs)]
    ppermute x4 -> x2, starting transfers between devices: 15.1 us -> 9.2 us  [edge(): return lax.ppermute(value, 'dom', pairs)]
    ppermute x4 -> x2, waiting for transfers between devices: 5.92 us -> 2.81 us  [edge(): return lax.ppermute(value, 'dom', pairs)]
    ppermute x0 -> x2, waiting for transfers between devices: none -> 1.07 us  [shifted(): return lax.ppermute(value, 'dom', pairs)]
where the time goes in v8:
time: 59.8 us; the launch traced here: 59.3 us
  starting transfers between devices  49.4 us (83%)
  Pallas kernels  4.81 us (8%)
  waiting for transfers between devices  4.29 us (7%)
  between operations  0.75 us (1%)
    all_to_all x2, starting transfers between devices, on_device(): every = lax.all_to_all(copies, 'inst', 0, 0)  24.2 us
    ppermute x2, starting transfers between devices, shifted(): return lax.ppermute(value, 'dom', pairs)  10.1 us
    ppermute x2, starting transfers between devices, edge(): return lax.ppermute(value, 'dom', pairs)  9.2 us
    ppermute x2, starting transfers between devices, swapped(): lax.ppermute(value, 'dom', [(source, source ^ 1) for source in range(coun...  5.94 us
    pallas_call x7, Pallas kernels, call(): pl.pallas_call(kernel, out_shape=outs, in_specs=specs, out_specs=jax.tree...  4.81 us
    ppermute x2, waiting for transfers between devices, edge(): return lax.ppermute(value, 'dom', pairs)  2.81 us
  transfers between devices with their start and end apart: 8, of which 3 were waited for; matrix products, arithmetic and copies ran while one was open for 0% of the time, Pallas kernels for 2%

profile of v8, /device:TPU:1, one launch (start us, length us, event | category | flops | bytes accessed | tf_op | source)
XLA Modules:
  0.0 59.3 jit_solution(18195011712254394278)
XLA Ops:
  0.0 2.2 %prep.1 = (f32[2,5,8,128]{3,2,1,0:T(8,128)S(1)}, f32[2,5,8,128]{3,2,1,0:T(8,128)S(1)}, f32[8,80,128]{2,1,0:T(8,128)}, f32[5,8,8,128]{3,2,1,0:T(8,128)S(1)}, s32[...) custom-call(f32[5,16,128]{2,1,0:T(8,128)} %bitcast.28, ...), custom_call_target="tpu_custom_call" | custom-call | tf_op jit(solution)/shard_map/prep/pallas_call | solution.py:266
  2.2 17.2 %all-to-all-start = ((f32[8,80,128]{2,1,0:T(8,128)}), f32[8,80,128]{2,1,0:T(8,128)S(1)}, u32[]{:S(2)}, u32[]{:S(2)}) async-start(f32[8,80,128]{2,1,0:T(8,128)} %get-tuple-element.27), calls=%async_computation | async-start | bytes 655360 | tf_op jit(solution)/shard_map/all_to_all | solution.py:320
  19.4 2.9 %collective-permute-start = (f32[2,5,8,128]{3,2,1,0:T(8,128)S(1)}, f32[2,5,8,128]{3,2,1,0:T(8,128)S(1)}, u32[]{:S(2)}, u32[]{:S(2)}) collective-permute-start(f32[2,5,8,128]{3,2,1,0:T(8,128)S(1)} %get-tuple-element.34), channel_id=1, source_target_pairs={{0,8},{8,0},{16,24},{24,16},{32,40},{40,32},{48,56},{56,48},{64,72... | collective-permute-start | bytes 122888 | tf_op jit(solution)/shard_map/ppermute | solution.py:280
  22.9 0.5 near_first.1
  23.4 0.0 collective-permute-done.came.refs_2_
  23.4 3.3 %collective-permute-start.1 = (f32[2,5,8,128]{3,2,1,0:T(8,128)S(1)}, f32[2,5,8,128]{3,2,1,0:T(8,128)S(1)}, u32[]{:S(2)}, u32[]{:S(2)}) collective-permute-start(f32[2,5,8,128]{3,2,1,0:T(8,128)S(1)} %get-tuple-element.36), channel_id=1, source_target_pairs={{0,16},{8,24},{16,32},{24,40},{32,48},{40,56},{48,64},{56,72},{64,... | collective-permute-start | bytes 122888 | tf_op jit(solution)/shard_map/ppermute | solution.py:286
  26.7 6.8 %collective-permute-start.2 = (f32[2,5,8,128]{3,2,1,0:T(8,128)S(1)}, f32[2,5,8,128]{3,2,1,0:T(8,128)S(1)}, u32[]{:S(2)}, u32[]{:S(2)}) collective-permute-start(f32[2,5,8,128]{3,2,1,0:T(8,128)S(1)} %get-tuple-element.37), channel_id=1, source_target_pairs={{0,1008},{8,1016},{16,0},{24,8},{32,16},{40,24},{48,32},{56,40},{6... | collective-permute-start | bytes 122888 | tf_op jit(solution)/shard_map/ppermute | solution.py:286
  33.6 0.0 collective-permute-done.1.refs_3_
  33.6 1.1 %collective-permute-done.2.refs_4_ = f32[2,5,8,128]{3,2,1,0:T(8,128)S(1)} collective-permute-done((f32[2,5,8,128]{3,2,1,0:T(8,128)S(1)}, f32[2,5,8,128]{3,2,1,0:T(8,128)S(1)}, u32[]{:S(2)}, u32[]{:S(2)}) %collective-permute-start.2) | collective-permute-done | bytes 40992 | tf_op jit(solution)/shard_map/ppermute | solution.py:286
  34.6 0.0 all-to-all-done.refs_0_
  34.6 0.9 %finish_first.1 = (f32[2,5,8,128]{3,2,1,0:T(8,128)S(1)}, f32[2,5,8,128]{3,2,1,0:T(8,128)S(1)}, f32[8,80,128]{2,1,0:T(8,128)}, f32[5,8,8,128]{3,2,1,0:T(8,128)S(1)}) custom-call(f32[8,80,128]{2,1,0:T(8,128)S(1)} %all-to-all-done.refs_0_, f32[5,16,128]{2,1,0:T(8,128)S(1)} %get-tuple-element.33._.refs_1_, ...), custom_call_target="tpu_custom_call" | custom-call | tf_op jit(solution)/shard_map/finish_first/pallas_call | solution.py:266
  35.6 6.9 %all-to-all-start.1 = ((f32[8,80,128]{2,1,0:T(8,128)}), f32[8,80,128]{2,1,0:T(8,128)S(1)}, u32[]{:S(2)}, u32[]{:S(2)}) async-start(f32[8,80,128]{2,1,0:T(8,128)} %get-tuple-element.43), calls=%async_computation.1 | async-start | bytes 655360 | tf_op jit(solution)/shard_map/all_to_all | solution.py:342
  42.5 3.1 %collective-permute-start.3 = (f32[2,5,8,128]{3,2,1,0:T(8,128)S(1)}, f32[2,5,8,128]{3,2,1,0:T(8,128)S(1)}, u32[]{:S(2)}, u32[]{:S(2)}) collective-permute-start(f32[2,5,8,128]{3,2,1,0:T(8,128)S(1)} %get-tuple-element.45), channel_id=1, source_target_pairs={{0,8},{8,0},{16,24},{24,16},{32,40},{40,32},{48,56},{56,48},{64,72... | collective-permute-start | bytes 122888 | tf_op jit(solution)/shard_map/ppermute | solution.py:280
  45.6 0.4 near_second.1._.refs_1_
  46.0 0.4 collective-permute-done.3.came.refs_2_
  46.4 7.3 %collective-permute-start.4 = (f32[2,5,8,128]{3,2,1,0:T(8,128)S(1)}, f32[2,5,8,128]{3,2,1,0:T(8,128)S(1)}, u32[]{:S(2)}, u32[]{:S(2)}) collective-permute-start(f32[2,5,8,128]{3,2,1,0:T(8,128)S(1)} %get-tuple-element.47), channel_id=1, source_target_pairs={{0,1008},{8,1016},{16,32},{24,40},{32,16},{40,24},{48,64},{56,72},... | collective-permute-start | bytes 122888 | tf_op jit(solution)/shard_map/ppermute | solution.py:295
  53.7 1.9 %collective-permute-start.5 = (f32[2,5,8,128]{3,2,1,0:T(8,128)S(1)}, f32[2,5,8,128]{3,2,1,0:T(8,128)S(1)}, u32[]{:S(2)}, u32[]{:S(2)}) collective-permute-start(f32[2,5,8,128]{3,2,1,0:T(8,128)S(1)} %get-tuple-element.48), channel_id=1, source_target_pairs={{0,16},{8,24},{16,0},{24,8},{32,48},{40,56},{48,32},{56,40},{64,80... | collective-permute-start | bytes 122888 | tf_op jit(solution)/shard_map/ppermute | solution.py:295
  55.7 0.0 collective-permute-done.4.refs_3_
  55.7 2.8 %collective-permute-done.5.refs_4_ = f32[2,5,8,128]{3,2,1,0:T(8,128)S(1)} collective-permute-done((f32[2,5,8,128]{3,2,1,0:T(8,128)S(1)}, f32[2,5,8,128]{3,2,1,0:T(8,128)S(1)}, u32[]{:S(2)}, u32[]{:S(2)}) %collective-permute-start.5) | collective-permute-done | bytes 40992 | tf_op jit(solution)/shard_map/ppermute | solution.py:295
  58.5 0.0 all-to-all-done.1.refs_0_
  58.5 0.8 %finish_second.1 = f32[5,16,128]{2,1,0:T(8,128)} custom-call(f32[8,80,128]{2,1,0:T(8,128)S(1)} %all-to-all-done.1.refs_0_, f32[5,16,128]{2,1,0:T(8,128)S(1)} %near_second.1._.refs_1_, f32[2,5,8,128]{3,2,1,0:T(8,128)S(1)} %collective-permute-done.3.came.refs_2_, f32[2,5,8,128]{3,2,1,0:T(8,128)S(1)} %collective-permute-done.4.refs_3_, ...), custom_call_target="tpu_custom_call" | custom-call | tf_op jit(solution)/shard_map/finish_second/pallas_call | solution.py:266
  (2 shorter events, 0.0 us)
Async XLA Ops:
  2.2 32.5 %all-to-all-start = ((f32[8,80,128]{2,1,0:T(8,128)}), f32[8,80,128]{2,1,0:T(8,128)S(1)}, u32[]{:S(2)}, u32[]{:S(2)}) async-start(f32[8,80,128]{2,1,0:T(8,128)} %get-tuple-element.27), calls=%async_computation | async-start | bytes 655360 | tf_op jit(solution)/shard_map/all_to_all | solution.py:320
  19.4 4.0 %collective-permute-start = (f32[2,5,8,128]{3,2,1,0:T(8,128)S(1)}, f32[2,5,8,128]{3,2,1,0:T(8,128)S(1)}, u32[]{:S(2)}, u32[]{:S(2)}) collective-permute-start(f32[2,5,8,128]{3,2,1,0:T(8,128)S(1)} %get-tuple-element.34), channel_id=1, source_target_pairs={{0,8},{8,0},{16,24},{24,16},{32,40},{40,32},{48,56},{56,48},{64,72... | collective-permute-start | bytes 122888 | tf_op jit(solution)/shard_map/ppermute | solution.py:280
  23.4 10.1 %collective-permute-start.1 = (f32[2,5,8,128]{3,2,1,0:T(8,128)S(1)}, f32[2,5,8,128]{3,2,1,0:T(8,128)S(1)}, u32[]{:S(2)}, u32[]{:S(2)}) collective-permute-start(f32[2,5,8,128]{3,2,1,0:T(8,128)S(1)} %get-tuple-element.36), channel_id=1, source_target_pairs={{0,16},{8,24},{16,32},{24,40},{32,48},{40,56},{48,64},{56,72},{64,... | collective-permute-start | bytes 122888 | tf_op jit(solution)/shard_map/ppermute | solution.py:286
  26.7 7.9 %collective-permute-start.2 = (f32[2,5,8,128]{3,2,1,0:T(8,128)S(1)}, f32[2,5,8,128]{3,2,1,0:T(8,128)S(1)}, u32[]{:S(2)}, u32[]{:S(2)}) collective-permute-start(f32[2,5,8,128]{3,2,1,0:T(8,128)S(1)} %get-tuple-element.37), channel_id=1, source_target_pairs={{0,1008},{8,1016},{16,0},{24,8},{32,16},{40,24},{48,32},{56,40},{6... | collective-permute-start | bytes 122888 | tf_op jit(solution)/shard_map/ppermute | solution.py:286
  35.6 22.9 %all-to-all-start.1 = ((f32[8,80,128]{2,1,0:T(8,128)}), f32[8,80,128]{2,1,0:T(8,128)S(1)}, u32[]{:S(2)}, u32[]{:S(2)}) async-start(f32[8,80,128]{2,1,0:T(8,128)} %get-tuple-element.43), calls=%async_computation.1 | async-start | bytes 655360 | tf_op jit(solution)/shard_map/all_to_all | solution.py:342
  42.5 3.9 %collective-permute-start.3 = (f32[2,5,8,128]{3,2,1,0:T(8,128)S(1)}, f32[2,5,8,128]{3,2,1,0:T(8,128)S(1)}, u32[]{:S(2)}, u32[]{:S(2)}) collective-permute-start(f32[2,5,8,128]{3,2,1,0:T(8,128)S(1)} %get-tuple-element.45), channel_id=1, source_target_pairs={{0,8},{8,0},{16,24},{24,16},{32,40},{40,32},{48,56},{56,48},{64,72... | collective-permute-start | bytes 122888 | tf_op jit(solution)/shard_map/ppermute | solution.py:280
  46.4 9.2 %collective-permute-start.4 = (f32[2,5,8,128]{3,2,1,0:T(8,128)S(1)}, f32[2,5,8,128]{3,2,1,0:T(8,128)S(1)}, u32[]{:S(2)}, u32[]{:S(2)}) collective-permute-start(f32[2,5,8,128]{3,2,1,0:T(8,128)S(1)} %get-tuple-element.47), channel_id=1, source_target_pairs={{0,1008},{8,1016},{16,32},{24,40},{32,16},{40,24},{48,64},{56,72},... | collective-permute-start | bytes 122888 | tf_op jit(solution)/shard_map/ppermute | solution.py:295
  53.7 4.7 %collective-permute-start.5 = (f32[2,5,8,128]{3,2,1,0:T(8,128)S(1)}, f32[2,5,8,128]{3,2,1,0:T(8,128)S(1)}, u32[]{:S(2)}, u32[]{:S(2)}) collective-permute-start(f32[2,5,8,128]{3,2,1,0:T(8,128)S(1)} %get-tuple-element.48), channel_id=1, source_target_pairs={{0,16},{8,24},{16,0},{24,8},{32,48},{40,56},{48,32},{56,40},{64,80... | collective-permute-start | bytes 122888 | tf_op jit(solution)/shard_map/ppermute | solution.py:295

commit v9 on v3

--- a/solution.py
+++ b/solution.py
@@ -90,18 +90,20 @@
     ]
     for load in loads:
         load.start()
-    for load in loads:
-        load.wait()
+    loads[0].wait()
+    repeats = [pltpu.make_async_copy(adj, copies.at[n], sems.at[2 + n]) for n in range(8)]
+    for repeat in repeats:
+        repeat.start()
     for var in range(NV):
         for half in range(2):
-            value = adj[var, half * HALF : (half + 1) * HALF, :]
-            fill_table(half, value, var, table)
-            for peer in range(8):
-                at = var * ROWS + half * HALF
-                copies[peer, at : at + HALF, :] = value
+            at = var * ROWS + half * HALF
+            fill_table(half, adj[at : at + HALF, :], var, table)
+    loads[1].wait()
     for slot in range(SLOTS):
         rows[2 * slot : 2 * slot + 2, :] = jnp.broadcast_to(sends[slot : slot + 1, :], (2, LANES))
     send_blocks(table, rows[...], swap, own)
+    for repeat in repeats:
+        repeat.wait()
 
 
 def join_kernel(own, came, plus, minus):
@@ -260,7 +262,7 @@
 HALOS = pltpu.VMEM((SLOTS, NV, HALF, LANES), jnp.float32)
 
 
-def call(kernel, name, args, outs, scratch=(), hbm=(), smem=(), cost=None):
+def call(kernel, name, args, outs, scratch=(), hbm=(), smem=(), hbm_out=(), cost=None):
     specs = [HBM if n in hbm else SMEM if n in smem else VMEM for n in range(len(args))]
     args = [
         pltpu.with_memory_space_constraint(arg, pltpu.HBM) if n in hbm else arg
@@ -270,7 +272,7 @@
         kernel,
         out_shape=outs,
         in_specs=specs,
-        out_specs=jax.tree.map(lambda _: VMEM, outs),
+        out_specs=jax.tree.map(lambda out: HBM if out in hbm_out else VMEM, outs),
         scratch_shapes=scratch,
         compiler_params=PARAMS,
         cost_estimate=cost,
@@ -293,14 +295,15 @@
     swap, own, copies, table, rows = call(
         prep_kernel,
         "prep",
-        (dense(adjoint), send_rows),
+        (dense(adjoint).reshape(NV * ROWS, LANES), send_rows),
         (PAIR, PAIR, COPIES, TABLE, ROW_INDEX),
         [
-            pltpu.VMEM(CURRENT.shape, jnp.float32),
+            pltpu.VMEM((NV * ROWS, LANES), jnp.float32),
             pltpu.VMEM((SLOTS, LANES), jnp.int32),
-            pltpu.SemaphoreType.DMA((2,)),
+            pltpu.SemaphoreType.DMA((10,)),
         ],
         hbm=(0, 1),
+        hbm_out=(COPIES,),
     )
     came = swapped(swap)
     every = lax.all_to_all(copies, "inst", 0, 0)

time: 57.5 us -> 57.6 us (level)
  no operation moved by 1% of the time
where the time goes in v9:
time: 57.6 us; the launch traced here: 56.9 us
  starting transfers between devices  48.6 us (84%)
  Pallas kernels  5.25 us (9%)
  waiting for transfers between devices  2.32 us (4%)
  between operations  0.76 us (1%)
    all_to_all x2, starting transfers between devices, on_device(): every = lax.all_to_all(copies, 'inst', 0, 0)  24.2 us
    ppermute x4, starting transfers between devices, shifted(): return lax.ppermute(value, 'dom', pairs)  18.8 us
    ppermute x2, starting transfers between devices, swapped(): lax.ppermute(value, 'dom', [(source, source ^ 1) for source in range(coun...  5.66 us
    pallas_call x7, Pallas kernels, call(): pl.pallas_call(kernel, out_shape=outs, in_specs=specs, out_specs=jax.tree...  5.25 us
    ppermute x2, waiting for transfers between devices, swapped(): lax.ppermute(value, 'dom', [(source, source ^ 1) for source in range(coun...  1.7 us
  transfers between devices with their start and end apart: 8, of which 3 were waited for; matrix products, arithmetic and copies ran while one was open for 0% of the time, Pallas kernels for 3%

profile of v9, /device:TPU:1, one launch (start us, length us, event | category | flops | bytes accessed | tf_op | source)
XLA Modules:
  0.0 56.9 jit_solution(14793149901415242596)
XLA Ops:
  0.0 1.6 %prep.1 = (f32[2,5,8,128]{3,2,1,0:T(8,128)S(1)}, f32[2,5,8,128]{3,2,1,0:T(8,128)S(1)}, f32[8,80,128]{2,1,0:T(8,128)}, f32[5,8,8,128]{3,2,1,0:T(8,128)S(1)}, s32[8,128]{1,0:T(8,128)S(1)}) custom-call(f32[80,128]{1,0:T(8,128)} %bitcast.28, s32[4,128]{1,0:T(4,128)} %sends_hbm.1), custom_call_target="tpu_custom_call" | custom-call | tf_op jit(solution)/shard_map/prep/pallas_call | solution.py:271
  1.6 17.2 %all-to-all-start = ((f32[8,80,128]{2,1,0:T(8,128)}), f32[8,80,128]{2,1,0:T(8,128)S(1)}, u32[]{:S(2)}, u32[]{:S(2)}) async-start(f32[8,80,128]{2,1,0:T(8,128)} %get-tuple-element.26), calls=%async_computation | async-start | bytes 655360 | tf_op jit(solution)/shard_map/all_to_all | solution.py:309
  18.8 2.9 %collective-permute-start = (f32[2,5,8,128]{3,2,1,0:T(8,128)S(1)}, f32[2,5,8,128]{3,2,1,0:T(8,128)S(1)}, u32[]{:S(2)}, u32[]{:S(2)}) collective-permute-start(f32[2,5,8,128]{3,2,1,0:T(8,128)S(1)} %get-tuple-element.28), channel_id=1, source_target_pairs={{0,8},{8,0},{16,24},{24,16},{32,40},{40,32},{48,56},{56,48},{64,72... | collective-permute-start | bytes 122888 | tf_op jit(solution)/shard_map/ppermute | solution.py:285
  21.7 0.8 %collective-permute-done.came.refs_1_ = f32[2,5,8,128]{3,2,1,0:T(8,128)S(1)} collective-permute-done((f32[2,5,8,128]{3,2,1,0:T(8,128)S(1)}, f32[2,5,8,128]{3,2,1,0:T(8,128)S(1)}, u32[]{:S(2)}, u32[]{:S(2)}) %collective-permute-start) | collective-permute-done | bytes 40992 | tf_op jit(solution)/shard_map/ppermute | solution.py:285
  22.6 3.3 %collective-permute-start.1 = (f32[2,5,8,128]{3,2,1,0:T(8,128)S(1)}, f32[2,5,8,128]{3,2,1,0:T(8,128)S(1)}, u32[]{:S(2)}, u32[]{:S(2)}) collective-permute-start(f32[2,5,8,128]{3,2,1,0:T(8,128)S(1)} %get-tuple-element.30), channel_id=1, source_target_pairs={{0,16},{8,24},{16,32},{24,40},{32,48},{40,56},{48,64},{56,72},{64,... | collective-permute-start | bytes 122888 | tf_op jit(solution)/shard_map/ppermute | solution.py:291
  25.9 6.8 %collective-permute-start.2 = (f32[2,5,8,128]{3,2,1,0:T(8,128)S(1)}, f32[2,5,8,128]{3,2,1,0:T(8,128)S(1)}, u32[]{:S(2)}, u32[]{:S(2)}) collective-permute-start(f32[2,5,8,128]{3,2,1,0:T(8,128)S(1)} %get-tuple-element.31), channel_id=1, source_target_pairs={{0,1008},{8,1016},{16,0},{24,8},{32,16},{40,24},{48,32},{56,40},{6... | collective-permute-start | bytes 122888 | tf_op jit(solution)/shard_map/ppermute | solution.py:291
  33.3 0.0 all-to-all-done.every
  33.3 1.5 %inner_first.1 = (f32[5,16,128]{2,1,0:T(8,128)S(1)}, s32[6,16,128]{2,1,0:T(8,128)S(1)}, f32[6,5,5,16,128]{4,3,2,1,0:T(8,128)S(1)}, f32[5,5,16,128]{3,2,1,0:T(8,1...) custom-call(f32[5,8,8,128]{3,2,1,0:T(8,128)S(1)} %get-tuple-element.25.table, ...), custom_call_target="tpu_custom_call" | custom-call | flops 1000000 | bytes 4000000 | tf_op jit(solution)/shard_map/inner_first/pallas_call | solution.py:271
  34.8 0.0 collective-permute-done.1.refs_2_
  34.8 0.0 collective-permute-done.2.refs_3_
  34.9 0.9 %finish_first.1 = (f32[2,5,8,128]{3,2,1,0:T(8,128)S(1)}, f32[2,5,8,128]{3,2,1,0:T(8,128)S(1)}, f32[8,80,128]{2,1,0:T(8,128)}, f32[5,8,8,128]{3,2,1,0:T(8,128)S(1)}) custom-call(f32[5,16,128]{2,1,0:T(8,128)S(1)} %get-tuple-element.27.refs_0_, f32[2,5,8,128]{3,2,1,0:T(8,128)S(1)} %collective-permute-done.came.refs_1_, ...), custom_call_target="tpu_custom_call" | custom-call | tf_op jit(solution)/shard_map/finish_first/pallas_call | solution.py:271
  35.8 6.9 %all-to-all-start.1 = ((f32[8,80,128]{2,1,0:T(8,128)}), f32[8,80,128]{2,1,0:T(8,128)S(1)}, u32[]{:S(2)}, u32[]{:S(2)}) async-start(f32[8,80,128]{2,1,0:T(8,128)} %get-tuple-element.38), calls=%async_computation.1 | async-start | bytes 655360 | tf_op jit(solution)/shard_map/all_to_all | solution.py:343
  42.7 2.8 %collective-permute-start.3 = (f32[2,5,8,128]{3,2,1,0:T(8,128)S(1)}, f32[2,5,8,128]{3,2,1,0:T(8,128)S(1)}, u32[]{:S(2)}, u32[]{:S(2)}) collective-permute-start(f32[2,5,8,128]{3,2,1,0:T(8,128)S(1)} %get-tuple-element.41), channel_id=1, source_target_pairs={{0,8},{8,0},{16,24},{24,16},{32,40},{40,32},{48,56},{56,48},{64,72... | collective-permute-start | bytes 122888 | tf_op jit(solution)/shard_map/ppermute | solution.py:285
  45.5 0.8 %collective-permute-done.3.came.refs_1_ = f32[2,5,8,128]{3,2,1,0:T(8,128)S(1)} collective-permute-done((f32[2,5,8,128]{3,2,1,0:T(8,128)S(1)}, f32[2,5,8,128]{3,2,1,0:T(8,128)S(1)}, u32[]{:S(2)}, u32[]{:S(2)}) %collective-permute-start.3) | collective-permute-done | bytes 40992 | tf_op jit(solution)/shard_map/ppermute | solution.py:285
  46.4 1.9 %collective-permute-start.4 = (f32[2,5,8,128]{3,2,1,0:T(8,128)S(1)}, f32[2,5,8,128]{3,2,1,0:T(8,128)S(1)}, u32[]{:S(2)}, u32[]{:S(2)}) collective-permute-start(f32[2,5,8,128]{3,2,1,0:T(8,128)S(1)} %get-tuple-element.43), channel_id=1, source_target_pairs={{0,16},{8,24},{16,32},{24,40},{32,48},{40,56},{48,64},{56,72},{64,... | collective-permute-start | bytes 122888 | tf_op jit(solution)/shard_map/ppermute | solution.py:291
  48.3 6.7 %collective-permute-start.5 = (f32[2,5,8,128]{3,2,1,0:T(8,128)S(1)}, f32[2,5,8,128]{3,2,1,0:T(8,128)S(1)}, u32[]{:S(2)}, u32[]{:S(2)}) collective-permute-start(f32[2,5,8,128]{3,2,1,0:T(8,128)S(1)} %get-tuple-element.44), channel_id=1, source_target_pairs={{0,1008},{8,1016},{16,0},{24,8},{32,16},{40,24},{48,32},{56,40},{6... | collective-permute-start | bytes 122888 | tf_op jit(solution)/shard_map/ppermute | solution.py:291
  55.0 0.0 all-to-all-done.1.every
  55.1 0.4 inner_second.1.refs_0_
  55.5 0.0 collective-permute-done.4.refs_2_
  55.5 0.6 %collective-permute-done.5.refs_3_ = f32[2,5,8,128]{3,2,1,0:T(8,128)S(1)} collective-permute-done((f32[2,5,8,128]{3,2,1,0:T(8,128)S(1)}, f32[2,5,8,128]{3,2,1,0:T(8,128)S(1)}, u32[]{:S(2)}, u32[]{:S(2)}) %collective-permute-start.5) | collective-permute-done | bytes 40992 | tf_op jit(solution)/shard_map/ppermute | solution.py:291
  56.1 0.8 %finish_second.1 = f32[5,16,128]{2,1,0:T(8,128)} custom-call(f32[5,16,128]{2,1,0:T(8,128)S(1)} %inner_second.1.refs_0_, f32[2,5,8,128]{3,2,1,0:T(8,128)S(1)} %collective-permute-done.3.came.refs_1_, f32[2,5,8,128]{3,2,1,0:T(8,128)S(1)} %collective-permute-done.4.refs_2_, f32[2,5,8,128]{3,2,1,0:T(8,128)S(1)} %collective-permute-done.5.refs_3_, ...), custom_call_target="tpu_custom_call" | custom-call | tf_op jit(solution)/shard_map/finish_second/pallas_call | solution.py:271
  (2 shorter events, 0.0 us)
Async XLA Ops:
  1.6 31.7 %all-to-all-start = ((f32[8,80,128]{2,1,0:T(8,128)}), f32[8,80,128]{2,1,0:T(8,128)S(1)}, u32[]{:S(2)}, u32[]{:S(2)}) async-start(f32[8,80,128]{2,1,0:T(8,128)} %get-tuple-element.26), calls=%async_computation | async-start | bytes 655360 | tf_op jit(solution)/shard_map/all_to_all | solution.py:309
  18.8 3.7 %collective-permute-start = (f32[2,5,8,128]{3,2,1,0:T(8,128)S(1)}, f32[2,5,8,128]{3,2,1,0:T(8,128)S(1)}, u32[]{:S(2)}, u32[]{:S(2)}) collective-permute-start(f32[2,5,8,128]{3,2,1,0:T(8,128)S(1)} %get-tuple-element.28), channel_id=1, source_target_pairs={{0,8},{8,0},{16,24},{24,16},{32,40},{40,32},{48,56},{56,48},{64,72... | collective-permute-start | bytes 122888 | tf_op jit(solution)/shard_map/ppermute | solution.py:285
  22.6 12.3 %collective-permute-start.1 = (f32[2,5,8,128]{3,2,1,0:T(8,128)S(1)}, f32[2,5,8,128]{3,2,1,0:T(8,128)S(1)}, u32[]{:S(2)}, u32[]{:S(2)}) collective-permute-start(f32[2,5,8,128]{3,2,1,0:T(8,128)S(1)} %get-tuple-element.30), channel_id=1, source_target_pairs={{0,16},{8,24},{16,32},{24,40},{32,48},{40,56},{48,64},{56,72},{64,... | collective-permute-start | bytes 122888 | tf_op jit(solution)/shard_map/ppermute | solution.py:291
  25.9 9.0 %collective-permute-start.2 = (f32[2,5,8,128]{3,2,1,0:T(8,128)S(1)}, f32[2,5,8,128]{3,2,1,0:T(8,128)S(1)}, u32[]{:S(2)}, u32[]{:S(2)}) collective-permute-start(f32[2,5,8,128]{3,2,1,0:T(8,128)S(1)} %get-tuple-element.31), channel_id=1, source_target_pairs={{0,1008},{8,1016},{16,0},{24,8},{32,16},{40,24},{48,32},{56,40},{6... | collective-permute-start | bytes 122888 | tf_op jit(solution)/shard_map/ppermute | solution.py:291
  35.8 19.3 %all-to-all-start.1 = ((f32[8,80,128]{2,1,0:T(8,128)}), f32[8,80,128]{2,1,0:T(8,128)S(1)}, u32[]{:S(2)}, u32[]{:S(2)}) async-start(f32[8,80,128]{2,1,0:T(8,128)} %get-tuple-element.38), calls=%async_computation.1 | async-start | bytes 655360 | tf_op jit(solution)/shard_map/all_to_all | solution.py:343
  42.7 3.7 %collective-permute-start.3 = (f32[2,5,8,128]{3,2,1,0:T(8,128)S(1)}, f32[2,5,8,128]{3,2,1,0:T(8,128)S(1)}, u32[]{:S(2)}, u32[]{:S(2)}) collective-permute-start(f32[2,5,8,128]{3,2,1,0:T(8,128)S(1)} %get-tuple-element.41), channel_id=1, source_target_pairs={{0,8},{8,0},{16,24},{24,16},{32,40},{40,32},{48,56},{56,48},{64,72... | collective-permute-start | bytes 122888 | tf_op jit(solution)/shard_map/ppermute | solution.py:285
  46.4 9.1 %collective-permute-start.4 = (f32[2,5,8,128]{3,2,1,0:T(8,128)S(1)}, f32[2,5,8,128]{3,2,1,0:T(8,128)S(1)}, u32[]{:S(2)}, u32[]{:S(2)}) collective-permute-start(f32[2,5,8,128]{3,2,1,0:T(8,128)S(1)} %get-tuple-element.43), channel_id=1, source_target_pairs={{0,16},{8,24},{16,32},{24,40},{32,48},{40,56},{48,64},{56,72},{64,... | collective-permute-start | bytes 122888 | tf_op jit(solution)/shard_map/ppermute | solution.py:291
  48.3 7.8 %collective-permute-start.5 = (f32[2,5,8,128]{3,2,1,0:T(8,128)S(1)}, f32[2,5,8,128]{3,2,1,0:T(8,128)S(1)}, u32[]{:S(2)}, u32[]{:S(2)}) collective-permute-start(f32[2,5,8,128]{3,2,1,0:T(8,128)S(1)} %get-tuple-element.44), channel_id=1, source_target_pairs={{0,1008},{8,1016},{16,0},{24,8},{32,16},{40,24},{48,32},{56,40},{6... | collective-permute-start | bytes 122888 | tf_op jit(solution)/shard_map/ppermute | solution.py:291
